TPU v7x, 32 devices: a whole 2x2x4 slice. The times are simulated.
32 devices in a mesh: seq: 8 (over z, x), tp: 4 (over y, core).
Axes of the slice: x: 2, y: 2, z: 4, core: 2. Of those that a mesh axis runs over, the one named last changes fastest.
Arguments:
- stream: float32 [8192, 2048], P('seq', 'tp')
- norm1_gain: float32 [2048], P('tp'), may hold values from 0.25 to 1.75
- in_weight: bfloat16 [2048, 3, 2048], P('seq', None, 'tp'), may hold values from -0.125 to 0.125
- conv_weight: float32 [3, 2048], P(None, 'tp'), may hold values from -3 to 3
- out_weight: bfloat16 [2048, 2048], P('seq', 'tp'), may hold values from -0.125 to 0.125
- norm2_gain: float32 [2048], P('tp'), may hold values from 0.25 to 1.75
- gate_weight: bfloat16 [2048, 8192], P('seq', 'tp'), may hold values from -0.125 to 0.125
- up_weight: bfloat16 [2048, 8192], P('seq', 'tp'), may hold values from -0.125 to 0.125
- down_weight: bfloat16 [2048, 8192], P('seq', 'tp'), may hold values from -0.09375 to 0.09375
- doc_starts: int32 [4], replicated, may hold values from 0 to 7167, as said below
- out_grad: float32 [8192, 2048], P('seq', 'tp'), may hold values from -6 to 6
Outputs:
- result: float32 [8192, 2048], P('seq', 'tp')
- stream_grad: float32 [8192, 2048], P('seq', 'tp')
- norm1_gain_grad: float32 [2048], P('tp')
- in_weight_grad: float32 [2048, 3, 2048], P('seq', None, 'tp')
- conv_weight_grad: float32 [3, 2048], P(None, 'tp')
- out_weight_grad: float32 [2048, 2048], P('seq', 'tp')
- norm2_gain_grad: float32 [2048], P('tp')
- gate_weight_grad: float32 [2048, 8192], P('seq', 'tp')
- up_weight_grad: float32 [2048, 8192], P('seq', 'tp')
- down_weight_grad: float32 [2048, 8192], P('seq', 'tp')
- rms_values: float32 [2, 8192], P(None, 'seq')
Inputs may be any that keep to these rules, and one draw needn't show every extreme that they name: doc_starts[0] = 0; for 1 <= j < 3, doc_starts[j] lies between 2 j * 1024 + 2 and 2 j * 1024 + 1023; when 4 > 1 the last entry is exactly 2 (3) * 1024 + 1023; so the entries rise.
All inputs are finite; a program needn't handle non-finite values.
Results may differ from a plain program's by a relative error of at most 0.0094.
Values may be sent and summed in bfloat16 or wider, within the bound.
A program may use at most 320 MiB of HBM per device.

v0:
```python
import jax
import jax.numpy as jnp
from jax import lax
from jax.sharding import PartitionSpec as P

epsilon = 1e-05


def from_behind(shard, axis, by):
    count = lax.axis_size(axis)
    pairs = [(i, i + by) for i in range(count) if 0 <= i + by < count]
    return lax.ppermute(shard, axis, pairs)


def doc_count(doc_starts, positions):
    return jnp.sum((doc_starts[None, :] <= positions[:, None]).astype(jnp.int32), axis=1)


def lag_masks(doc_starts, positions):
    current = doc_count(doc_starts, positions)
    one = (positions >= 1) & (doc_count(doc_starts, positions - 1) == current)
    two = (positions >= 2) & (doc_count(doc_starts, positions - 2) == current)
    return (one.astype(jnp.float32)[:, None], two.astype(jnp.float32)[:, None])


def contract_rows(left, right):
    return lax.dot_general(
        left, right, (((0,), (0,)), ((), ())), preferred_element_type=jnp.float32
    )


def contract_cols(left, right):
    return lax.dot_general(
        left, right, (((1,), (1,)), ((), ())), preferred_element_type=jnp.float32
    )


def reduce_tp(partial_rows):
    return lax.psum_scatter(partial_rows, "tp", scatter_dimension=1, tiled=True)


def gather_grads(grad_rows):
    return lax.all_gather(grad_rows, "tp", axis=1, tiled=True)


def normalize(values, gain):
    width = gain.shape[0] * lax.axis_size("tp")
    squares = lax.psum(jnp.sum(values * values, axis=1, keepdims=True), "tp")
    inverse = lax.rsqrt(squares / width + epsilon)
    normed = lax.all_gather(
        (values * inverse * gain).astype(jnp.bfloat16), "tp", axis=1, tiled=True
    )
    return (normed, inverse, jnp.sqrt(squares[:, 0] / width + epsilon))


def norm_backward(values, gain, inverse, grad_rows):
    width = gain.shape[0] * lax.axis_size("tp")
    gained = gain * grad_rows
    total = lax.psum(jnp.sum(values * gained, axis=1, keepdims=True), "tp")
    grad_values = inverse * gained - values * inverse**3 * (total / width)
    grad_gain = jnp.sum(grad_rows * values * inverse, axis=0)
    return (grad_values, grad_gain)


def on_device(
    stream,
    norm1_gain,
    in_weight,
    conv_weight,
    out_weight,
    norm2_gain,
    gate_weight,
    up_weight,
    down_weight,
    doc_starts,
    out_grad,
):
    tokens = stream.shape[0]
    local = stream.shape[1]
    hidden_local = gate_weight.shape[1]
    rows_here = in_weight.shape[0]
    whole_in, whole_out, whole_gate, whole_up, whole_down = (
        lax.all_gather(in_weight, "seq", axis=0, tiled=True),
        lax.all_gather(out_weight, "seq", axis=0, tiled=True),
        lax.all_gather(gate_weight, "seq", axis=0, tiled=True),
        lax.all_gather(up_weight, "seq", axis=0, tiled=True),
        lax.all_gather(down_weight, "seq", axis=0, tiled=True),
    )
    width = whole_out.shape[0]
    in_matrix = whole_in.reshape(width, 3 * local)
    positions = lax.axis_index("seq") * tokens + jnp.arange(tokens, dtype=jnp.int32)
    mask_one, mask_two = lag_masks(doc_starts, positions)
    normed_in, inverse_in, rms_in = normalize(stream, norm1_gain)
    projected = jnp.dot(normed_in, in_matrix, preferred_element_type=jnp.float32)
    in_gate = projected[:, :local]
    out_gate = projected[:, local : 2 * local]
    carried = projected[:, 2 * local :]
    mixed = in_gate * carried
    previous = from_behind(mixed[-2:], "seq", 1)
    extended = jnp.concatenate([previous, mixed], axis=0)
    convolved = (
        conv_weight[0] * mixed
        + mask_one * conv_weight[1] * extended[1:-1]
        + mask_two * conv_weight[2] * extended[:-2]
    )
    gated = (out_gate * convolved).astype(jnp.bfloat16)
    middle = stream + reduce_tp(contract_cols(gated, whole_out))
    normed_mid, inverse_mid, rms_mid = normalize(middle, norm2_gain)
    gate = jnp.dot(normed_mid, whole_gate, preferred_element_type=jnp.float32)
    upward = jnp.dot(normed_mid, whole_up, preferred_element_type=jnp.float32)
    hidden = (jax.nn.silu(gate) * upward).astype(jnp.bfloat16)
    result = middle + reduce_tp(contract_cols(hidden, whole_down))
    out_full = gather_grads(out_grad.astype(jnp.bfloat16))
    hidden_grad = jnp.dot(out_full, whole_down, preferred_element_type=jnp.float32)
    sigmoid_gate = jax.nn.sigmoid(gate)
    gate_rows = (hidden_grad * upward * sigmoid_gate * (1.0 + gate * (1.0 - sigmoid_gate))).astype(
        jnp.bfloat16
    )
    up_rows = (hidden_grad * gate * sigmoid_gate).astype(jnp.bfloat16)
    normed_mid_grad = reduce_tp(
        contract_cols(gate_rows, whole_gate) + contract_cols(up_rows, whole_up)
    )
    middle_norm_grad, gain_mid_grad = norm_backward(
        middle, norm2_gain, inverse_mid, normed_mid_grad
    )
    middle_grad = out_grad + middle_norm_grad
    branch_full = gather_grads(middle_grad.astype(jnp.bfloat16))
    gated_grad = jnp.dot(branch_full, whole_out, preferred_element_type=jnp.float32)
    out_gate_grad = gated_grad * convolved
    conv_grad = gated_grad * out_gate
    lag_one = mask_one * conv_grad
    lag_two = mask_two * conv_grad
    next_one, next_two = from_behind((lag_one[:2], lag_two[:2]), "seq", -1)
    after_one = jnp.concatenate([lag_one, next_one], axis=0)
    after_two = jnp.concatenate([lag_two, next_two], axis=0)
    mixed_grad = (
        conv_weight[0] * conv_grad
        + conv_weight[1] * after_one[1 : tokens + 1]
        + conv_weight[2] * after_two[2:]
    )
    tap_grads = jnp.stack(
        [
            jnp.sum(conv_grad * mixed, axis=0),
            jnp.sum(lag_one * extended[1:-1], axis=0),
            jnp.sum(lag_two * extended[:-2], axis=0),
        ]
    )
    projected_grad = jnp.concatenate(
        [mixed_grad * carried, out_gate_grad, mixed_grad * in_gate], axis=1
    ).astype(jnp.bfloat16)
    normed_in_grad = reduce_tp(contract_cols(projected_grad, in_matrix))
    stream_norm_grad, gain_in_grad = norm_backward(stream, norm1_gain, inverse_in, normed_in_grad)
    stream_grad = middle_grad + stream_norm_grad
    conv_total, gain_in_total, gain_mid_total = lax.psum(
        (tap_grads, gain_in_grad, gain_mid_grad), "seq"
    )
    everything = lax.psum_scatter(
        jnp.concatenate(
            [
                jnp.concatenate(
                    [contract_rows(normed_in, projected_grad), contract_rows(branch_full, gated)],
                    axis=1,
                ),
                jnp.concatenate(
                    [
                        contract_rows(normed_mid, gate_rows),
                        contract_rows(normed_mid, up_rows),
                        contract_rows(out_full, hidden),
                    ],
                    axis=1,
                ),
            ],
            axis=1,
        ),
        "seq",
        scatter_dimension=0,
        tiled=True,
    )
    mixer_cols = everything[:, : 4 * local]
    ffn_cols = everything[:, 4 * local :]
    in_weight_grad = mixer_cols[:, : 3 * local].reshape(rows_here, 3, local)
    out_weight_grad = mixer_cols[:, 3 * local :]
    gate_weight_grad = ffn_cols[:, :hidden_local]
    up_weight_grad = ffn_cols[:, hidden_local : 2 * hidden_local]
    down_weight_grad = ffn_cols[:, 2 * hidden_local :]
    rms_values = jnp.stack([rms_in, rms_mid])
    return (
        result,
        stream_grad,
        gain_in_total,
        in_weight_grad,
        conv_total,
        out_weight_grad,
        gain_mid_total,
        gate_weight_grad,
        up_weight_grad,
        down_weight_grad,
        rms_values,
    )


def solution(mesh):
    return jax.shard_map(
        on_device,
        mesh=mesh,
        in_specs=(
            P("seq", "tp"),
            P("tp"),
            P("seq", None, "tp"),
            P(None, "tp"),
            P("seq", "tp"),
            P("tp"),
            P("seq", "tp"),
            P("seq", "tp"),
            P("seq", "tp"),
            P(),
            P("seq", "tp"),
        ),
        out_specs=(
            P("seq", "tp"),
            P("seq", "tp"),
            P("tp"),
            P("seq", None, "tp"),
            P(None, "tp"),
            P("seq", "tp"),
            P("tp"),
            P("seq", "tp"),
            P("seq", "tp"),
            P("seq", "tp"),
            P(None, "seq"),
        ),
        check_vma=False,
    )
```

profile of v0, /device:TPU:0, one launch (start us, length us, event | category | flops | bytes accessed | tf_op | source)
XLA Modules:
  0.0 2155.1 jit_solution(179710486303152162)
XLA Ops:
  7.2 2.0 multiply_reduce_fusion.8
  9.2 8.4 psum.49
  18.8 1.9 multiply_convert_fusion.8
  20.8 1.2 copy.33
  22.0 0.7 all-gather.14.cloned.1.call-update
  22.9 32.8 %all-gather.10.cloned.1.call-done = bf16[1024,2048]{1,0:T(8,128)(2,1)} async-done(((bf16[1024,512]{1,0:T(8,128)(2,1)}), bf16[1024,2048]{1,0:T(8,128)(2,1)}) %all-gather.10.cloned.1.call-update) | async-done | bytes 4194320 | tf_op jit(solution)/shard_map/all_gather | solution.py:50
  55.7 102.6 %all-gather.12.cloned.1.call-done = bf16[2048,3,512]{0,2,1:T(8,128)(2,1)} async-done(((bf16[256,3,512]{0,2,1:T(8,128)(2,1)}), bf16[2048,3,512]{0,2,1:T(8,128)(2,1)}) %all-gather.12.cloned.1.call-update) | async-done | bytes 6291472 | tf_op jit(solution)/shard_map/all_gather | solution.py:83
  158.2 10.1 fusion.24
  168.9 3.4 collective-permute-start
  172.3 1.3 collective-permute-done
  173.5 2.2 multiply_convert_fusion.7
  175.7 32.2 %all-gather.14.cloned.1.call-done = bf16[2048,512]{1,0:T(8,128)(2,1)} async-done(((bf16[256,512]{1,0:T(8,128)(2,1)}), bf16[2048,512]{1,0:T(8,128)(2,1)}) %all-gather.14.cloned.1.call-update) | async-done | bytes 2097168 | tf_op jit(solution)/shard_map/all_gather | solution.py:84
  207.9 7.2 fusion.25
  215.8 69.7 %reduce-scatter.6.cloned.1.call-done = f32[1024,512]{1,0:T(8,128)} async-done(((f32[1024,2048]{1,0:T(8,128)}), f32[1024,512]{1,0:T(8,128)}) %reduce-scatter.6.cloned.1.call-update) | async-done | bytes 2097168 | tf_op jit(solution)/shard_map/reduce_scatter | solution.py:39
  285.5 3.1 multiply_reduce_fusion.7
  288.6 5.9 psum.50
  295.1 3.1 multiply_convert_fusion.6
  298.2 0.7 all-gather.18.cloned.1.call-update
  299.0 1.1 convert_element_type.57
  301.4 111.2 %all-gather.20.cloned.1.call-done = bf16[2048,2048]{1,0:T(8,128)(2,1)} async-done(((bf16[256,2048]{1,0:T(8,128)(2,1)}), bf16[2048,2048]{1,0:T(8,128)(2,1)}) %all-gather.20.cloned.1.call-update) | async-done | bytes 8388624 | tf_op jit(solution)/shard_map/all_gather | solution.py:86
  412.6 34.8 %all-gather.16.cloned.1.call-done = bf16[1024,2048]{1,0:T(8,128)(2,1)} async-done(((bf16[1024,512]{1,0:T(8,128)(2,1)}), bf16[1024,2048]{1,0:T(8,128)(2,1)}) %all-gather.16.cloned.1.call-update) | async-done | bytes 4194320 | tf_op jit(solution)/shard_map/all_gather | solution.py:50
  447.4 14.4 fusion.27
  461.8 112.9 %all-gather.18.cloned.1.call-done = bf16[2048,2048]{1,0:T(8,128)(2,1)} async-done(((bf16[256,2048]{1,0:T(8,128)(2,1)}), bf16[2048,2048]{1,0:T(8,128)(2,1)}) %all-gather.18.cloned.1.call-update) | async-done | bytes 8388624 | tf_op jit(solution)/shard_map/all_gather | solution.py:85
  574.7 14.4 fusion.26
  589.1 20.5 all-gather.24.cloned.1.call-done
  609.6 127.3 %all-gather.22.cloned.1.call-done = bf16[2048,2048]{1,0:T(8,128)(2,1)} async-done(((bf16[256,2048]{1,0:T(8,128)(2,1)}), bf16[2048,2048]{1,0:T(8,128)(2,1)}) %all-gather.22.cloned.1.call-update) | async-done | bytes 8388624 | tf_op jit(solution)/shard_map/all_gather | solution.py:87
  736.9 21.1 multiply_convert_fusion
  758.0 14.1 fusion.29
  772.1 13.3 convolution_add_fusion
  785.5 14.5 fusion.28
  800.1 55.4 %reduce-scatter.10.cloned.1.call-done = f32[1024,512]{1,0:T(8,128)} async-done(((f32[1024,2048]{1,0:T(8,128)}), f32[1024,512]{1,0:T(8,128)}) %reduce-scatter.10.cloned.1.call-update) | async-done | bytes 2097168 | tf_op jit(solution)/shard_map/reduce_scatter | solution.py:39
  855.6 2.2 multiply_reduce_fusion
  857.7 5.8 psum.51
  863.5 66.4 %reduce-scatter.8.cloned.1.call-done = f32[1024,512]{1,0:T(8,128)} async-done(((f32[1024,2048]{1,0:T(8,128)}), f32[1024,512]{1,0:T(8,128)}) %reduce-scatter.8.cloned.1.call-update) | async-done | bytes 2097168 | tf_op jit(solution)/shard_map/reduce_scatter | solution.py:39
  929.9 4.9 fusion.20
  934.9 34.6 %all-gather.26.cloned.1.call-done = bf16[1024,2048]{1,0:T(8,128)(2,1)} async-done(((bf16[1024,512]{1,0:T(8,128)(2,1)}), bf16[1024,2048]{1,0:T(8,128)(2,1)}) %all-gather.26.cloned.1.call-update) | async-done | bytes 4194320 | tf_op jit(solution)/shard_map/all_gather | solution.py:43
  969.5 5.3 fusion.30
  974.9 2.8 multiply_reduce_fusion.2
  977.7 1.3 collective-permute-start.2
  979.0 1.3 collective-permute-start.1
  980.3 2.9 collective-permute-done.2
  983.2 1.9 collective-permute-done.1
  985.1 2.9 multiply_convert_fusion.5
  987.9 1.9 multiply_convert_fusion.3
  989.9 8.8 fusion.5
  998.9 12.5 convolution_dynamic-update-slice_fusion.2
  1011.4 4.6 convolution_dynamic-update-slice_fusion.3
  1015.9 1.4 copy-done.26
  1017.4 11.6 convolution_dynamic-update-slice_fusion.1
  1029.0 11.6 convolution_dynamic-update-slice_fusion
  1040.6 11.8 bitcast_dynamic-update-slice_fusion
  1053.8 17.4 reduce-scatter.12.cloned.1.call-done
  1071.2 2.2 multiply_reduce_fusion.4
  1073.4 39.0 %all-reduce = (f32[512]{0:T(512)}, f32[3,512]{1,0:T(4,128)}, f32[512]{0:T(512)}) all-reduce(f32[512]{0:T(512)S(1)} %get-tuple-element.46, f32[3,512]{1,0:T(4,128)S(1)} %pad_maximum_fusion.6, f32[512]{0:T(512)S(1)} %get-tuple-element.44), channel_id=1, replica_groups=mesh['seq'=8,'tp'=4] {'seq'}, use_global_device_ids=true, to_apply=%region_16.17 | all-reduce | flops 2560 | bytes 20480 | tf_op jit(solution)/shard_map/psum | solution.py:154
  1112.4 6.0 psum.52
  1118.4 4.1 subtract_add_fusion
  1122.5 1008.3 %reduce-scatter.14.cloned.1.call-done = f32[256,8192]{0,1:T(8,128)} async-done(((f32[2048,8192]{0,1:T(8,128)}), f32[256,8192]{0,1:T(8,128)}) %reduce-scatter.14.cloned.1.call-update) | async-done | bytes 8388624 | tf_op jit(solution)/shard_map/reduce_scatter | solution.py:157
  2130.8 1.1 slice.93
  2131.9 1.0 copy.35
  2132.9 5.7 fusion.22
  2138.6 3.0 copy.38
  2141.6 1.6 copy.34
  2143.2 3.0 copy.37
  2146.2 1.8 copy.36
  (103 shorter events, 6.3 us)
Async XLA Ops:
  7.2 11.6 copy-start
  7.2 48.5 %all-gather.10.cloned.1.call-start = ((), (), s32[]{:S(2)}) async-start(), calls=%async_computation.5 | async-start | bytes 5242880 | tf_op jit(solution)/shard_map/all_gather | solution.py:50
  7.2 13.5 copy-start.11
  18.2 0.6 copy-start.12
  18.8 4.0 copy-start.20
  20.7 137.5 %all-gather.12.cloned.1.call-start = ((), (), s32[]{:S(2)}) async-start(), calls=%async_computation.6 | async-start | bytes 7077888 | tf_op jit(solution)/shard_map/all_gather | solution.py:83
  22.0 186.0 %all-gather.14.cloned.1.call-start = ((), (), s32[]{:S(2)}) async-start(), calls=%async_computation.7 | async-start | bytes 2359296 | tf_op jit(solution)/shard_map/all_gather | solution.py:84
  22.7 262.8 %reduce-scatter.6.cloned.1.call-start = ((), (), s32[]{:S(2)}) async-start(), calls=%async_computation.8 | async-start | bytes 10485760 | tf_op jit(solution)/shard_map/reduce_scatter | solution.py:39
  168.3 5.2 copy-start.3
  168.3 3.9 copy-start.19
  168.8 4.7 copy-start.4
  168.9 4.7 collective-permute-start
  175.7 39.4 %copy-start.9 = (bf16[1024,512]{1,0:T(8,128)(2,1)}, bf16[1024,512]{1,0:T(8,128)(2,1)S(1)}, u32[]{:S(2)}) copy-start(bf16[1024,512]{1,0:T(8,128)(2,1)S(1)} %get-tuple-element.70) | copy-start | bytes 3145732
  215.1 197.5 %all-gather.20.cloned.1.call-start = ((), (), s32[]{:S(2)}) async-start(), calls=%async_computation.11 | async-start | bytes 9437184 | tf_op jit(solution)/shard_map/all_gather | solution.py:86
  215.7 79.4 %copy-start.14 = (f32[512]{0:T(512)S(1)}, f32[512]{0:T(512)}, u32[]{:S(2)}) copy-start(f32[512]{0:T(512)} %param.16) | copy-start | bytes 6148
  215.7 231.7 %all-gather.16.cloned.1.call-start = ((), (), s32[]{:S(2)}) async-start(), calls=%async_computation.9 | async-start | bytes 5242880 | tf_op jit(solution)/shard_map/all_gather | solution.py:50
  288.6 10.4 copy-start.7
  298.2 276.5 %all-gather.18.cloned.1.call-start = ((), (), s32[]{:S(2)}) async-start(), calls=%async_computation.10 | async-start | bytes 9437184 | tf_op jit(solution)/shard_map/all_gather | solution.py:85
  298.9 310.7 %all-gather.24.cloned.1.call-start = ((), (), s32[]{:S(2)}) async-start(), calls=%async_computation.14 | async-start | bytes 5242880 | tf_op jit(solution)/shard_map/all_gather | solution.py:43
  300.1 436.8 %all-gather.22.cloned.1.call-start = ((), (), s32[]{:S(2)}) async-start(), calls=%async_computation.12 | async-start | bytes 9437184 | tf_op jit(solution)/shard_map/all_gather | solution.py:87
  300.9 554.7 %reduce-scatter.10.cloned.1.call-start = ((), (), s32[]{:S(2)}) async-start(), calls=%async_computation.15 | async-start | bytes 10485760 | tf_op jit(solution)/shard_map/reduce_scatter | solution.py:39
  758.0 14.1 copy-start.24
  785.5 144.4 %reduce-scatter.8.cloned.1.call-start = ((), (), s32[]{:S(2)}) async-start(), calls=%async_computation.13 | async-start | bytes 10485760 | tf_op jit(solution)/shard_map/reduce_scatter | solution.py:39
  800.1 55.5 %copy-start.2 = (f32[1024,512]{1,0:T(8,128)S(1)}, f32[1024,512]{1,0:T(8,128)}, u32[]{:S(2)}) copy-start(f32[1024,512]{1,0:T(8,128)} %get-tuple-element.69) | copy-start | bytes 6291460
  800.1 169.4 %all-gather.26.cloned.1.call-start = ((), (), s32[]{:S(2)}) async-start(), calls=%async_computation.16 | async-start | bytes 5242880 | tf_op jit(solution)/shard_map/all_gather | solution.py:43
  934.9 40.0 %copy-start.5 = (f32[1024,512]{1,0:T(8,128)S(1)}, f32[1024,512]{1,0:T(8,128)}, u32[]{:S(2)}) copy-start(f32[1024,512]{1,0:T(8,128)} %copy-done.4) | copy-start | bytes 6291460
  934.9 136.4 %reduce-scatter.12.cloned.1.call-start = ((), (), s32[]{:S(2)}) async-start(), calls=%async_computation.17 | async-start | bytes 10485760 | tf_op jit(solution)/shard_map/reduce_scatter | solution.py:39
  969.5 5.3 copy-start.6
  974.9 15.0 slice-start.1
  977.7 5.5 collective-permute-start.2
  979.0 6.1 collective-permute-start.1
  985.1 4.8 slice-start.2
  998.8 1132.0 %reduce-scatter.14.cloned.1.call-start = ((), (), s32[]{:S(2)}) async-start(), calls=%async_computation.18 | async-start | bytes 75497472 | tf_op jit(solution)/shard_map/reduce_scatter | solution.py:157
  998.8 12.5 copy-start.10
  998.9 12.5 copy-start.23
  1011.3 4.6 copy-start.21
  1011.3 6.0 copy-start.26
  1017.4 11.6 copy-start.25
  1029.0 11.6 copy-start.22
  1029.0 11.6 copy-start.27
  1052.5 0.7 copy-start.17
  1052.5 0.7 copy-start.18
  1052.5 18.7 copy-start.1
  1052.5 18.7 copy-start.13
  1052.5 18.7 copy-start.15
  1052.6 65.9 %copy-start.16 = (f32[1024,1]{0,1:T(1,128)S(1)}, f32[1024,1]{0,1:T(1,128)}, u32[]{:S(2)}) copy-start(f32[1024,1]{0,1:T(1,128)} %get-tuple-element.60) | copy-start | bytes 12292
  2138.6 3.0 slice-start
  2143.2 3.0 copy-start.8
Sparse Core Ops, SparseCore 0:
  20.9 34.7 all-gather.9
  58.3 99.9 all-gather.11
  160.4 47.5 all-gather.13
  215.3 70.1 reduce-scatter.5
  287.7 124.9 all-gather.19
  414.7 32.6 all-gather.15
  449.8 124.9 all-gather.17
  576.9 32.6 all-gather.23
  612.0 124.9 all-gather.21
  785.6 69.9 reduce-scatter.9
  858.1 71.7 reduce-scatter.7
  935.0 34.4 all-gather.25
  998.9 72.2 reduce-scatter.11
  1074.8 1055.9 reduce-scatter.13
where the time goes:
time: 2160 us
  waiting for transfers between devices  1830 us (85%)
  matrix products  175 us (8%)
  blocking collectives  65 us (3%)
  other arithmetic  36.7 us (2%)
    reduce_scatter x1, waiting for transfers between devices, on_device(): lax.psum_scatter(jnp.concatenate([jnp.concatenate([contract_rows(normed_i...  1010 us
    reduce_scatter x4, waiting for transfers between devices, reduce_tp(): return lax.psum_scatter(partial_rows, 'tp', scatter_dimension=1, tiled=True)  209 us
    all_gather x1, waiting for transfers between devices, on_device(): lax.all_gather(down_weight, 'seq', axis=0, tiled=True)  127 us
    all_gather x1, waiting for transfers between devices, on_device(): lax.all_gather(gate_weight, 'seq', axis=0, tiled=True)  113 us
    all_gather x1, waiting for transfers between devices, on_device(): lax.all_gather(up_weight, 'seq', axis=0, tiled=True)  111 us
    all_gather x1, waiting for transfers between devices, on_device(): lax.all_gather(in_weight, 'seq', axis=0, tiled=True)  103 us
    all_gather x2, waiting for transfers between devices, normalize(): lax.all_gather((values * inverse * gain).astype(jnp.bfloat16), 'tp', axis...  67.5 us
    dot_general x5, matrix products, contract_cols(): lax.dot_general(left, right, (((1,), (1,)), ((), ())), preferred_element_...  58 us
  transfers between devices with their start and end apart: 17, of which 17 were waited for; matrix products, arithmetic and copies ran while one was open for 6% of the time, Pallas kernels for 0%

commit v1 on v0

--- a/solution.py
+++ b/solution.py
@@ -36,7 +36,15 @@
 
 
 def reduce_tp(partial_rows):
-    return lax.psum_scatter(partial_rows, "tp", scatter_dimension=1, tiled=True)
+    return lax.psum_scatter(
+        partial_rows.astype(jnp.bfloat16), "tp", scatter_dimension=1, tiled=True
+    ).astype(jnp.float32)
+
+
+def reduce_seq(partial_grad):
+    return lax.psum_scatter(
+        partial_grad.astype(jnp.bfloat16), "seq", scatter_dimension=0, tiled=True
+    ).astype(jnp.float32)
 
 
 def gather_grads(grad_rows):
@@ -77,7 +85,6 @@
 ):
     tokens = stream.shape[0]
     local = stream.shape[1]
-    hidden_local = gate_weight.shape[1]
     rows_here = in_weight.shape[0]
     whole_in, whole_out, whole_gate, whole_up, whole_down = (
         lax.all_gather(in_weight, "seq", axis=0, tiled=True),
@@ -154,35 +161,13 @@
     conv_total, gain_in_total, gain_mid_total = lax.psum(
         (tap_grads, gain_in_grad, gain_mid_grad), "seq"
     )
-    everything = lax.psum_scatter(
-        jnp.concatenate(
-            [
-                jnp.concatenate(
-                    [contract_rows(normed_in, projected_grad), contract_rows(branch_full, gated)],
-                    axis=1,
-                ),
-                jnp.concatenate(
-                    [
-                        contract_rows(normed_mid, gate_rows),
-                        contract_rows(normed_mid, up_rows),
-                        contract_rows(out_full, hidden),
-                    ],
-                    axis=1,
-                ),
-            ],
-            axis=1,
-        ),
-        "seq",
-        scatter_dimension=0,
-        tiled=True,
-    )
-    mixer_cols = everything[:, : 4 * local]
-    ffn_cols = everything[:, 4 * local :]
-    in_weight_grad = mixer_cols[:, : 3 * local].reshape(rows_here, 3, local)
-    out_weight_grad = mixer_cols[:, 3 * local :]
-    gate_weight_grad = ffn_cols[:, :hidden_local]
-    up_weight_grad = ffn_cols[:, hidden_local : 2 * hidden_local]
-    down_weight_grad = ffn_cols[:, 2 * hidden_local :]
+    down_weight_grad = reduce_seq(contract_rows(out_full, hidden))
+    gate_weight_grad = reduce_seq(contract_rows(normed_mid, gate_rows))
+    up_weight_grad = reduce_seq(contract_rows(normed_mid, up_rows))
+    out_weight_grad = reduce_seq(contract_rows(branch_full, gated))
+    in_weight_grad = reduce_seq(contract_rows(normed_in, projected_grad)).reshape(
+        rows_here, 3, local
+    )
     rms_values = jnp.stack([rms_in, rms_mid])
     return (
         result,

time: 2160 us -> 1600 us (0.74)
  waiting for transfers between devices: 1830 us -> 1270 us
    reduce_scatter x5 -> x9, waiting for transfers between devices: 1220 us -> 685 us  [the longest x5 530 us: reduce_seq(): lax.psum_scatter(partial_grad.astype(jnp.bfloat16), 'seq', scatter_dimens...]
    all_gather x2, waiting for transfers between devices: 55.1 us -> 20.5 us  [gather_grads(): return lax.all_gather(grad_rows, 'tp', axis=1, tiled=True)]
  transfers between devices with their start and end apart: 17 -> 21, of which waited for: 17 -> 20; matrix products, arithmetic and copies ran while one was open for 6% -> 10% of each run, Pallas kernels for 0% -> 0%
where the time goes in v1:
time: 1600 us; the launch traced here: 1590 us
  waiting for transfers between devices  1270 us (79%)
  matrix products  181 us (11%)
  blocking collectives  65.1 us (4%)
  other arithmetic  43 us (3%)
    reduce_scatter x5, waiting for transfers between devices, reduce_seq(): lax.psum_scatter(partial_grad.astype(jnp.bfloat16), 'seq', scatter_dimens...  530 us
    reduce_scatter x4, waiting for transfers between devices, reduce_tp(): lax.psum_scatter(partial_rows.astype(jnp.bfloat16), 'tp', scatter_dimensi...  155 us
    all_gather x1, waiting for transfers between devices, on_device(): lax.all_gather(down_weight, 'seq', axis=0, tiled=True)  127 us
    all_gather x1, waiting for transfers between devices, on_device(): lax.all_gather(gate_weight, 'seq', axis=0, tiled=True)  113 us
    all_gather x1, waiting for transfers between devices, on_device(): lax.all_gather(up_weight, 'seq', axis=0, tiled=True)  112 us
    all_gather x1, waiting for transfers between devices, on_device(): lax.all_gather(in_weight, 'seq', axis=0, tiled=True)  103 us
    all_gather x2, waiting for transfers between devices, normalize(): lax.all_gather((values * inverse * gain).astype(jnp.bfloat16), 'tp', axis...  67.5 us
    dot_general x5, matrix products, contract_rows(): lax.dot_general(left, right, (((0,), (0,)), ((), ())), preferred_element_...  60 us
  transfers between devices with their start and end apart: 21, of which 20 were waited for; matrix products, arithmetic and copies ran while one was open for 10% of the time, Pallas kernels for 0%

profile of v1, /device:TPU:0, one launch (start us, length us, event | category | flops | bytes accessed | tf_op | source)
XLA Modules:
  0.0 1591.3 jit_solution(2467107204226462453)
XLA Ops:
  7.2 2.0 multiply_reduce_fusion.4
  9.2 8.4 psum.49
  18.8 1.9 multiply_convert_fusion.8
  20.8 1.2 copy.28
  22.9 32.7 %all-gather.10.cloned.1.call-done = bf16[1024,2048]{1,0:T(8,128)(2,1)} async-done(((bf16[1024,512]{1,0:T(8,128)(2,1)}), bf16[1024,2048]{1,0:T(8,128)(2,1)}) %all-gather.10.cloned.1.call-update) | async-done | bytes 4194320 | tf_op jit(solution)/shard_map/all_gather | solution.py:58
  55.7 102.6 %all-gather.12.cloned.1.call-done = bf16[2048,3,512]{0,2,1:T(8,128)(2,1)} async-done(((bf16[256,3,512]{0,2,1:T(8,128)(2,1)}), bf16[2048,3,512]{0,2,1:T(8,128)(2,1)}) %all-gather.12.cloned.1.call-update) | async-done | bytes 6291472 | tf_op jit(solution)/shard_map/all_gather | solution.py:90
  158.2 10.1 fusion.37
  168.8 3.4 collective-permute-start
  172.3 1.3 collective-permute-done
  174.1 2.2 multiply_convert_fusion.7
  176.3 31.6 %all-gather.14.cloned.1.call-done = bf16[2048,512]{1,0:T(8,128)(2,1)} async-done(((bf16[256,512]{1,0:T(8,128)(2,1)}), bf16[2048,512]{1,0:T(8,128)(2,1)}) %all-gather.14.cloned.1.call-update) | async-done | bytes 2097168 | tf_op jit(solution)/shard_map/all_gather | solution.py:91
  207.9 6.0 convolution_convert_fusion.5
  214.6 42.5 %reduce-scatter.10.cloned.1.call-done = bf16[1024,512]{1,0:T(8,128)(2,1)} async-done(((bf16[1024,2048]{1,0:T(8,128)(2,1)}), bf16[1024,512]{1,0:T(8,128)(2,1)}) %reduce-scatter.10.cloned.1.call-update) | async-done | bytes 1048592 | tf_op jit(solution)/shard_map/reduce_scatter | solution.py:39
  257.1 2.8 multiply_reduce_fusion.3
  259.9 5.9 psum.50
  266.4 3.1 multiply_convert_fusion.6
  272.4 111.8 %all-gather.20.cloned.1.call-done = bf16[2048,2048]{1,0:T(8,128)(2,1)} async-done(((bf16[256,2048]{1,0:T(8,128)(2,1)}), bf16[2048,2048]{1,0:T(8,128)(2,1)}) %all-gather.20.cloned.1.call-update) | async-done | bytes 8388624 | tf_op jit(solution)/shard_map/all_gather | solution.py:93
  384.2 34.8 %all-gather.16.cloned.1.call-done = bf16[1024,2048]{1,0:T(8,128)(2,1)} async-done(((bf16[1024,512]{1,0:T(8,128)(2,1)}), bf16[1024,2048]{1,0:T(8,128)(2,1)}) %all-gather.16.cloned.1.call-update) | async-done | bytes 4194320 | tf_op jit(solution)/shard_map/all_gather | solution.py:58
  419.0 14.4 fusion.39
  433.4 112.9 %all-gather.18.cloned.1.call-done = bf16[2048,2048]{1,0:T(8,128)(2,1)} async-done(((bf16[256,2048]{1,0:T(8,128)(2,1)}), bf16[2048,2048]{1,0:T(8,128)(2,1)}) %all-gather.18.cloned.1.call-update) | async-done | bytes 8388624 | tf_op jit(solution)/shard_map/all_gather | solution.py:92
  546.3 14.4 fusion.38
  560.7 20.5 %all-gather.24.cloned.1.call-done = bf16[1024,2048]{1,0:T(8,128)(2,1)} async-done(((bf16[1024,512]{1,0:T(8,128)(2,1)}), bf16[1024,2048]{1,0:T(8,128)(2,1)}) %all-gather.24.cloned.1.call-update) | async-done | bytes 4194320 | tf_op jit(solution)/shard_map/all_gather | solution.py:51
  581.2 127.3 %all-gather.22.cloned.1.call-done = bf16[2048,2048]{1,0:T(8,128)(2,1)} async-done(((bf16[256,2048]{1,0:T(8,128)(2,1)}), bf16[2048,2048]{1,0:T(8,128)(2,1)}) %all-gather.22.cloned.1.call-update) | async-done | bytes 8388624 | tf_op jit(solution)/shard_map/all_gather | solution.py:94
  708.6 21.2 %multiply_convert_fusion = (bf16[1024,2048]{1,0:T(8,128)(2,1)S(1)}, bf16[1024,2048]{1,0:T(8,128)(2,1)}, bf16[1024,2048]{1,0:T(8,128)(2,1)}) fusion(f32[1024,2048]{1,0:T(8,128)} %fusion.38, f32[1024,2048]{1,0:T(8,128)} %fusion.39, bf16[1024,2048]{1,0:T(8,128)(2,1)} %all-gather.24.cloned.1.call-done, bf16[2048,2048]{1,0:T(8,128)(2,1)} %all-gather.22.cloned.1.call-done), kind=kOutput, calls=%fused_computation.2 | convolution fusion | flops 8623489024 | bytes 41943040 | tf_op jit(solution)/shard_map/dot_general | solution.py:121
  729.7 14.0 fusion.40
  743.8 12.8 add_convert_fusion
  756.7 14.0 convolution_convert_fusion.4
  770.7 28.8 %reduce-scatter.14.cloned.1.call-done = bf16[1024,512]{1,0:T(8,128)(2,1)} async-done(((bf16[1024,2048]{1,0:T(8,128)(2,1)}), bf16[1024,512]{1,0:T(8,128)(2,1)}) %reduce-scatter.14.cloned.1.call-update) | async-done | bytes 1048592 | tf_op jit(solution)/shard_map/reduce_scatter | solution.py:39
  799.5 2.1 fusion.12
  801.6 5.8 psum.51
  807.4 39.1 %reduce-scatter.12.cloned.1.call-done = bf16[1024,512]{1,0:T(8,128)(2,1)} async-done(((bf16[1024,2048]{1,0:T(8,128)(2,1)}), bf16[1024,512]{1,0:T(8,128)(2,1)}) %reduce-scatter.12.cloned.1.call-update) | async-done | bytes 1048592 | tf_op jit(solution)/shard_map/reduce_scatter | solution.py:39
  846.5 4.3 fusion.33
  850.9 14.1 convolution_convert_fusion
  865.1 14.0 convolution_convert_fusion.1
  879.2 14.3 convert_bitcast_fusion
  893.6 1.1 copy-done.15
  894.7 6.1 convolution_convert_fusion.6
  901.0 5.3 fusion.41
  906.4 2.8 multiply_reduce_fusion.1
  909.3 1.3 collective-permute-start.2
  910.6 1.3 collective-permute-start.1
  911.9 2.9 collective-permute-done.2
  914.8 1.9 collective-permute-done.1
  916.7 2.9 multiply_convert_fusion.5
  919.6 2.4 multiply_convert_fusion.3
  922.9 8.6 convolution_convert_fusion.3
  931.6 1.2 copy-done.11
  933.2 11.4 convolution_convert_fusion.2
  945.9 92.7 %reduce-scatter.24.cloned.1.call-done = bf16[256,2048]{1,0:T(8,128)(2,1)} async-done(((bf16[2048,2048]{1,0:T(8,128)(2,1)}), bf16[256,2048]{1,0:T(8,128)(2,1)}) %reduce-scatter.24.cloned.1.call-update) | async-done | bytes 1048592 | tf_op jit(solution)/shard_map/reduce_scatter | solution.py:45
  1038.6 2.8 convert_element_type.130
  1041.4 148.7 %reduce-scatter.22.cloned.1.call-done = bf16[256,2048]{1,0:T(8,128)(2,1)} async-done(((bf16[2048,2048]{1,0:T(8,128)(2,1)}), bf16[256,2048]{1,0:T(8,128)(2,1)}) %reduce-scatter.22.cloned.1.call-update) | async-done | bytes 1048592 | tf_op jit(solution)/shard_map/reduce_scatter | solution.py:45
  1190.1 2.8 convert_element_type.128
  1192.9 149.5 %reduce-scatter.26.cloned.1.call-done = bf16[256,2048]{0,1:T(8,128)(2,1)} async-done(((bf16[2048,2048]{0,1:T(8,128)(2,1)}), bf16[256,2048]{0,1:T(8,128)(2,1)}) %reduce-scatter.26.cloned.1.call-update) | async-done | bytes 1048592 | tf_op jit(solution)/shard_map/reduce_scatter | solution.py:45
  1342.5 2.6 copy.31
  1345.0 67.6 %reduce-scatter.20.cloned.1.call-done = bf16[256,512]{1,0:T(8,128)(2,1)} async-done(((bf16[2048,512]{1,0:T(8,128)(2,1)}), bf16[256,512]{1,0:T(8,128)(2,1)}) %reduce-scatter.20.cloned.1.call-update) | async-done | bytes 262160 | tf_op jit(solution)/shard_map/reduce_scatter | solution.py:45
  1412.7 1.8 convert_element_type.126
  1414.5 44.1 %reduce-scatter.16.cloned.1.call-done = bf16[1024,512]{1,0:T(8,128)(2,1)} async-done(((bf16[1024,2048]{1,0:T(8,128)(2,1)}), bf16[1024,512]{1,0:T(8,128)(2,1)}) %reduce-scatter.16.cloned.1.call-update) | async-done | bytes 1048592 | tf_op jit(solution)/shard_map/reduce_scatter | solution.py:39
  1458.6 2.1 fusion.14
  1460.8 39.0 %all-reduce = (f32[512]{0:T(512)}, f32[3,512]{1,0:T(4,128)}, f32[512]{0:T(512)}) all-reduce(f32[512]{0:T(512)S(1)} %get-tuple-element.46, f32[3,512]{1,0:T(4,128)S(1)} %pad_maximum_fusion.6, f32[512]{0:T(512)S(1)} %get-tuple-element.44), channel_id=1, replica_groups=mesh['seq'=8,'tp'=4] {'seq'}, use_global_device_ids=true, to_apply=%region_16.17 | all-reduce | flops 2560 | bytes 20480 | tf_op jit(solution)/shard_map/psum | solution.py:161
  1499.8 6.0 psum.52
  1505.8 3.5 fusion.6
  1509.3 71.6 %reduce-scatter.18.cloned.1.call-done = bf16[256,1536]{1,0:T(8,128)(2,1)} async-done(((bf16[2048,1536]{1,0:T(8,128)(2,1)}), bf16[256,1536]{1,0:T(8,128)(2,1)}) %reduce-scatter.18.cloned.1.call-update) | async-done | bytes 786448 | tf_op jit(solution)/shard_map/reduce_scatter | solution.py:45
  1581.0 1.4 copy.29
  1582.4 1.6 copy.30
  (134 shorter events, 10.7 us)
Async XLA Ops:
  7.2 11.6 copy-start
  7.2 48.5 %all-gather.10.cloned.1.call-start = ((), (), s32[]{:S(2)}) async-start(), calls=%async_computation.9 | async-start | bytes 5242880 | tf_op jit(solution)/shard_map/all_gather | solution.py:58
  7.2 13.5 copy-start.16
  18.2 0.6 copy-start.17
  18.8 4.0 copy-start.37
  20.7 137.5 %all-gather.12.cloned.1.call-start = ((), (), s32[]{:S(2)}) async-start(), calls=%async_computation.10 | async-start | bytes 7077888 | tf_op jit(solution)/shard_map/all_gather | solution.py:90
  22.0 186.0 %all-gather.14.cloned.1.call-start = ((), (), s32[]{:S(2)}) async-start(), calls=%async_computation.11 | async-start | bytes 2359296 | tf_op jit(solution)/shard_map/all_gather | solution.py:91
  22.7 234.4 %reduce-scatter.10.cloned.1.call-start = ((), (), s32[]{:S(2)}) async-start(), calls=%async_computation.12 | async-start | bytes 5242880 | tf_op jit(solution)/shard_map/reduce_scatter | solution.py:39
  22.9 150.6 %copy-start.19 = (f32[1024]{0:T(1024)}, f32[1024]{0:T(1024)S(1)}, u32[]{:S(2)}) copy-start(f32[1024]{0:T(1024)S(1)} %get-tuple-element.82) | copy-start | bytes 12292
  22.9 150.6 %copy-start.21 = (f32[1024]{0:T(1024)}, f32[1024]{0:T(1024)S(1)}, u32[]{:S(2)}) copy-start(f32[1024]{0:T(1024)S(1)} %get-tuple-element.83) | copy-start | bytes 12292
  168.3 5.2 copy-start.3
  168.3 3.9 copy-start.36
  168.8 4.7 copy-start.4
  168.8 4.7 collective-permute-start
  172.2 1.3 copy-start.25
  172.3 1.3 copy-start.27
  172.3 1.3 copy-start.29
  173.5 0.6 copy-start.31
  176.3 37.6 %copy-start.14 = (bf16[1024,512]{1,0:T(8,128)(2,1)}, bf16[1024,512]{1,0:T(8,128)(2,1)S(1)}, u32[]{:S(2)}) copy-start(bf16[1024,512]{1,0:T(8,128)(2,1)S(1)} %get-tuple-element.70) | copy-start | bytes 3145732
  213.9 52.5 %copy-start.23 = (f32[512]{0:T(512)S(1)}, f32[512]{0:T(512)}, u32[]{:S(2)}) copy-start(f32[512]{0:T(512)} %param.16) | copy-start | bytes 6148
  213.9 170.3 %all-gather.20.cloned.1.call-start = ((), (), s32[]{:S(2)}) async-start(), calls=%async_computation.15 | async-start | bytes 9437184 | tf_op jit(solution)/shard_map/all_gather | solution.py:93
  214.5 204.5 %all-gather.16.cloned.1.call-start = ((), (), s32[]{:S(2)}) async-start(), calls=%async_computation.13 | async-start | bytes 5242880 | tf_op jit(solution)/shard_map/all_gather | solution.py:58
  259.9 10.4 copy-start.6
  269.5 276.8 %all-gather.18.cloned.1.call-start = ((), (), s32[]{:S(2)}) async-start(), calls=%async_computation.14 | async-start | bytes 9437184 | tf_op jit(solution)/shard_map/all_gather | solution.py:92
  270.2 311.0 %all-gather.24.cloned.1.call-start = ((), (), s32[]{:S(2)}) async-start(), calls=%async_computation.18 | async-start | bytes 5242880 | tf_op jit(solution)/shard_map/all_gather | solution.py:51
  271.4 437.1 %all-gather.22.cloned.1.call-start = ((), (), s32[]{:S(2)}) async-start(), calls=%async_computation.16 | async-start | bytes 9437184 | tf_op jit(solution)/shard_map/all_gather | solution.py:94
  272.2 527.3 %reduce-scatter.14.cloned.1.call-start = ((), (), s32[]{:S(2)}) async-start(), calls=%async_computation.19 | async-start | bytes 5242880 | tf_op jit(solution)/shard_map/reduce_scatter | solution.py:39
  729.7 14.0 copy-start.38
  756.6 89.9 %reduce-scatter.12.cloned.1.call-start = ((), (), s32[]{:S(2)}) async-start(), calls=%async_computation.17 | async-start | bytes 5242880 | tf_op jit(solution)/shard_map/reduce_scatter | solution.py:39
  770.6 28.9 %copy-start.2 = (f32[1024,512]{1,0:T(8,128)S(1)}, f32[1024,512]{1,0:T(8,128)}, u32[]{:S(2)}) copy-start(f32[1024,512]{1,0:T(8,128)} %get-tuple-element.69) | copy-start | bytes 6291460
  770.6 123.0 %all-gather.26.cloned.1.call-start = ((), (), s32[]{:S(2)}) async-start(), calls=%async_computation.20 | async-start | bytes 5242880 | tf_op jit(solution)/shard_map/all_gather | solution.py:51
  799.5 47.0 %copy-start.8 = (bf16[1024,512]{1,0:T(8,128)(2,1)S(1)}, bf16[1024,512]{1,0:T(8,128)(2,1)}, u32[]{:S(2)}) copy-start(bf16[1024,512]{1,0:T(8,128)(2,1)} %reduce-scatter.14.cloned.1.call-done) | copy-start | bytes 3145732
  850.8 187.8 %reduce-scatter.24.cloned.1.call-start = ((), (), s32[]{:S(2)}) async-start(), calls=%async_computation.25 | async-start | bytes 9437184 | tf_op jit(solution)/shard_map/reduce_scatter | solution.py:45
  865.0 325.1 %reduce-scatter.22.cloned.1.call-start = ((), (), s32[]{:S(2)}) async-start(), calls=%async_computation.24 | async-start | bytes 9437184 | tf_op jit(solution)/shard_map/reduce_scatter | solution.py:45
  879.1 463.3 %reduce-scatter.26.cloned.1.call-start = ((), (), s32[]{:S(2)}) async-start(), calls=%async_computation.26 | async-start | bytes 9437184 | tf_op jit(solution)/shard_map/reduce_scatter | solution.py:45
  893.5 1.2 copy-start.15
  893.5 519.1 %reduce-scatter.20.cloned.1.call-start = ((), (), s32[]{:S(2)}) async-start(), calls=%async_computation.23 | async-start | bytes 2359296 | tf_op jit(solution)/shard_map/reduce_scatter | solution.py:45
  900.9 5.4 copy-start.5
  900.9 5.4 copy-start.20
  900.9 5.4 copy-start.22
  901.0 5.4 copy-start.32
  901.0 557.6 %reduce-scatter.16.cloned.1.call-start = ((), (), s32[]{:S(2)}) async-start(), calls=%async_computation.21 | async-start | bytes 5242880 | tf_op jit(solution)/shard_map/reduce_scatter | solution.py:39
  901.0 5.4 copy-start.7
  906.4 10.3 copy-start.26
  906.4 10.3 copy-start.28
  906.4 10.3 copy-start.30
  906.4 16.5 %slice-start = ((s8[6291456]{0:T(1024)(128)(4,1)}), s8[4194304]{0:T(1024)(128)(4,1)S(1)}, s32[]{:S(2)}) async-start(s8[6291456]{0:T(1024)(128)(4,1)} %bitcast.77), calls=%async_computation.27 | async-start | bytes 8388608
  909.3 5.5 collective-permute-start.2
  910.6 6.1 collective-permute-start.1
  916.7 6.2 slice-start.1
  919.6 2.4 copy-start.10
  922.0 1.0 copy-start.12
  931.5 1.2 copy-start.11
  931.5 1.7 copy-start.13
  931.6 649.4 %reduce-scatter.18.cloned.1.call-start = ((), (), s32[]{:S(2)}) async-start(), calls=%async_computation.22 | async-start | bytes 7077888 | tf_op jit(solution)/shard_map/reduce_scatter | solution.py:45
  944.5 0.7 copy-start.34
  944.5 0.7 copy-start.35
  1041.4 417.2 %copy-start.1 = (f32[1024,512]{1,0:T(8,128)S(1)}, f32[1024,512]{1,0:T(8,128)}, u32[]{:S(2)}) copy-start(f32[1024,512]{1,0:T(8,128)} %param.11) | copy-start | bytes 6291460
  1041.4 417.2 %copy-start.18 = (f32[1024,1]{0,1:T(1,128)S(1)}, f32[1024,1]{0,1:T(1,128)}, u32[]{:S(2)}) copy-start(f32[1024,1]{0,1:T(1,128)} %copy-done.17) | copy-start | bytes 12292
  1041.4 417.2 %copy-start.24 = (f32[512]{0:T(512)S(1)}, f32[512]{0:T(512)}, u32[]{:S(2)}) copy-start(f32[512]{0:T(512)} %param.12) | copy-start | bytes 6148
  1192.9 312.9 %copy-start.33 = (f32[1024,1]{0,1:T(1,128)S(1)}, f32[1024,1]{0,1:T(1,128)}, u32[]{:S(2)}) copy-start(f32[1024,1]{0,1:T(1,128)} %get-tuple-element.60) | copy-start | bytes 12292
  1458.6 47.2 %copy-start.9 = (bf16[1024,512]{1,0:T(8,128)(2,1)S(1)}, bf16[1024,512]{1,0:T(8,128)(2,1)}, u32[]{:S(2)}) copy-start(bf16[1024,512]{1,0:T(8,128)(2,1)} %reduce-scatter.16.cloned.1.call-done) | copy-start | bytes 3145732
Sparse Core Ops, SparseCore 0:
  20.8 34.7 all-gather.9
  58.3 99.9 all-gather.11
  160.4 47.5 all-gather.13
  214.0 43.0 reduce-scatter.9
  259.3 124.9 all-gather.19
  386.3 32.6 all-gather.15
  421.4 124.9 all-gather.17
  548.5 32.6 all-gather.23
  583.6 124.9 all-gather.21
  756.7 42.6 reduce-scatter.13
  802.0 44.4 reduce-scatter.11
  851.0 34.4 all-gather.25
  889.5 149.0 reduce-scatter.23
  1042.1 147.9 reduce-scatter.21
  1194.0 148.3 reduce-scatter.25
  1345.8 66.7 reduce-scatter.19
  1415.0 43.5 reduce-scatter.15
  1462.5 118.4 reduce-scatter.17

commit v2 on v1

--- a/solution.py
+++ b/solution.py
@@ -1,7 +1,9 @@
 import jax
 import jax.numpy as jnp
 from jax import lax
-from jax.sharding import PartitionSpec as P
+from jax.experimental import pallas as pl
+from jax.experimental.pallas import tpu as pltpu
+from jax.sharding import Mesh, PartitionSpec as P
 
 epsilon = 1e-05
 
@@ -184,35 +186,814 @@
     )
 
 
+MESH = pl.DeviceIdType.MESH
+BF = jnp.bfloat16
+F32 = jnp.float32
+ANY = pl.BlockSpec(memory_space=pl.ANY)
+VMEM = pl.BlockSpec(memory_space=pltpu.VMEM)
+OWN, MATE, NEAR, FAR = 0, 1, 2, 3
+
+
+def remote(src, dst, send_sem, recv_sem, device):
+    return pltpu.make_async_remote_copy(
+        src_ref=src,
+        dst_ref=dst,
+        send_sem=send_sem,
+        recv_sem=recv_sem,
+        device_id=device,
+        device_id_type=MESH,
+    )
+
+
+class Place:
+    def __init__(self):
+        self.zh, self.zl = lax.axis_index("zh"), lax.axis_index("zl")
+        self.x, self.y, self.c = lax.axis_index("x"), lax.axis_index("y"), lax.axis_index("c")
+        self.z = 2 * self.zh + self.zl
+        self.inner = (self.z == 1) | (self.z == 2)
+        self.outer = (self.z == 0) | (self.z == 3)
+        self.rows = [self.z, 2 * self.zh + 1 - self.zl, 2 - self.zh, 3 - 3 * self.zh]
+        self.mate = (self.zh, 1 - self.zl, self.x, self.y, self.c)
+        self.mid = (1 - self.zh, 1 - self.zl, self.x, self.y, self.c)
+        self.across = (self.zh, self.zl, 1 - self.x, self.y, self.c)
+
+    def block(self, which, x):
+        return self.rows[which] * 2 + x
+
+    def enter(self):
+        barrier = pltpu.get_barrier_semaphore()
+
+        def greet(device):
+            pl.semaphore_signal(barrier, inc=1, device_id=device, device_id_type=MESH)
+
+        greet(self.mate)
+        greet(self.across)
+
+        @pl.when(self.inner)
+        def _():
+            greet(self.mid)
+
+        @pl.when(self.inner)
+        def _():
+            pl.semaphore_wait(barrier, 3)
+
+        @pl.when(self.outer)
+        def _():
+            pl.semaphore_wait(barrier, 2)
+
+
+def in_stages(chunks):
+    stages = len(chunks[0])
+    for step in range(len(chunks) + stages - 1):
+        for stage in range(stages):
+            if 0 <= step - stage < len(chunks):
+                chunks[step - stage][stage]()
+
+
+def pair_gather_chunk(p, weight, out, relay, ss, rs, first, count, rows):
+    half = out.shape[1]
+    here = pl.ds(first, count)
+    own = weight.at[here, pl.ds(pl.multiple_of(p.zl * half, half), half)]
+    other = weight.at[here, pl.ds(pl.multiple_of((1 - p.zl) * half, half), half)]
+
+    def block(which, x):
+        return out.at[pl.ds(pl.multiple_of(p.block(which, x) * rows + first, count), count), :]
+
+    held = [relay.at[i, here, :] for i in range(3)]
+
+    def send(slot, src, dst, recv, device):
+        return remote(src, dst, ss.at[slot], rs.at[recv], device)
+
+    def arrived(recv, dst):
+        remote(dst, dst, ss.at[0], rs.at[recv], p.mate).wait_recv()
+
+    local = pltpu.make_async_copy(own, block(OWN, p.x), ss.at[11])
+    across = [
+        send(7 + k, own if k == OWN else block(k, p.x), block(k, p.x), 6 + k, p.across)
+        for k in range(4)
+    ]
+    to_mate = send(0, other, block(OWN, p.x), 0, p.mate)
+    outer_own = send(1, own, held[0], 3, p.mate)
+    mid_other = send(3, other, block(OWN, p.x), 1, p.mid)
+    mid_own = send(4, own, held[1], 4, p.mid)
+    mid_far = send(5, held[0], block(MATE, p.x), 2, p.mid)
+    mid_far_own = send(6, block(MATE, p.x), held[2], 5, p.mid)
+    back_near = send(1, held[1], block(NEAR, p.x), 1, p.mate)
+    back_far = send(2, held[2], block(FAR, p.x), 2, p.mate)
+
+    def begin():
+        @pl.when(p.inner)
+        def _():
+            mid_other.start()
+            mid_own.start()
+
+        to_mate.start()
+
+        @pl.when(p.outer)
+        def _():
+            outer_own.start()
+
+        across[OWN].start()
+        local.start()
+
+    def mate_here():
+        arrived(0, block(MATE, p.x))
+
+        @pl.when(p.inner)
+        def _():
+            arrived(3, held[0])
+            mid_far.start()
+            mid_far_own.start()
+            arrived(4, held[1])
+            back_near.start()
+
+        across[MATE].start()
+
+    def near_here():
+        arrived(1, block(NEAR, p.x))
+        across[NEAR].start()
+
+        @pl.when(p.inner)
+        def _():
+            arrived(5, held[2])
+            back_far.start()
+
+    def far_here():
+        arrived(2, block(FAR, p.x))
+        across[FAR].start()
+
+    def finish():
+        for k in range(4):
+            arrived(6 + k, block(k, 1 - p.x))
+            across[k].wait_send()
+        local.wait()
+        to_mate.wait_send()
+
+        @pl.when(p.inner)
+        def _():
+            for copy in (mid_other, mid_own, mid_far, mid_far_own, back_near, back_far):
+                copy.wait_send()
+
+        @pl.when(p.outer)
+        def _():
+            outer_own.wait_send()
+
+    return [begin, mate_here, near_here, far_here, finish]
+
+
+def gather_pair(weights, collective, split=4):
+    n = len(weights)
+    rows, width = weights[0].shape
+    half = width // 2
+    count = rows // split
+
+    def kernel(*refs):
+        ins, outs = refs[:n], refs[n : 2 * n]
+        relay, ss, rs = refs[2 * n :]
+        p = Place()
+        p.enter()
+        in_stages(
+            [
+                pair_gather_chunk(
+                    p, ins[i], outs[i], relay.at[i], ss.at[i * split + c], rs.at[i * split + c],
+                    c * count, count, rows,
+                )
+                for i in range(n)
+                for c in range(split)
+            ]
+        )
+
+    return pl.pallas_call(
+        kernel,
+        out_shape=[jax.ShapeDtypeStruct((8 * rows, half), BF)] * n,
+        in_specs=[ANY] * n,
+        out_specs=[ANY] * n,
+        scratch_shapes=[
+            pltpu.VMEM((n, 3, rows, half), BF),
+            pltpu.SemaphoreType.DMA((n * split, 12)),
+            pltpu.SemaphoreType.DMA((n * split, 10)),
+        ],
+        compiler_params=pltpu.CompilerParams(
+            collective_id=collective, has_side_effects=True, vmem_limit_bytes=32 << 20
+        ),
+        cost_estimate=pl.CostEstimate(flops=0, bytes_accessed=n * (100 << 20), transcendentals=0),
+        name="gather_pair",
+    )(*weights)
+
+
+def line_gather_chunk(p, weight, out, ss, rs, first, count, rows):
+    own = weight.at[pl.ds(first, count), :]
+
+    def block(which, x):
+        return out.at[pl.ds(pl.multiple_of(p.block(which, x) * rows + first, count), count), :]
+
+    def send(slot, src, dst, recv, device):
+        return remote(src, dst, ss.at[slot], rs.at[recv], device)
+
+    def arrived(recv, dst):
+        remote(dst, dst, ss.at[0], rs.at[recv], p.mate).wait_recv()
+
+    local = pltpu.make_async_copy(own, block(OWN, p.x), ss.at[9])
+    across = [
+        send(k, own if k == OWN else block(k, p.x), block(k, p.x), 3 + k, p.across)
+        for k in range(4)
+    ]
+    to_mate = send(4, own, block(OWN, p.x), MATE - 1, p.mate)
+    to_mid = send(5, own, block(OWN, p.x), NEAR - 1, p.mid)
+    mid_far = send(6, block(MATE, p.x), block(MATE, p.x), FAR - 1, p.mid)
+    back_near = send(7, block(NEAR, p.x), block(NEAR, p.x), NEAR - 1, p.mate)
+    back_far = send(8, block(FAR, p.x), block(FAR, p.x), FAR - 1, p.mate)
+
+    def begin():
+        @pl.when(p.inner)
+        def _():
+            to_mid.start()
+
+        to_mate.start()
+        across[OWN].start()
+        local.start()
+
+    def mate_here():
+        arrived(MATE - 1, block(MATE, p.x))
+
+        @pl.when(p.inner)
+        def _():
+            mid_far.start()
+
+        across[MATE].start()
+
+    def near_here():
+        arrived(NEAR - 1, block(NEAR, p.x))
+
+        @pl.when(p.inner)
+        def _():
+            back_near.start()
+
+        across[NEAR].start()
+
+    def far_here():
+        arrived(FAR - 1, block(FAR, p.x))
+
+        @pl.when(p.inner)
+        def _():
+            back_far.start()
+
+        across[FAR].start()
+
+    def finish():
+        for k in range(4):
+            arrived(3 + k, block(k, 1 - p.x))
+            across[k].wait_send()
+        local.wait()
+        to_mate.wait_send()
+
+        @pl.when(p.inner)
+        def _():
+            for copy in (to_mid, mid_far, back_near, back_far):
+                copy.wait_send()
+
+    return [begin, mate_here, near_here, far_here, finish]
+
+
+def gather_line(weights, collective, split=2):
+    n = len(weights)
+    rows = weights[0].shape[0]
+    count = rows // split
+
+    def kernel(*refs):
+        ins, outs = refs[:n], refs[n : 2 * n]
+        ss, rs = refs[2 * n :]
+        p = Place()
+        p.enter()
+        in_stages(
+            [
+                line_gather_chunk(
+                    p, ins[i], outs[i], ss.at[i * split + c], rs.at[i * split + c],
+                    c * count, count, rows,
+                )
+                for i in range(n)
+                for c in range(split)
+            ]
+        )
+
+    return pl.pallas_call(
+        kernel,
+        out_shape=[jax.ShapeDtypeStruct((8 * rows, w.shape[1]), BF) for w in weights],
+        in_specs=[ANY] * n,
+        out_specs=[ANY] * n,
+        scratch_shapes=[
+            pltpu.SemaphoreType.DMA((n * split, 10)),
+            pltpu.SemaphoreType.DMA((n * split, 7)),
+        ],
+        compiler_params=pltpu.CompilerParams(
+            collective_id=collective, has_side_effects=True, vmem_limit_bytes=32 << 20
+        ),
+        cost_estimate=pl.CostEstimate(flops=0, bytes_accessed=n * (100 << 20), transcendentals=0),
+        name="gather_line",
+    )(*weights)
+
+
+def contract_tokens(left, right):
+    return lax.dot_general(left, right, (((0,), (0,)), ((), ())), preferred_element_type=F32)
+
+
+def scatter_pair(lefts, rights, which, collective):
+    n, nx = len(rights), len(lefts)
+    half = rights[0].shape[1]
+    rows = lefts[0].shape[1] // 8
+
+    def kernel(*refs):
+        left, right, out = refs[:nx], refs[nx : nx + n], refs[nx + n : nx + 2 * n]
+        sx, rx, sz, rz, rm, own, ss, rs = refs[nx + 2 * n :]
+        p = Place()
+        p.enter()
+
+        def product(i, k, x):
+            cols = pl.ds(pl.multiple_of(p.block(k, x) * rows, rows), rows)
+            return contract_tokens(left[which[i]][:, cols], right[i][...])
+
+        def across(i, k):
+            return remote(sx.at[i, k], rx.at[i, k], ss.at[i, k], rs.at[i, k], p.across)
+
+        def outward(i, j):
+            return remote(sz.at[i, j], rz.at[i, j], ss.at[i, 4 + j], rs.at[i, 4 + j], p.mate)
+
+        def middle(i, j):
+            return remote(sz.at[i, j], rm.at[i, j], ss.at[i, 7 + j], rs.at[i, 7 + j], p.mid)
+
+        def relay(i, j):
+            return remote(rz.at[i, j], rm.at[i, 2 + j], ss.at[i, 9 + j], rs.at[i, 9 + j], p.mid)
+
+        def forward(i):
+            return remote(rm.at[i, 0], rz.at[i, 0], ss.at[i, 4], rs.at[i, 4], p.mate)
+
+        def back(i):
+            return remote(sz.at[i, 2], rz.at[i, 1], ss.at[i, 5], rs.at[i, 5], p.mate)
+
+        def cols_of(place):
+            return pl.ds(pl.multiple_of(place * half, half), half)
+
+        def send_across(i):
+            for k in (FAR, NEAR, MATE, OWN):
+                sx[i, k] = product(i, k, 1 - p.x).astype(BF)
+                across(i, k).start()
+
+        def send_on(i, k, j):
+            total = product(i, k, p.x)
+            across(i, k).wait_recv()
+            sz[i, j] = (total + rx[i, k].astype(F32)).astype(BF)
+
+            @pl.when(p.outer)
+            def _():
+                outward(i, j).start()
+
+            @pl.when(p.inner)
+            def _():
+                middle(i, j).start()
+
+        def send_relay(i, j):
+            @pl.when(p.inner)
+            def _():
+                outward(i, j).wait_recv()
+                relay(i, j).start()
+
+        def mate_rows(i):
+            total = product(i, MATE, p.x)
+            across(i, MATE).wait_recv()
+            total = total + rx[i, MATE].astype(F32)
+
+            @pl.when(p.outer)
+            def _():
+                sz[i, 2] = total.astype(BF)
+                outward(i, 2).start()
+
+            @pl.when(p.inner)
+            def _():
+                own[i, 0] = total
+
+        def send_forward(i):
+            @pl.when(p.inner)
+            def _():
+                middle(i, 0).wait_recv()
+                forward(i).start()
+
+        def own_rows(i):
+            total = product(i, OWN, p.x)
+            across(i, OWN).wait_recv()
+            own[i, 1] = total + rx[i, OWN].astype(F32)
+
+        def finish(i):
+            @pl.when(p.inner)
+            def _():
+                relay(i, 0).wait_recv()
+                sz[i, 2] = (own[i, 0] + rm[i, 2].astype(F32)).astype(BF)
+                back(i).start()
+                relay(i, 1).wait_recv()
+                out[i][:, cols_of(p.zl)] = own[i, 1] + rm[i, 3].astype(F32)
+                outward(i, 2).wait_recv()
+                middle(i, 1).wait_recv()
+                out[i][:, cols_of(1 - p.zl)] = rz[i, 2].astype(F32) + rm[i, 1].astype(F32)
+
+            @pl.when(p.outer)
+            def _():
+                forward(i).wait_recv()
+                out[i][:, cols_of(p.zl)] = own[i, 1] + rz[i, 0].astype(F32)
+                back(i).wait_recv()
+                out[i][:, cols_of(1 - p.zl)] = rz[i, 1].astype(F32)
+                for j in range(3):
+                    outward(i, j).wait_send()
+
+            for k in range(4):
+                across(i, k).wait_send()
+
+            @pl.when(p.inner)
+            def _():
+                for j in range(2):
+                    middle(i, j).wait_send()
+                    relay(i, j).wait_send()
+                forward(i).wait_send()
+                back(i).wait_send()
+
+        send_across(0)
+        for i in range(n):
+            if i + 1 < n:
+                send_across(i + 1)
+            send_on(i, FAR, 0)
+            send_on(i, NEAR, 1)
+            send_relay(i, 0)
+            mate_rows(i)
+            send_relay(i, 1)
+            send_forward(i)
+            own_rows(i)
+            if i > 0:
+                finish(i - 1)
+        finish(n - 1)
+
+    return pl.pallas_call(
+        kernel,
+        out_shape=[jax.ShapeDtypeStruct((rows, 2 * half), F32)] * n,
+        in_specs=[VMEM] * (nx + n),
+        out_specs=[VMEM] * n,
+        scratch_shapes=[
+            pltpu.VMEM((n, 4, rows, half), BF),
+            pltpu.VMEM((n, 4, rows, half), BF),
+            pltpu.VMEM((n, 3, rows, half), BF),
+            pltpu.VMEM((n, 3, rows, half), BF),
+            pltpu.VMEM((n, 4, rows, half), BF),
+            pltpu.VMEM((n, 2, rows, half), F32),
+            pltpu.SemaphoreType.DMA((n, 11)),
+            pltpu.SemaphoreType.DMA((n, 11)),
+        ],
+        compiler_params=pltpu.CompilerParams(
+            collective_id=collective, has_side_effects=True, vmem_limit_bytes=60 << 20
+        ),
+        cost_estimate=pl.CostEstimate(flops=0, bytes_accessed=n * (150 << 20), transcendentals=0),
+        name="scatter_pair",
+    )(*lefts, *rights)
+
+
+def scatter_line(lefts, rights, which, collective):
+    n, nx, ny = len(which), len(lefts), len(rights)
+    rows = lefts[0].shape[1] // 8
+    width = min(r.shape[1] for r in rights)
+
+    def kernel(*refs):
+        left, right, out = refs[:nx], refs[nx : nx + ny], refs[nx + ny : nx + 2 * ny]
+        sx, rx, sz, rz, rm, own, ss, rs = refs[nx + 2 * ny :]
+        p = Place()
+        p.enter()
+
+        def product(i, k, x):
+            a, b, group = which[i]
+            cols = pl.ds(pl.multiple_of(p.block(k, x) * rows, rows), rows)
+            return contract_tokens(
+                left[a][:, cols], right[b][:, group * width : (group + 1) * width]
+            )
+
+        def across(i, k):
+            return remote(sx.at[i, k], rx.at[i, k], ss.at[i, k], rs.at[i, k], p.across)
+
+        def outward(i, j):
+            return remote(sz.at[i, j], rz.at[i, j], ss.at[i, 4 + j], rs.at[i, 4 + j], p.mate)
+
+        def middle(i, j):
+            return remote(sz.at[i, j], rm.at[i, j], ss.at[i, 7 + j], rs.at[i, 7 + j], p.mid)
+
+        def back(i):
+            return remote(sz.at[i, 2], rz.at[i, 0], ss.at[i, 4], rs.at[i, 4], p.mate)
+
+        def send_across(i):
+            for k in (FAR, NEAR, MATE, OWN):
+                sx[i, k] = product(i, k, 1 - p.x).astype(BF)
+                across(i, k).start()
+
+        def summed(i, k):
+            total = product(i, k, p.x)
+            across(i, k).wait_recv()
+            return total + rx[i, k].astype(F32)
+
+        def send_on(i, k, j):
+            total = summed(i, k)
+
+            @pl.when(p.outer)
+            def _():
+                sz[i, j] = total.astype(BF)
+                outward(i, j).start()
+
+            @pl.when(p.inner)
+            def _():
+                outward(i, j).wait_recv()
+                sz[i, j] = (total + rz[i, j].astype(F32)).astype(BF)
+                middle(i, j).start()
+
+        def mate_rows(i):
+            total = summed(i, MATE)
+
+            @pl.when(p.outer)
+            def _():
+                sz[i, 2] = total.astype(BF)
+                outward(i, 2).start()
+
+            @pl.when(p.inner)
+            def _():
+                own[i, 0] = total
+
+        def own_rows(i):
+            own[i, 1] = summed(i, OWN)
+
+        def finish(i):
+            b, group = which[i][1:]
+            here = pl.ds(group * width, width)
+
+            @pl.when(p.inner)
+            def _():
+                middle(i, 0).wait_recv()
+                sz[i, 2] = (own[i, 0] + rm[i, 0].astype(F32)).astype(BF)
+                back(i).start()
+                outward(i, 2).wait_recv()
+                middle(i, 1).wait_recv()
+                out[b][:, here] = own[i, 1] + rz[i, 2].astype(F32) + rm[i, 1].astype(F32)
+
+            @pl.when(p.outer)
+            def _():
+                back(i).wait_recv()
+                out[b][:, here] = own[i, 1] + rz[i, 0].astype(F32)
+                for j in range(3):
+                    outward(i, j).wait_send()
+
+            for k in range(4):
+                across(i, k).wait_send()
+
+            @pl.when(p.inner)
+            def _():
+                for j in range(2):
+                    middle(i, j).wait_send()
+                back(i).wait_send()
+
+        send_across(0)
+        for i in range(n):
+            if i + 1 < n:
+                send_across(i + 1)
+            send_on(i, FAR, 0)
+            send_on(i, NEAR, 1)
+            mate_rows(i)
+            own_rows(i)
+            if i > 0:
+                finish(i - 1)
+        finish(n - 1)
+
+    return pl.pallas_call(
+        kernel,
+        out_shape=[jax.ShapeDtypeStruct((rows, r.shape[1]), F32) for r in rights],
+        in_specs=[VMEM] * (nx + ny),
+        out_specs=[VMEM] * ny,
+        scratch_shapes=[
+            pltpu.VMEM((n, 4, rows, width), BF),
+            pltpu.VMEM((n, 4, rows, width), BF),
+            pltpu.VMEM((n, 3, rows, width), BF),
+            pltpu.VMEM((n, 3, rows, width), BF),
+            pltpu.VMEM((n, 2, rows, width), BF),
+            pltpu.VMEM((n, 2, rows, width), F32),
+            pltpu.SemaphoreType.DMA((n, 9)),
+            pltpu.SemaphoreType.DMA((n, 9)),
+        ],
+        compiler_params=pltpu.CompilerParams(
+            collective_id=collective, has_side_effects=True, vmem_limit_bytes=60 << 20
+        ),
+        cost_estimate=pl.CostEstimate(flops=0, bytes_accessed=n * (80 << 20), transcendentals=0),
+        name="scatter_line",
+    )(*lefts, *rights)
+
+
+SEQ = ("zh", "zl", "x")
+TP = ("y", "c")
+PAIR = ("zl", "y", "c")
+
+
+def after(value, *others):
+    return lax.optimization_barrier((value, *others))[0]
+
+
+def gather_pair_rows(rows):
+    tokens, local = rows.shape
+    pair, parts = lax.axis_size("zl"), lax.axis_size(TP)
+    blocks = lax.all_gather(rows, PAIR, axis=0).reshape(pair, parts, tokens, local)
+    return blocks.transpose(0, 2, 1, 3).reshape(pair * tokens, parts * local)
+
+
+def reduce_pair_rows(partial_rows):
+    pair, parts = lax.axis_size("zl"), lax.axis_size(TP)
+    tokens, local = partial_rows.shape[0] // pair, partial_rows.shape[1] // parts
+    blocks = partial_rows.astype(BF).reshape(pair, tokens, parts, local).transpose(0, 2, 1, 3)
+    return lax.psum_scatter(
+        blocks.reshape(pair * parts * tokens, local), PAIR, scatter_dimension=0, tiled=True
+    ).astype(F32)
+
+
+def reduce_features(partial_rows):
+    return lax.psum_scatter(
+        partial_rows.astype(BF), TP, scatter_dimension=1, tiled=True
+    ).astype(F32)
+
+
+def rms_scale(values, gain):
+    width = gain.shape[0] * lax.axis_size(TP)
+    squares = lax.psum(jnp.sum(values * values, axis=1, keepdims=True), TP)
+    inverse = lax.rsqrt(squares / width + epsilon)
+    return (values * inverse * gain).astype(BF), inverse, jnp.sqrt(squares[:, 0] / width + epsilon)
+
+
+def scale_backward(values, gain, inverse, grad_rows):
+    width = gain.shape[0] * lax.axis_size(TP)
+    gained = gain * grad_rows
+    total = lax.psum(jnp.sum(values * gained, axis=1, keepdims=True), TP)
+    grad_values = inverse * gained - values * inverse**3 * (total / width)
+    return grad_values, jnp.sum(grad_rows * values * inverse, axis=0)
+
+
+def dot(left, right):
+    return jnp.dot(left, right, preferred_element_type=F32)
+
+
+def paired_on_device(
+    stream,
+    norm1_gain,
+    in_weight,
+    conv_weight,
+    out_weight,
+    norm2_gain,
+    gate_weight,
+    up_weight,
+    down_weight,
+    doc_starts,
+    out_grad,
+):
+    tokens, local = stream.shape
+    rows_here = in_weight.shape[0]
+    positions = lax.axis_index(SEQ) * tokens + jnp.arange(tokens, dtype=jnp.int32)
+    mask_one, mask_two = lag_masks(doc_starts, positions)
+    normed_here, inverse_in, rms_in = rms_scale(stream, norm1_gain)
+    normed_in = lax.all_gather(normed_here, TP, axis=1, tiled=True)
+    in_matrix, whole_out = gather_line(
+        [after(in_weight.reshape(rows_here, 3 * local), normed_here), out_weight], 0
+    )
+    out_full = gather_pair_rows(after(out_grad.astype(BF), normed_in))
+    projected = dot(normed_in, in_matrix)
+    in_gate = projected[:, :local]
+    out_gate = projected[:, local : 2 * local]
+    carried = projected[:, 2 * local :]
+    mixed = in_gate * carried
+    previous = from_behind(mixed[-2:], SEQ, 1)
+    extended = jnp.concatenate([previous, mixed], axis=0)
+    convolved = (
+        conv_weight[0] * mixed
+        + mask_one * conv_weight[1] * extended[1:-1]
+        + mask_two * conv_weight[2] * extended[:-2]
+    )
+    gated = (out_gate * convolved).astype(BF)
+    mixer_partial = contract_cols(gated, whole_out).astype(BF)
+    mixer_out = reduce_features(mixer_partial)
+    (whole_gate,) = gather_pair([after(gate_weight, mixer_partial)], 1)
+    mixer_out = after(mixer_out, whole_gate)
+    middle = stream + mixer_out
+    normed_mid_here, inverse_mid, rms_mid = rms_scale(middle, norm2_gain)
+    normed_mid = gather_pair_rows(normed_mid_here)
+    (whole_up,) = gather_pair([after(up_weight, normed_mid_here)], 2)
+    normed_mid = after(normed_mid, whole_up)
+    gate = dot(normed_mid, whole_gate)
+    upward = dot(normed_mid, whole_up)
+    (whole_down,) = gather_pair([after(down_weight, whole_up)], 3)
+    sigmoid_gate = jax.nn.sigmoid(gate)
+    hidden = (gate * sigmoid_gate * upward).astype(BF)
+    hidden_grad = dot(out_full, whole_down)
+    gate_rows = (
+        hidden_grad * upward * sigmoid_gate * (1.0 + gate * (1.0 - sigmoid_gate))
+    ).astype(BF)
+    up_rows = (hidden_grad * gate * sigmoid_gate).astype(BF)
+    mid_partial = (contract_cols(gate_rows, whole_gate) + contract_cols(up_rows, whole_up)).astype(BF)
+    normed_mid_grad = reduce_pair_rows(mid_partial)
+    (down_weight_grad,) = scatter_pair([out_full], [after(hidden, mid_partial)], [0], 4)
+    normed_mid_grad = after(normed_mid_grad, down_weight_grad)
+    middle_norm_grad, gain_mid_grad = scale_backward(
+        middle, norm2_gain, inverse_mid, normed_mid_grad
+    )
+    middle_grad = out_grad + middle_norm_grad
+    branch_here = middle_grad.astype(BF)
+    branch_full = lax.all_gather(branch_here, TP, axis=1, tiled=True)
+    ffn_partial = contract_cols(hidden, whole_down)
+    result = middle + reduce_pair_rows(after(ffn_partial, branch_here))
+    gate_weight_grad, up_weight_grad = scatter_pair(
+        [normed_mid], [after(gate_rows, branch_here), up_rows], [0, 0], 5
+    )
+    branch_full = after(branch_full, gate_weight_grad)
+    gated_grad = dot(branch_full, whole_out)
+    out_gate_grad = gated_grad * convolved
+    conv_grad = gated_grad * out_gate
+    lag_one = mask_one * conv_grad
+    lag_two = mask_two * conv_grad
+    next_one, next_two = from_behind((lag_one[:2], lag_two[:2]), SEQ, -1)
+    after_one = jnp.concatenate([lag_one, next_one], axis=0)
+    after_two = jnp.concatenate([lag_two, next_two], axis=0)
+    mixed_grad = (
+        conv_weight[0] * conv_grad
+        + conv_weight[1] * after_one[1 : tokens + 1]
+        + conv_weight[2] * after_two[2:]
+    )
+    tap_grads = jnp.stack(
+        [
+            jnp.sum(conv_grad * mixed, axis=0),
+            jnp.sum(lag_one * extended[1:-1], axis=0),
+            jnp.sum(lag_two * extended[:-2], axis=0),
+        ]
+    )
+    projected_grad = jnp.concatenate(
+        [mixed_grad * carried, out_gate_grad, mixed_grad * in_gate], axis=1
+    ).astype(BF)
+    in_partial = contract_cols(projected_grad, in_matrix).astype(BF)
+    normed_in_grad = reduce_features(in_partial)
+    out_weight_grad, in_weight_grad = scatter_line(
+        [normed_in, branch_full],
+        [after(gated, in_partial), projected_grad],
+        [(1, 0, 0), (0, 1, 0), (0, 1, 1), (0, 1, 2)],
+        6,
+    )
+    normed_in_grad = after(normed_in_grad, in_weight_grad)
+    stream_norm_grad, gain_in_grad = scale_backward(stream, norm1_gain, inverse_in, normed_in_grad)
+    stream_grad = middle_grad + stream_norm_grad
+    conv_total, gain_in_total, gain_mid_total = lax.psum(
+        (tap_grads, gain_in_grad, gain_mid_grad), SEQ
+    )
+    return (
+        result,
+        stream_grad,
+        gain_in_total,
+        in_weight_grad.reshape(rows_here, 3, local),
+        conv_total,
+        out_weight_grad,
+        gain_mid_total,
+        gate_weight_grad,
+        up_weight_grad,
+        down_weight_grad,
+        jnp.stack([rms_in, rms_mid]),
+    )
+
+
 def solution(mesh):
+    seq, tp = mesh.shape["seq"], mesh.shape["tp"]
+    if (seq, tp) == (8, 4):
+        shape, names = (2, 2, 2, 2, 2), ("zh", "zl", "x", "y", "c")
+        mesh = Mesh(mesh.devices.reshape(shape), names)
+        body, rows, cols = paired_on_device, SEQ, TP
+    else:
+        body, rows, cols = on_device, "seq", "tp"
     return jax.shard_map(
-        on_device,
+        body,
         mesh=mesh,
         in_specs=(
-            P("seq", "tp"),
-            P("tp"),
-            P("seq", None, "tp"),
-            P(None, "tp"),
-            P("seq", "tp"),
-            P("tp"),
-            P("seq", "tp"),
-            P("seq", "tp"),
-            P("seq", "tp"),
+            P(rows, cols),
+            P(cols),
+            P(rows, None, cols),
+            P(None, cols),
+            P(rows, cols),
+            P(cols),
+            P(rows, cols),
+            P(rows, cols),
+            P(rows, cols),
             P(),
-            P("seq", "tp"),
+            P(rows, cols),
         ),
         out_specs=(
-            P("seq", "tp"),
-            P("seq", "tp"),
-            P("tp"),
-            P("seq", None, "tp"),
-            P(None, "tp"),
-            P("seq", "tp"),
-            P("tp"),
-            P("seq", "tp"),
-            P("seq", "tp"),
-            P("seq", "tp"),
-            P(None, "seq"),
+            P(rows, cols),
+            P(rows, cols),
+            P(cols),
+            P(rows, None, cols),
+            P(None, cols),
+            P(rows, cols),
+            P(cols),
+            P(rows, cols),
+            P(rows, cols),
+            P(rows, cols),
+            P(None, rows),
         ),
         check_vma=False,
     )

time: 1600 us -> 993 us (0.62)
  waiting for transfers between devices: 1270 us -> 6.55 us
  Pallas kernels: 0 us -> 616 us
  local copies, waits for them, and re-layouts: 12.4 us -> 116 us
  matrix products: 181 us -> 118 us
    reduce_scatter x9 -> x4, waiting for transfers between devices: 685 us -> 0.7 us  [the longest x2 0.7 us: reduce_pair_rows(): lax.psum_scatter(blocks.reshape(pair * parts * tokens, local), PAIR, scat...]
    pallas_call x0 -> x7, Pallas kernels: none -> 616 us  [the longest x2 215 us: scatter_pair(): pl.pallas_call(kernel, out_shape=[jax.ShapeDtypeStruct((rows, 2 * half),...]
    all_gather x9 -> x4, waiting for transfers between devices: 574 us -> 0.04 us  [the longest x1 0.02 us: paired_on_device(): normed_in = lax.all_gather(normed_here, TP, axis=1, tiled=True)]
    dot_general x10 -> x5, matrix products: 125 us -> 61.8 us  [dot(): return jnp.dot(left, right, preferred_element_type=F32)]
    reshape x1 -> x5, local copies, waits for them, and re-layouts: 1.4 us -> 58.4 us  [the longest x4 46.1 us: reduce_pair_rows(): partial_rows.astype(BF).reshape(pair, tokens, parts, local)]
    unnamed x85 -> x122, local copies, waits for them, and re-layouts: 10.9 us -> 43.4 us
  transfers between devices with their start and end apart: 21 -> 11, of which waited for: 20 -> 4; matrix products, arithmetic and copies ran while one was open for 10% -> 8% of each run, Pallas kernels for 0% -> 63%
where the time goes in v2:
time: 993 us; the launch traced here: 984 us
  Pallas kernels  616 us (62%)
  matrix products  118 us (12%)
  local copies, waits for them, and re-layouts  116 us (12%)
  blocking collectives  64.5 us (6%)
  other arithmetic  40.6 us (4%)
  between operations  15.1 us (2%)
    pallas_call x2, Pallas kernels, scatter_pair(): pl.pallas_call(kernel, out_shape=[jax.ShapeDtypeStruct((rows, 2 * half),...  215 us
    pallas_call x3, Pallas kernels, gather_pair(): pl.pallas_call(kernel, out_shape=[jax.ShapeDtypeStruct((8 * rows, half),...  179 us
    pallas_call x1, Pallas kernels, scatter_line(): pl.pallas_call(kernel, out_shape=[jax.ShapeDtypeStruct((rows, r.shape[1])...  126 us
    pallas_call x1, Pallas kernels, gather_line(): pl.pallas_call(kernel, out_shape=[jax.ShapeDtypeStruct((8 * rows, w.shape...  94.7 us
    dot_general x5, matrix products, dot(): return jnp.dot(left, right, preferred_element_type=F32)  61.8 us
    dot_general x5, matrix products, contract_cols(): lax.dot_general(left, right, (((1,), (1,)), ((), ())), preferred_element_...  56.7 us
    reshape x4, local copies, waits for them, and re-layouts, reduce_pair_rows(): partial_rows.astype(BF).reshape(pair, tokens, parts, local)  46.1 us
    unnamed x122, local copies, waits for them, and re-layouts  43.4 us
  transfers between devices with their start and end apart: 11, of which 4 were waited for; matrix products, arithmetic and copies ran while one was open for 8% of the time, Pallas kernels for 63%

profile of v2, /device:TPU:0, one launch (start us, length us, event | category | flops | bytes accessed | tf_op | source)
XLA Modules:
  0.0 983.9 jit_solution(7628265899356729401)
XLA Ops:
  7.2 1.9 multiply_reduce_fusion.8
  9.2 8.4 psum.49
  18.2 1.2 multiply_convert_fusion.8
  20.4 94.7 %gather_line.1 = (bf16[2048,1536]{1,0:T(8,128)(2,1)S(1)}, bf16[2048,512]{1,0:T(8,128)(2,1)S(1)}) custom-call(bf16[256,1536]{1,0:T(8,128)(2,1)S(1)} %copy.37.refs_0_, bf16[256,512]{1,0:T(8,128)(2,1)S(1)} %copy-done.10), custom_call_target="tpu_custom_call" | custom-call | bytes 209715200 | tf_op jit(solution)/shard_map/gather_line/pallas_call | solution.py:479
  115.1 2.7 copy-done.11
  118.0 10.6 %fusion.20 = f32[1024,1536]{1,0:T(8,128)S(1)} fusion(bf16[1024,2048]{1,0:T(8,128)(2,1)} %all-gather.7.cloned.1.call-done.refs_0_, bf16[2048,1536]{1,0:T(8,128)(2,1)} %copy-done.11), kind=kOutput, calls=%fused_computation.67 | convolution fusion | flops 6442450944 | bytes 16777216 | tf_op jit(solution)/shard_map/dot_general | solution.py:835
  129.1 3.4 collective-permute-start
  132.6 1.3 collective-permute-done
  133.9 2.2 multiply_convert_fusion.7
  137.1 4.4 convolution_convert_fusion.1
  141.6 1.5 copy-done.26
  143.1 1.1 convert_element_type.83
  144.3 53.6 %gather_pair.3 = bf16[2048,1024]{1,0:T(8,128)(2,1)S(1)} custom-call(bf16[256,2048]{1,0:T(8,128)(2,1)S(1)} %copy-done.7), custom_call_target="tpu_custom_call" | custom-call | bytes 104857600 | tf_op jit(solution)/shard_map/gather_pair/pallas_call | solution.py:366
  197.9 2.0 copy-done.2
  200.0 1.6 convert_element_type.80
  201.9 1.7 multiply_reduce_fusion.7
  203.5 6.3 psum.50
  210.5 2.9 multiply_convert_fusion.6
  213.5 60.4 %gather_pair.4 = bf16[2048,1024]{1,0:T(8,128)(2,1)S(1)} custom-call(bf16[256,2048]{1,0:T(8,128)(2,1)S(1)} %copy-done.8), custom_call_target="tpu_custom_call" | custom-call | bytes 104857600 | tf_op jit(solution)/shard_map/gather_pair/pallas_call | solution.py:366
  273.9 2.0 copy-done.4
  275.9 65.4 %gather_pair.5 = bf16[2048,1024]{1,0:T(8,128)(2,1)S(1)} custom-call(bf16[256,2048]{1,0:T(8,128)(2,1)S(1)} %copy-done.9), custom_call_target="tpu_custom_call" | custom-call | bytes 104857600 | tf_op jit(solution)/shard_map/gather_pair/pallas_call | solution.py:366
  341.3 2.0 copy-done
  343.3 12.3 %copy.39 = bf16[2,4,1024,512]{3,1,2,0:T(4,128)(2,1)} copy(bf16[2,4,1024,512]{3,2,1,0:T(8,128)(2,1)} %bitcast.69) | data formatting | bytes 16777216 | tf_op jit(solution)/shard_map/reshape | solution.py:800
  355.6 10.2 %copy.45 = bf16[256,8,4,512]{3,1,2,0:T(8,128)(2,1)} copy(bf16[256,8,4,512]{3,2,1,0:T(4,128)(2,1)} %bitcast.67) | data formatting | bytes 16777216
  365.8 12.2 %copy.38 = bf16[2,1024,4,512]{3,2,1,0:T(4,128)(2,1)} copy(bf16[2,1024,4,512]{3,1,2,0:T(8,128)(2,1)} %bitcast.70) | data formatting | bytes 16777216 | tf_op jit(solution)/shard_map/transpose | solution.py:801
  378.0 10.5 %copy.44 = bf16[256,8,4,512]{3,1,2,0:T(8,128)(2,1)} copy(bf16[256,8,4,512]{3,2,1,0:T(4,128)(2,1)} %bitcast.68) | data formatting | bytes 16777216
  388.5 13.8 %fusion.22 = f32[2048,1024]{1,0:T(8,128)} fusion(bf16[2048,2048]{1,0:T(8,128)(2,1)} %bitcast.63, bf16[2048,1024]{1,0:T(8,128)(2,1)S(1)} %copy-done.5), kind=kOutput, calls=%fused_computation.69 | convolution fusion | flops 8589934592 | bytes 20971520 | tf_op jit(solution)/shard_map/dot_general | solution.py:835
  402.3 11.1 %fusion.21 = f32[2048,1024]{1,0:T(8,128)} fusion(bf16[2048,2048]{1,0:T(8,128)(2,1)S(1)} %bitcast.65, bf16[2048,1024]{1,0:T(8,128)(2,1)S(1)} %copy-done.3), kind=kOutput, calls=%fused_computation.68 | convolution fusion | flops 8589934592 | bytes 20971520 | tf_op jit(solution)/shard_map/dot_general | solution.py:835
  413.4 21.7 %multiply_convert_fusion = (bf16[2048,1024]{1,0:T(8,128)(2,1)}, bf16[2048,1024]{1,0:T(8,128)(2,1)}, bf16[2048,1024]{1,0:T(8,128)(2,1)}) fusion(f32[2048,1024]{1,0:T(8,128)} %fusion.21, f32[2048,1024]{1,0:T(8,128)} %fusion.22, bf16[2048,2048]{1,0:T(8,128)(2,1)} %bitcast.60, bf16[2048,1024]{1,0:T(8,128)(2,1)S(1)} %copy-done.1), kind=kOutput, calls=%fused_computation.1 | convolution fusion | flops 8623489024 | bytes 41943040 | tf_op jit(solution)/shard_map/dot_general | solution.py:835
  435.1 15.4 %fusion.24 = f32[2048,2048]{1,0:T(8,128)} fusion(bf16[2048,1024]{1,0:T(8,128)(2,1)} %get-tuple-element.43.refs_1_, bf16[2048,1024]{1,0:T(8,128)(2,1)} %copy-done.2), kind=kOutput, calls=%fused_computation.71 | convolution fusion | flops 8589934592 | bytes 25165824 | tf_op jit(solution)/shard_map/dot_general | solution.py:35
  450.4 14.5 %add_convert_fusion = bf16[2048,2048]{1,0:T(8,128)(2,1)} fusion(f32[2048,2048]{1,0:T(8,128)} %fusion.24, bf16[2048,1024]{1,0:T(8,128)(2,1)S(1)} %copy-done.28, bf16[2048,1024]{1,0:T(8,128)(2,1)S(1)} %copy-done.6), kind=kOutput, calls=%fused_computation | convolution fusion | flops 8598323200 | bytes 33554432 | tf_op jit(solution)/shard_map/dot_general | solution.py:35
  465.0 14.6 %reshape.132 = bf16[2,1024,4,512]{3,2,1,0:T(4,128)(2,1)} reshape(bf16[2048,2048]{1,0:T(8,128)(2,1)} %add_convert_fusion) | data formatting | bytes 16777216 | tf_op jit(solution)/shard_map/reshape | solution.py:807
  479.5 8.4 copy.40
  488.0 90.1 %scatter_pair.2 = f32[256,2048]{1,0:T(8,128)} custom-call(bf16[2048,2048]{1,0:T(8,128)(2,1)} %bitcast.61, bf16[2048,1024]{1,0:T(8,128)(2,1)} %get-tuple-element.40.refs_1_), custom_call_target="tpu_custom_call" | custom-call | bytes 157286400 | tf_op jit(solution)/shard_map/scatter_pair/pallas_call | solution.py:632
  578.8 1.5 convert_element_type.87
  581.6 6.5 psum.51
  588.1 3.7 fusion.17
  591.9 125.4 %scatter_pair.3 = (f32[256,2048]{1,0:T(8,128)}, f32[256,2048]{1,0:T(8,128)}) custom-call(bf16[2048,2048]{1,0:T(8,128)(2,1)} %bitcast.64, bf16[2048,1024]{1,0:T(8,128)(2,1)} %get-tuple-element.43.refs_1_, bf16[2048,1024]{1,0:T(8,128)(2,1)} %get-tuple-element.112.refs_2_), custom_call_target="tpu_custom_call" | custom-call | bytes 314572800 | tf_op jit(solution)/shard_map/scatter_pair/pallas_call | solution.py:632
  717.4 4.7 fusion.25
  722.1 2.8 multiply_reduce_fusion.2
  725.0 1.3 collective-permute-start.1
  726.3 1.7 collective-permute-start.2
  728.0 2.5 collective-permute-done.1
  730.5 1.9 collective-permute-done.2
  732.5 2.9 multiply_convert_fusion.5
  735.3 1.9 multiply_convert_fusion.3
  737.3 8.3 convolution_convert_fusion
  745.7 14.1 %fusion.23 = bf16[2048,2048]{1,0:T(8,128)(2,1)} fusion(bf16[2048,1024]{1,0:T(8,128)(2,1)} %get-tuple-element.40.refs_1_, bf16[2048,1024]{1,0:T(8,128)(2,1)} %copy-done), kind=kOutput, calls=%fused_computation.70 | convolution fusion | flops 8589934592 | bytes 16777216 | tf_op jit(solution)/shard_map/dot_general | solution.py:35
  759.8 14.6 %reshape.134 = bf16[2,1024,4,512]{3,2,1,0:T(4,128)(2,1)} reshape(bf16[2048,2048]{1,0:T(8,128)(2,1)} %fusion.23) | data formatting | bytes 16777216 | tf_op jit(solution)/shard_map/reshape | solution.py:807
  774.4 8.5 copy.41
  784.3 1.8 pad_maximum_fusion.refs_3_
  786.0 126.3 %scatter_line.1 = (f32[256,512]{1,0:T(8,128)}, f32[256,1536]{1,0:T(8,128)}) custom-call(bf16[1024,2048]{1,0:T(8,128)(2,1)} %all-gather.7.cloned.1.call-done.refs_0_, bf16[1024,2048]{1,0:T(8,128)(2,1)} %all-gather.9.cloned.1.call-done.refs_1_, bf16[1024,512]{1,0:T(8,128)(2,1)} %copy-done.27, bf16[1024,1536]{1,0:T(8,128)(2,1)} %pad_maximum_fusion.refs_3_), custom_call_target="tpu_custom_call" | custom-call | bytes 335544320 | tf_op jit(solution)/shard_map/scatter_line/pallas_call | solution.py:765
  912.3 1.9 copy.42
  914.2 1.6 copy.43
  915.8 1.7 convert_element_type.92
  919.1 35.5 %all-reduce = (f32[512]{0:T(512)}, f32[3,512]{1,0:T(4,128)}, f32[512]{0:T(512)}) all-reduce(f32[512]{0:T(512)S(1)} %get-tuple-element.86, f32[3,512]{1,0:T(4,128)S(1)} %pad_maximum_fusion.4, f32[512]{0:T(512)S(1)} %get-tuple-element.84), channel_id=1, replica_groups=mesh['zh'=2,'zl'=2,'x'=2,'y'=2,'c'=2] {'zh','zl','x'}, use_global_device_ids=true, to_apply=%region_16.0 | all-reduce | flops 2560 | bytes 20480 | tf_op jit(solution)/shard_map/psum | solution.py:943
  954.5 7.8 psum.52
  962.4 4.1 subtract_add_fusion
  966.4 3.7 convert_add_fusion
  970.9 1.3 copy.51
  972.2 1.0 copy-done.29
  973.2 1.3 copy.52
  974.5 1.0 copy-done.24
  975.6 1.3 copy.53
  (152 shorter events, 10.3 us)
Async XLA Ops:
  7.2 11.0 %copy-start.14 = (f32[1024,512]{1,0:T(8,128)S(1)}, f32[1024,512]{1,0:T(8,128)}, u32[]{:S(2)}) copy-start(f32[1024,512]{1,0:T(8,128)} %param.11) | copy-start | bytes 6291460
  7.2 11.0 %copy-start.39 = (f32[512]{0:T(512)S(1)}, f32[512]{0:T(512)}, u32[]{:S(2)}) copy-start(f32[512]{0:T(512)} %param.12) | copy-start | bytes 6148
  7.2 110.8 %all-gather.7.cloned.1.call-start = ((), (), s32[]{:S(2)}) async-start(), calls=%async_computation.4 | async-start | bytes 5242880 | tf_op jit(solution)/shard_map/all_gather | solution.py:856
  18.2 1.2 copy-start.33
  18.2 1.3 copy-start.31
  19.4 180.5 %reduce-scatter.5.cloned.1.call-start = ((), (), s32[]{:S(2)}) async-start(), calls=%async_computation.5 | async-start | bytes 5242880 | tf_op jit(solution)/shard_map/reduce_scatter | solution.py:814
  19.5 98.3 %copy-start.54 = (s32[4]{0:T(128)S(1)}, s32[4]{0:T(128)}, u32[]{:S(2)}) copy-start(s32[4]{0:T(128)} %param.20) | copy-start | bytes 52
  115.1 2.7 copy-start.11
  117.8 18.3 %copy-start.12 = (bf16[2048,512]{1,0:T(8,128)(2,1)}, bf16[2048,512]{1,0:T(8,128)(2,1)S(1)}, u32[]{:S(2)}) copy-start(bf16[2048,512]{1,0:T(8,128)(2,1)S(1)} %get-tuple-element.33) | copy-start | bytes 6291460
  118.0 15.9 %copy-start.35 = (f32[1024]{0:T(1024)}, f32[1024]{0:T(1024)S(1)}, u32[]{:S(2)}) copy-start(f32[1024]{0:T(1024)S(1)} %get-tuple-element.121) | copy-start | bytes 12292
  118.0 15.9 %copy-start.37 = (f32[1024]{0:T(1024)}, f32[1024]{0:T(1024)S(1)}, u32[]{:S(2)}) copy-start(f32[1024]{0:T(1024)S(1)} %get-tuple-element.122) | copy-start | bytes 12292
  128.6 5.3 copy-start.19
  128.6 3.9 copy-start.53
  129.1 7.0 copy-start.20
  129.1 4.7 collective-permute-start
  132.6 3.5 copy-start.42
  132.6 3.5 copy-start.44
  132.6 3.5 copy-start.46
  133.9 2.3 copy-start.49
  141.5 1.6 copy-start.26
  141.5 2.7 copy-start.7
  141.5 201.8 %all-gather.13.cloned.1.call-start = ((), (), s32[]{:S(2)}) async-start(), calls=%async_computation.11 | async-start | bytes 9437184 | tf_op jit(solution)/shard_map/all_gather | solution.py:800
  144.2 221.6 %all-gather.11.cloned.1.call-start = ((), (), s32[]{:S(2)}) async-start(), calls=%async_computation.10 | async-start | bytes 9437184 | tf_op jit(solution)/shard_map/all_gather | solution.py:800
  197.9 2.1 copy-start.2
  199.9 1.9 copy-start.15
  201.9 8.6 copy-start.41
  210.5 3.0 copy-start.8
  213.4 62.5 %copy-start.9 = (bf16[256,2048]{1,0:T(8,128)(2,1)S(1)}, bf16[256,2048]{1,0:T(8,128)(2,1)}, u32[]{:S(2)}) copy-start(bf16[256,2048]{1,0:T(8,128)(2,1)} %refs_0_.2) | copy-start | bytes 3145732
  213.4 365.4 %reduce-scatter.7.cloned.1.call-start = ((), (), s32[]{:S(2)}) async-start(), calls=%async_computation.6 | async-start | bytes 9437184 | tf_op jit(solution)/shard_map/reduce_scatter | solution.py:808
  273.9 2.0 copy-start.4
  341.3 2.0 copy-start
  378.0 10.5 %copy-start.5 = (bf16[2048,1024]{1,0:T(8,128)(2,1)S(1)}, bf16[2048,1024]{1,0:T(8,128)(2,1)}, u32[]{:S(2)}) copy-start(bf16[2048,1024]{1,0:T(8,128)(2,1)} %copy-done.4) | copy-start | bytes 12582916
  388.5 13.9 %copy-start.3 = (bf16[2048,1024]{1,0:T(8,128)(2,1)S(1)}, bf16[2048,1024]{1,0:T(8,128)(2,1)}, u32[]{:S(2)}) copy-start(bf16[2048,1024]{1,0:T(8,128)(2,1)} %copy-done.2) | copy-start | bytes 12582916
  388.5 13.9 %copy-start.18 = (bf16[256,8,4,512]{3,1,2,0:T(8,128)(2,1)S(1)}, bf16[256,8,4,512]{3,1,2,0:T(8,128)(2,1)}, u32[]{:S(2)}) copy-start(bf16[256,8,4,512]{3,1,2,0:T(8,128)(2,1)} %copy.44) | copy-start | bytes 25165828
  402.3 11.1 %copy-start.1 = (bf16[2048,1024]{1,0:T(8,128)(2,1)S(1)}, bf16[2048,1024]{1,0:T(8,128)(2,1)}, u32[]{:S(2)}) copy-start(bf16[2048,1024]{1,0:T(8,128)(2,1)} %copy-done) | copy-start | bytes 12582916
  435.1 15.4 %copy-start.6 = (bf16[2048,1024]{1,0:T(8,128)(2,1)S(1)}, bf16[2048,1024]{1,0:T(8,128)(2,1)}, u32[]{:S(2)}) copy-start(bf16[2048,1024]{1,0:T(8,128)(2,1)} %copy-done.4) | copy-start | bytes 12582916
  435.1 15.4 %copy-start.28 = (bf16[2048,1024]{1,0:T(8,128)(2,1)S(1)}, bf16[2048,1024]{1,0:T(8,128)(2,1)}, u32[]{:S(2)}) copy-start(bf16[2048,1024]{1,0:T(8,128)(2,1)} %get-tuple-element.112.refs_2_) | copy-start | bytes 12582916
  488.0 229.3 %all-gather.9.cloned.1.call-start = ((), (), s32[]{:S(2)}) async-start(), calls=%async_computation.8 | async-start | bytes 5242880 | tf_op jit(solution)/shard_map/all_gather | solution.py:902
  578.1 2.2 copy-start.17
  580.3 1.3 copy-start.23
  591.9 125.5 %copy-start.13 = (bf16[2048,512]{1,0:T(8,128)(2,1)S(1)}, bf16[2048,512]{1,0:T(8,128)(2,1)}, u32[]{:S(2)}) copy-start(bf16[2048,512]{1,0:T(8,128)(2,1)} %copy-done.12) | copy-start | bytes 6291460
  591.9 324.0 %reduce-scatter.11.cloned.1.call-start = ((), (), s32[]{:S(2)}) async-start(), calls=%async_computation.9 | async-start | bytes 5242880 | tf_op jit(solution)/shard_map/reduce_scatter | solution.py:814
  717.3 4.7 copy-start.21
  717.3 4.7 copy-start.25
  717.4 4.7 copy-start.36
  717.4 4.7 copy-start.38
  717.4 4.7 copy-start.50
  722.1 10.3 %copy-start.43 = (f32[1,512]{1,0:T(1,128)S(1)}, f32[1,512]{1,0:T(1,128)}, u32[]{:S(2)}) copy-start(f32[1,512]{1,0:T(1,128)} %copy-done.42) | copy-start | bytes 6148
  722.1 10.3 %copy-start.45 = (f32[1,512]{1,0:T(1,128)S(1)}, f32[1,512]{1,0:T(1,128)}, u32[]{:S(2)}) copy-start(f32[1,512]{1,0:T(1,128)} %copy-done.44) | copy-start | bytes 6148
  722.1 10.3 %copy-start.47 = (f32[1,512]{1,0:T(1,128)S(1)}, f32[1,512]{1,0:T(1,128)}, u32[]{:S(2)}) copy-start(f32[1,512]{1,0:T(1,128)} %copy-done.46) | copy-start | bytes 6148
  722.1 15.1 %slice-start = ((s8[6291456]{0:T(1024)(128)(4,1)}), s8[4194304]{0:T(1024)(128)(4,1)S(1)}, s32[]{:S(2)}) async-start(s8[6291456]{0:T(1024)(128)(4,1)} %bitcast.58), calls=%async_computation.12 | async-start | bytes 8388608
  725.0 5.5 collective-permute-start.1
  726.3 6.1 collective-permute-start.2
  732.5 4.8 slice-start.1
  745.6 220.8 %reduce-scatter.9.cloned.1.call-start = ((), (), s32[]{:S(2)}) async-start(), calls=%async_computation.7 | async-start | bytes 9437184 | tf_op jit(solution)/shard_map/reduce_scatter | solution.py:808
  915.8 1.9 copy-start.16
  915.8 1.9 copy-start.34
  915.8 1.9 copy-start.40
  917.7 1.3 copy-start.22
  917.7 44.6 %copy-start.48 = (f32[1024,1]{0,1:T(1,128)S(1)}, f32[1024,1]{0,1:T(1,128)}, u32[]{:S(2)}) copy-start(f32[1024,1]{0,1:T(1,128)} %get-tuple-element.100) | copy-start | bytes 12292
  966.4 3.7 copy-start.32
  966.4 4.5 copy-start.30
  970.9 2.3 copy-start.29
  973.2 2.3 copy-start.24
  (4 other events, 3.3 us)
Sparse Core Ops, SparseCore 0:
  19.6 34.7 all-gather.6
  141.6 44.4 reduce-scatter.4
  188.4 61.4 all-gather.12
  252.0 67.7 all-gather.10
  488.1 90.6 reduce-scatter.6
  592.0 34.3 all-gather.8
  745.8 46.6 reduce-scatter.10
  794.8 110.3 reduce-scatter.8

commit v3 on v2

--- a/solution.py
+++ b/solution.py
@@ -194,6 +194,10 @@
 OWN, MATE, NEAR, FAR = 0, 1, 2, 3
 
 
+def dot(left, right):
+    return jnp.dot(left, right, preferred_element_type=F32)
+
+
 def remote(src, dst, send_sem, recv_sem, device):
     return pltpu.make_async_remote_copy(
         src_ref=src,
@@ -220,7 +224,7 @@
     def block(self, which, x):
         return self.rows[which] * 2 + x
 
-    def enter(self):
+    def enter(self, *others):
         barrier = pltpu.get_barrier_semaphore()
 
         def greet(device):
@@ -228,6 +232,8 @@
 
         greet(self.mate)
         greet(self.across)
+        for device in others:
+            greet(device)
 
         @pl.when(self.inner)
         def _():
@@ -235,11 +241,11 @@
 
         @pl.when(self.inner)
         def _():
-            pl.semaphore_wait(barrier, 3)
+            pl.semaphore_wait(barrier, 3 + len(others))
 
         @pl.when(self.outer)
         def _():
-            pl.semaphore_wait(barrier, 2)
+            pl.semaphore_wait(barrier, 2 + len(others))
 
 
 def in_stages(chunks):
@@ -381,6 +387,97 @@
     )(*weights)
 
 
+def gather_down_and_hidden(weight, normed, gate, up, collective, split=4):
+    rows, width = weight.shape
+    half = width // 2
+    pair, owners, tokens, local = normed.shape
+    count = rows // split
+    tile = pair * tokens // 8
+
+    def kernel(*refs):
+        weight_ref, normed_ref, gate_ref, up_ref = refs[:4]
+        down_ref, hidden_ref, silu_ref, slope_ref = refs[4:8]
+        relay, x, results, ss, rs, x_sem, result_sem = refs[8:]
+
+        def loads(m, act):
+            start = m % (8 // pair) * tile
+            for j in range(owners):
+                copy = pltpu.make_async_copy(
+                    normed_ref.at[m // (8 // pair), j, pl.ds(start, tile), :],
+                    x.at[m % 2, :, pl.ds(j * local, local)],
+                    x_sem.at[m % 2, j],
+                )
+                getattr(copy, act)()
+
+        def stores(m, act):
+            for i, ref in enumerate((hidden_ref, silu_ref, slope_ref)):
+                copy = pltpu.make_async_copy(
+                    results.at[m % 2, i], ref.at[pl.ds(m * tile, tile), :], result_sem.at[m % 2, i]
+                )
+                getattr(copy, act)()
+
+        loads(0, "start")
+        loads(1, "start")
+        p = Place()
+        p.enter()
+        chunks = [
+            pair_gather_chunk(
+                p, weight_ref, down_ref, relay.at[0], ss.at[c], rs.at[c], c * count, count, rows
+            )
+            for c in range(split)
+        ]
+
+        def compute(m):
+            loads(m, "wait")
+            if m >= 2:
+                stores(m - 2, "wait")
+            for part in range(2):
+                here = pl.ds(part * half // 2, half // 2)
+                value = dot(x[m % 2], gate_ref[:, here])
+                upward = dot(x[m % 2], up_ref[:, here])
+                sigmoid = jax.nn.sigmoid(value)
+                silu = value * sigmoid
+                results[m % 2, 0, :, here] = (silu * upward).astype(BF)
+                results[m % 2, 1, :, here] = silu.astype(BF)
+                results[m % 2, 2, :, here] = (
+                    upward * (sigmoid + silu * (1.0 - sigmoid))
+                ).astype(BF)
+            stores(m, "start")
+            if m + 2 < 8:
+                loads(m + 2, "start")
+
+        for step in range(split + 4):
+            for stage in range(5):
+                if 0 <= step - stage < split:
+                    chunks[step - stage][stage]()
+            for m in range(step * 8 // (split + 4), (step + 1) * 8 // (split + 4)):
+                compute(m)
+        stores(6, "wait")
+        stores(7, "wait")
+
+    units = jax.ShapeDtypeStruct((pair * tokens, half), BF)
+    return pl.pallas_call(
+        kernel,
+        out_shape=[jax.ShapeDtypeStruct((8 * rows, half), BF), units, units, units],
+        in_specs=[ANY, ANY, VMEM, VMEM],
+        out_specs=[ANY] * 4,
+        scratch_shapes=[
+            pltpu.VMEM((1, 3, rows, half), BF),
+            pltpu.VMEM((2, tile, owners * local), BF),
+            pltpu.VMEM((2, 3, tile, half), BF),
+            pltpu.SemaphoreType.DMA((split, 12)),
+            pltpu.SemaphoreType.DMA((split, 10)),
+            pltpu.SemaphoreType.DMA((2, owners)),
+            pltpu.SemaphoreType.DMA((2, 3)),
+        ],
+        compiler_params=pltpu.CompilerParams(
+            collective_id=collective, has_side_effects=True, vmem_limit_bytes=48 << 20
+        ),
+        cost_estimate=pl.CostEstimate(flops=0, bytes_accessed=100 << 20, transcendentals=0),
+        name="gather_down_and_hidden",
+    )(weight, normed, gate, up)
+
+
 def line_gather_chunk(p, weight, out, ss, rs, first, count, rows):
     own = weight.at[pl.ds(first, count), :]
 
@@ -497,159 +594,223 @@
     return lax.dot_general(left, right, (((0,), (0,)), ((), ())), preferred_element_type=F32)
 
 
-def scatter_pair(lefts, rights, which, collective):
-    n, nx = len(rights), len(lefts)
-    half = rights[0].shape[1]
-    rows = lefts[0].shape[1] // 8
-
-    def kernel(*refs):
-        left, right, out = refs[:nx], refs[nx : nx + n], refs[nx + n : nx + 2 * n]
-        sx, rx, sz, rz, rm, own, ss, rs = refs[nx + 2 * n :]
+class PairScatter:
+    def __init__(self, p, product, sx, rx, sz, rz, rm, held, out, ss, rs):
+        self.p, self.product = p, product
+        self.sx, self.rx, self.sz, self.rz, self.rm = sx, rx, sz, rz, rm
+        self.held, self.out, self.ss, self.rs = held, out, ss, rs
+        self.half = held.shape[1]
+
+    def across(self, k):
+        return remote(self.sx.at[k], self.rx.at[k], self.ss.at[k], self.rs.at[k], self.p.across)
+
+    def outward(self, j):
+        return remote(self.sz.at[j], self.rz.at[j], self.ss.at[4 + j], self.rs.at[4 + j], self.p.mate)
+
+    def middle(self, j):
+        return remote(self.sz.at[j], self.rm.at[j], self.ss.at[7 + j], self.rs.at[7 + j], self.p.mid)
+
+    def relay(self, j):
+        return remote(
+            self.rz.at[j], self.rm.at[2 + j], self.ss.at[9 + j], self.rs.at[9 + j], self.p.mid
+        )
+
+    def forward(self):
+        return remote(self.rm.at[0], self.rz.at[0], self.ss.at[4], self.rs.at[4], self.p.mate)
+
+    def back(self):
+        return remote(self.sz.at[2], self.rz.at[1], self.ss.at[5], self.rs.at[5], self.p.mate)
+
+    def cols_of(self, place):
+        return pl.ds(pl.multiple_of(place * self.half, self.half), self.half)
+
+    def send_across(self, k, *sent):
+        self.sx[k] = self.product(k, 1 - self.p.x).astype(BF)
+        self.sent(*sent)
+        self.across(k).start()
+
+    def summed(self, k):
+        total = self.product(k, self.p.x)
+        self.across(k).wait_recv()
+        return total + self.rx[k].astype(F32)
+
+    def send_on(self, k, j):
+        self.sz[j] = self.summed(k).astype(BF)
+
+        @pl.when(self.p.outer)
+        def _():
+            self.outward(j).start()
+
+        @pl.when(self.p.inner)
+        def _():
+            self.middle(j).start()
+
+    def send_relay(self, j):
+        @pl.when(self.p.inner)
+        def _():
+            self.outward(j).wait_recv()
+            self.relay(j).start()
+
+    def mate_rows(self):
+        total = self.summed(MATE)
+
+        @pl.when(self.p.outer)
+        def _():
+            self.sz[2] = total.astype(BF)
+            self.outward(2).start()
+
+        @pl.when(self.p.inner)
+        def _():
+            self.held[...] = total
+
+    def send_forward(self):
+        @pl.when(self.p.inner)
+        def _():
+            self.middle(0).wait_recv()
+            self.forward().start()
+
+    def own_rows(self):
+        self.out[:, self.cols_of(self.p.zl)] = self.summed(OWN)
+
+    def send_back(self):
+        @pl.when(self.p.inner)
+        def _():
+            self.relay(0).wait_recv()
+            self.sz[2] = (self.held[...] + self.rm[2].astype(F32)).astype(BF)
+            self.back().start()
+
+    def finish(self):
+        p, out = self.p, self.out
+        here, there = self.cols_of(p.zl), self.cols_of(1 - p.zl)
+
+        @pl.when(p.inner)
+        def _():
+            self.relay(1).wait_recv()
+            out[:, here] = out[:, here] + self.rm[3].astype(F32)
+            self.outward(2).wait_recv()
+            self.middle(1).wait_recv()
+            out[:, there] = self.rz[2].astype(F32) + self.rm[1].astype(F32)
+
+        @pl.when(p.outer)
+        def _():
+            self.forward().wait_recv()
+            out[:, here] = out[:, here] + self.rz[0].astype(F32)
+            self.back().wait_recv()
+            out[:, there] = self.rz[1].astype(F32)
+
+        @pl.when(p.inner)
+        def _():
+            for j in range(2):
+                self.relay(j).wait_send()
+            self.forward().wait_send()
+
+    def sent_on(self):
+        @pl.when(self.p.outer)
+        def _():
+            for j in range(3):
+                self.outward(j).wait_send()
+
+        @pl.when(self.p.inner)
+        def _():
+            for j in range(2):
+                self.middle(j).wait_send()
+            self.back().wait_send()
+
+    def sent(self, *which):
+        for k in which:
+            self.across(k).wait_send()
+
+
+def pair_scatter_scratch(n, rows, half):
+    return [
+        pltpu.VMEM((4, rows, half), BF),
+        pltpu.VMEM((n, 4, rows, half), BF),
+        pltpu.VMEM((3, rows, half), BF),
+        pltpu.VMEM((n, 3, rows, half), BF),
+        pltpu.VMEM((n, 4, rows, half), BF),
+        pltpu.VMEM((rows, half), F32),
+        pltpu.SemaphoreType.DMA((n, 11)),
+        pltpu.SemaphoreType.DMA((n, 11)),
+    ]
+
+
+class Columns:
+    def __init__(self, p, jobs, buffer, sems):
+        self.p, self.jobs, self.buffer, self.sems, self.at = p, jobs, buffer, sems, 0
+        for n in range(min(2, len(jobs))):
+            self.copies(n, "start")
+
+    def copies(self, n, act):
+        array, k, flip = self.jobs[n]
+        pair, _, tokens, local = array.shape
+        rows = self.buffer.shape[2]
+        start = self.p.block(k, 1 - self.p.x if flip else self.p.x) * rows
+        cols = pl.ds(pl.multiple_of(start % local, rows), rows)
+        for q in range(pair):
+            copy = pltpu.make_async_copy(
+                array.at[q, start // local, :, cols],
+                self.buffer.at[n % 2, pl.ds(q * tokens, tokens), :],
+                self.sems.at[n % 2, q],
+            )
+            getattr(copy, act)()
+
+    def times(self, right):
+        n = self.at
+        self.at += 1
+        self.copies(n, "wait")
+        product = contract_tokens(self.buffer[n % 2], right)
+        if n + 2 < len(self.jobs):
+            self.copies(n + 2, "start")
+        return product
+
+
+ORDER = (FAR, NEAR, MATE, OWN)
+
+
+def scatter_pair(left, right, collective):
+    tokens, half = right.shape
+    rows = left.shape[1] * left.shape[3] // 8
+
+    def kernel(left_ref, right_ref, out, *scratch):
+        sx, rx, sz, rz, rm, held, ss, rs, cols, cols_sem = scratch
         p = Place()
         p.enter()
-
-        def product(i, k, x):
-            cols = pl.ds(pl.multiple_of(p.block(k, x) * rows, rows), rows)
-            return contract_tokens(left[which[i]][:, cols], right[i][...])
-
-        def across(i, k):
-            return remote(sx.at[i, k], rx.at[i, k], ss.at[i, k], rs.at[i, k], p.across)
-
-        def outward(i, j):
-            return remote(sz.at[i, j], rz.at[i, j], ss.at[i, 4 + j], rs.at[i, 4 + j], p.mate)
-
-        def middle(i, j):
-            return remote(sz.at[i, j], rm.at[i, j], ss.at[i, 7 + j], rs.at[i, 7 + j], p.mid)
-
-        def relay(i, j):
-            return remote(rz.at[i, j], rm.at[i, 2 + j], ss.at[i, 9 + j], rs.at[i, 9 + j], p.mid)
-
-        def forward(i):
-            return remote(rm.at[i, 0], rz.at[i, 0], ss.at[i, 4], rs.at[i, 4], p.mate)
-
-        def back(i):
-            return remote(sz.at[i, 2], rz.at[i, 1], ss.at[i, 5], rs.at[i, 5], p.mate)
-
-        def cols_of(place):
-            return pl.ds(pl.multiple_of(place * half, half), half)
-
-        def send_across(i):
-            for k in (FAR, NEAR, MATE, OWN):
-                sx[i, k] = product(i, k, 1 - p.x).astype(BF)
-                across(i, k).start()
-
-        def send_on(i, k, j):
-            total = product(i, k, p.x)
-            across(i, k).wait_recv()
-            sz[i, j] = (total + rx[i, k].astype(F32)).astype(BF)
-
-            @pl.when(p.outer)
-            def _():
-                outward(i, j).start()
-
-            @pl.when(p.inner)
-            def _():
-                middle(i, j).start()
-
-        def send_relay(i, j):
-            @pl.when(p.inner)
-            def _():
-                outward(i, j).wait_recv()
-                relay(i, j).start()
-
-        def mate_rows(i):
-            total = product(i, MATE, p.x)
-            across(i, MATE).wait_recv()
-            total = total + rx[i, MATE].astype(F32)
-
-            @pl.when(p.outer)
-            def _():
-                sz[i, 2] = total.astype(BF)
-                outward(i, 2).start()
-
-            @pl.when(p.inner)
-            def _():
-                own[i, 0] = total
-
-        def send_forward(i):
-            @pl.when(p.inner)
-            def _():
-                middle(i, 0).wait_recv()
-                forward(i).start()
-
-        def own_rows(i):
-            total = product(i, OWN, p.x)
-            across(i, OWN).wait_recv()
-            own[i, 1] = total + rx[i, OWN].astype(F32)
-
-        def finish(i):
-            @pl.when(p.inner)
-            def _():
-                relay(i, 0).wait_recv()
-                sz[i, 2] = (own[i, 0] + rm[i, 2].astype(F32)).astype(BF)
-                back(i).start()
-                relay(i, 1).wait_recv()
-                out[i][:, cols_of(p.zl)] = own[i, 1] + rm[i, 3].astype(F32)
-                outward(i, 2).wait_recv()
-                middle(i, 1).wait_recv()
-                out[i][:, cols_of(1 - p.zl)] = rz[i, 2].astype(F32) + rm[i, 1].astype(F32)
-
-            @pl.when(p.outer)
-            def _():
-                forward(i).wait_recv()
-                out[i][:, cols_of(p.zl)] = own[i, 1] + rz[i, 0].astype(F32)
-                back(i).wait_recv()
-                out[i][:, cols_of(1 - p.zl)] = rz[i, 1].astype(F32)
-                for j in range(3):
-                    outward(i, j).wait_send()
-
-            for k in range(4):
-                across(i, k).wait_send()
-
-            @pl.when(p.inner)
-            def _():
-                for j in range(2):
-                    middle(i, j).wait_send()
-                    relay(i, j).wait_send()
-                forward(i).wait_send()
-                back(i).wait_send()
-
-        send_across(0)
-        for i in range(n):
-            if i + 1 < n:
-                send_across(i + 1)
-            send_on(i, FAR, 0)
-            send_on(i, NEAR, 1)
-            send_relay(i, 0)
-            mate_rows(i)
-            send_relay(i, 1)
-            send_forward(i)
-            own_rows(i)
-            if i > 0:
-                finish(i - 1)
-        finish(n - 1)
+        feed = Columns(
+            p, [(left_ref, k, flip) for flip in (True, False) for k in ORDER], cols, cols_sem
+        )
+        m = PairScatter(
+            p, lambda k, x: feed.times(right_ref[...]), sx, rx.at[0], sz, rz.at[0], rm.at[0],
+            held, out, ss.at[0], rs.at[0],
+        )
+        m.send_across(FAR)
+        m.send_across(NEAR)
+        m.send_across(MATE, FAR)
+        m.send_across(OWN, NEAR)
+        m.send_on(FAR, 0)
+        m.send_on(NEAR, 1)
+        m.send_relay(0)
+        m.mate_rows()
+        m.send_relay(1)
+        m.send_forward()
+        m.own_rows()
+        m.send_back()
+        m.finish()
+        m.sent_on()
+        m.sent(MATE, OWN)
 
     return pl.pallas_call(
         kernel,
-        out_shape=[jax.ShapeDtypeStruct((rows, 2 * half), F32)] * n,
-        in_specs=[VMEM] * (nx + n),
-        out_specs=[VMEM] * n,
-        scratch_shapes=[
-            pltpu.VMEM((n, 4, rows, half), BF),
-            pltpu.VMEM((n, 4, rows, half), BF),
-            pltpu.VMEM((n, 3, rows, half), BF),
-            pltpu.VMEM((n, 3, rows, half), BF),
-            pltpu.VMEM((n, 4, rows, half), BF),
-            pltpu.VMEM((n, 2, rows, half), F32),
-            pltpu.SemaphoreType.DMA((n, 11)),
-            pltpu.SemaphoreType.DMA((n, 11)),
-        ],
+        out_shape=jax.ShapeDtypeStruct((rows, 2 * half), F32),
+        in_specs=[ANY, VMEM],
+        out_specs=VMEM,
+        scratch_shapes=pair_scatter_scratch(1, rows, half)
+        + [pltpu.VMEM((2, tokens, rows), BF), pltpu.SemaphoreType.DMA((2, 2))],
         compiler_params=pltpu.CompilerParams(
-            collective_id=collective, has_side_effects=True, vmem_limit_bytes=60 << 20
+            collective_id=collective, has_side_effects=True, vmem_limit_bytes=40 << 20
         ),
-        cost_estimate=pl.CostEstimate(flops=0, bytes_accessed=n * (150 << 20), transcendentals=0),
+        cost_estimate=pl.CostEstimate(flops=0, bytes_accessed=150 << 20, transcendentals=0),
         name="scatter_pair",
-    )(*lefts, *rights)
+    )(left, right)
 
 
 def scatter_line(lefts, rights, which, collective):
@@ -785,6 +946,227 @@
     )(*lefts, *rights)
 
 
+def feed_forward_backward(out_rows, normed, hidden, silu, slope, gate, up, down, collective):
+    pair, owners, tokens, local = normed.shape
+    total, half = hidden.shape
+    rows = owners * local // 8
+    tile = total // 8
+    piece = total // 4
+
+    def kernel(*refs):
+        out_ref, normed_ref, hidden_ref, silu_ref, slope_ref, gate_ref, up_ref, down_ref = refs[:8]
+        normed_grad, down_grad, gate_grad, up_rows = refs[8:12]
+        gate_rows, weights, cols, outs, factors, to_core, sums, from_y, from_mate = refs[12:21]
+        cols_sem, outs_sem, factors_sem, weights_sem, move_ss, move_rs = refs[21:27]
+        sx, rx, sz, rz, rm, held, ss, rs = refs[27:]
+        p = Place()
+        core = (p.zh, p.zl, p.x, p.y, 1 - p.c)
+        side = (p.zh, p.zl, p.x, 1 - p.y, p.c)
+
+        down_load = pltpu.make_async_copy(down_ref, weights, weights_sem.at[0])
+        down_load.start()
+
+        def tile_loads(m, act):
+            start = m % (8 // pair) * tile
+            for j in range(owners):
+                copy = pltpu.make_async_copy(
+                    out_ref.at[m // (8 // pair), j, pl.ds(start, tile), :],
+                    outs.at[m % 2, :, pl.ds(j * local, local)],
+                    outs_sem.at[m % 2, j],
+                )
+                getattr(copy, act)()
+            for i, ref in enumerate((silu_ref, slope_ref)):
+                copy = pltpu.make_async_copy(
+                    ref.at[pl.ds(m * tile, tile), :], factors.at[m % 2, i], factors_sem.at[m % 2, i]
+                )
+                getattr(copy, act)()
+
+        D = (out_ref, normed_ref)
+        jobs = [(D[0], k, True) for k in ORDER] + [(D[0], FAR, False), (D[0], NEAR, False)]
+        jobs += [(D[1], FAR, True), (D[1], NEAR, True), (D[0], MATE, False), (D[0], OWN, False)]
+        jobs += [(D[1], MATE, True), (D[1], OWN, True)]
+        jobs += [(D[1], k, False) for k in ORDER]
+        feed = Columns(p, jobs, cols, cols_sem)
+        tile_loads(0, "start")
+        tile_loads(1, "start")
+        p.enter(core, side)
+
+        dm = PairScatter(
+            p, lambda k, x: feed.times(hidden_ref[...]), sx, rx.at[0], sz, rz.at[0],
+            rm.at[0], held, down_grad, ss.at[0], rs.at[0],
+        )
+        gm = PairScatter(
+            p, lambda k, x: feed.times(gate_rows[...]), sx, rx.at[1], sz, rz.at[1],
+            rm.at[1], held, gate_grad, ss.at[1], rs.at[1],
+        )
+
+        def rows_backward(m):
+            tile_loads(m, "wait")
+            here = pl.ds(m * tile, tile)
+            hidden_grad = dot(outs[m % 2], weights[...])
+            up_rows[here, :] = (hidden_grad * factors[m % 2, 0].astype(F32)).astype(BF)
+            gate_rows[here, :] = (hidden_grad * factors[m % 2, 1].astype(F32)).astype(BF)
+            if m + 2 < 8:
+                tile_loads(m + 2, "start")
+
+        owner = [
+            2 * (1 - p.y) + 1 - p.c, 2 * (1 - p.y) + p.c, 2 * p.y + 1 - p.c, 2 * p.y + p.c
+        ]
+
+        def weight_loads(n, act):
+            start = pl.multiple_of(owner[n] * local, local)
+            for i, ref in enumerate((gate_ref, up_ref)):
+                copy = pltpu.make_async_copy(
+                    ref.at[pl.ds(start, local), :],
+                    weights.at[pl.ds((n % 2 * 2 + i) * local, local), :],
+                    weights_sem.at[1 + n % 2 * 2 + i],
+                )
+                getattr(copy, act)()
+
+        def piece_rows(t):
+            place = p.zl if t >= 2 else 1 - p.zl
+            return pl.ds(pl.multiple_of(place * tokens + t % 2 * piece, piece), piece)
+
+        def core_copy(b, t):
+            return remote(
+                to_core.at[b, t], sums.at[b, t], move_ss.at[b, t], move_rs.at[b, t], core
+            )
+
+        def side_copy(t):
+            return remote(sums.at[0, t], from_y.at[t], move_ss.at[2, t], move_rs.at[2, t], side)
+
+        def mate_copy(t):
+            return remote(sums.at[1, t], from_mate.at[t], move_ss.at[3, t], move_rs.at[3, t], p.mate)
+
+        def partial_sum(n, t):
+            here = piece_rows(t)
+            first = n % 2 * 2 * local
+            return contract_cols(gate_rows[here, :], weights[first : first + local, :]) + contract_cols(
+                up_rows[here, :], weights[first + local : first + 2 * local, :]
+            )
+
+        def partial_block(n):
+            weight_loads(n, "wait")
+            for t in range(4):
+                value = partial_sum(n, t)
+                b = n // 2
+                if n % 2 == 0:
+                    to_core[b, t] = value.astype(BF)
+                    core_copy(b, t).start()
+                else:
+                    core_copy(b, t).wait_recv()
+                    sums[b, t] = (value + sums[b, t].astype(F32)).astype(BF)
+                    if b == 0 and t < 2:
+                        side_copy(t).start()
+            if n + 2 < 4:
+                weight_loads(n + 2, "start")
+
+        def side_next():
+            for t in range(2):
+                side_copy(t).wait_send()
+                side_copy(t + 2).start()
+
+        def to_mate(t):
+            side_copy(t).wait_recv()
+            sums[1, t] = (sums[1, t].astype(F32) + from_y[t].astype(F32)).astype(BF)
+            mate_copy(t).start()
+
+        def final(t):
+            side_copy(t).wait_recv()
+            mate_copy(t - 2).wait_recv()
+            normed_grad[pl.ds((t - 2) * piece, piece), :] = (
+                sums[1, t].astype(F32) + from_y[t].astype(F32) + from_mate[t - 2].astype(F32)
+            )
+
+        dm.send_across(FAR)
+        dm.send_across(NEAR)
+        down_load.wait()
+        for m in range(8):
+            rows_backward(m)
+        weight_loads(0, "start")
+        weight_loads(1, "start")
+        dm.send_across(MATE, FAR)
+        dm.send_across(OWN, NEAR)
+        dm.send_on(FAR, 0)
+        dm.send_on(NEAR, 1)
+        partial_block(0)
+        partial_block(1)
+        dm.send_relay(0)
+        partial_block(2)
+        dm.sent(MATE)
+        gm.send_across(FAR)
+        dm.sent(OWN)
+        gm.send_across(NEAR)
+        dm.mate_rows()
+        dm.send_relay(1)
+        dm.send_forward()
+        dm.own_rows()
+        partial_block(3)
+        side_next()
+        dm.send_back()
+        to_mate(0)
+        gm.send_across(MATE, FAR)
+        gm.send_across(OWN, NEAR)
+        to_mate(1)
+        dm.sent_on()
+        gm.send_on(FAR, 0)
+        gm.send_on(NEAR, 1)
+        gm.send_relay(0)
+        final(2)
+        final(3)
+        gm.mate_rows()
+        gm.send_relay(1)
+        gm.send_forward()
+        gm.own_rows()
+        gm.send_back()
+        dm.finish()
+        gm.finish()
+        gm.sent_on()
+        gm.sent(MATE, OWN)
+        for t in range(4):
+            core_copy(0, t).wait_send()
+            core_copy(1, t).wait_send()
+        for t in range(2):
+            side_copy(t + 2).wait_send()
+            mate_copy(t).wait_send()
+
+    grad = jax.ShapeDtypeStruct((rows, 2 * half), F32)
+    return pl.pallas_call(
+        kernel,
+        out_shape=[
+            jax.ShapeDtypeStruct((tokens, local), F32),
+            grad,
+            grad,
+            jax.ShapeDtypeStruct((total, half), BF),
+        ],
+        in_specs=[ANY, ANY, VMEM, ANY, ANY, ANY, ANY, ANY],
+        out_specs=[VMEM] * 4,
+        scratch_shapes=[
+            pltpu.VMEM((total, half), BF),
+            pltpu.VMEM((owners * local, half), BF),
+            pltpu.VMEM((2, total, rows), BF),
+            pltpu.VMEM((2, tile, owners * local), BF),
+            pltpu.VMEM((2, 2, tile, half), BF),
+            pltpu.VMEM((2, 4, piece, local), BF),
+            pltpu.VMEM((2, 4, piece, local), BF),
+            pltpu.VMEM((4, piece, local), BF),
+            pltpu.VMEM((2, piece, local), BF),
+            pltpu.SemaphoreType.DMA((2, pair)),
+            pltpu.SemaphoreType.DMA((2, owners)),
+            pltpu.SemaphoreType.DMA((2, 2)),
+            pltpu.SemaphoreType.DMA((5,)),
+            pltpu.SemaphoreType.DMA((4, 4)),
+            pltpu.SemaphoreType.DMA((4, 4)),
+        ]
+        + pair_scatter_scratch(2, rows, half),
+        compiler_params=pltpu.CompilerParams(
+            collective_id=collective, has_side_effects=True, vmem_limit_bytes=62 << 20
+        ),
+        cost_estimate=pl.CostEstimate(flops=0, bytes_accessed=300 << 20, transcendentals=0),
+        name="feed_forward_backward",
+    )(out_rows, normed, hidden, silu, slope, gate, up, down)
+
+
 SEQ = ("zh", "zl", "x")
 TP = ("y", "c")
 PAIR = ("zl", "y", "c")
@@ -795,19 +1177,23 @@
 
 
 def gather_pair_rows(rows):
-    tokens, local = rows.shape
+    blocks = lax.all_gather(rows, PAIR, axis=0)
+    return blocks.reshape(lax.axis_size("zl"), lax.axis_size(TP), *rows.shape)
+
+
+def reduce_pair_product(left, right):
     pair, parts = lax.axis_size("zl"), lax.axis_size(TP)
-    blocks = lax.all_gather(rows, PAIR, axis=0).reshape(pair, parts, tokens, local)
-    return blocks.transpose(0, 2, 1, 3).reshape(pair * tokens, parts * local)
-
-
-def reduce_pair_rows(partial_rows):
-    pair, parts = lax.axis_size("zl"), lax.axis_size(TP)
-    tokens, local = partial_rows.shape[0] // pair, partial_rows.shape[1] // parts
-    blocks = partial_rows.astype(BF).reshape(pair, tokens, parts, local).transpose(0, 2, 1, 3)
-    return lax.psum_scatter(
-        blocks.reshape(pair * parts * tokens, local), PAIR, scatter_dimension=0, tiled=True
-    ).astype(F32)
+    tokens, local = left.shape[0] // pair, right.shape[0] // parts
+    blocks = jnp.concatenate(
+        [
+            contract_cols(
+                left[q * tokens : (q + 1) * tokens], right[j * local : (j + 1) * local]
+            ).astype(BF)
+            for q in range(pair)
+            for j in range(parts)
+        ]
+    )
+    return lax.psum_scatter(blocks, PAIR, scatter_dimension=0, tiled=True).astype(F32)
 
 
 def reduce_features(partial_rows):
@@ -829,10 +1215,6 @@
     total = lax.psum(jnp.sum(values * gained, axis=1, keepdims=True), TP)
     grad_values = inverse * gained - values * inverse**3 * (total / width)
     return grad_values, jnp.sum(grad_rows * values * inverse, axis=0)
-
-
-def dot(left, right):
-    return jnp.dot(left, right, preferred_element_type=F32)
 
 
 def paired_on_device(
@@ -857,7 +1239,8 @@
     in_matrix, whole_out = gather_line(
         [after(in_weight.reshape(rows_here, 3 * local), normed_here), out_weight], 0
     )
-    out_full = gather_pair_rows(after(out_grad.astype(BF), normed_in))
+    out_full = gather_pair_rows(after(out_grad.astype(BF), normed_here))
+    in_matrix = after(in_matrix, out_full)
     projected = dot(normed_in, in_matrix)
     in_gate = projected[:, :local]
     out_gate = projected[:, local : 2 * local]
@@ -880,32 +1263,21 @@
     normed_mid = gather_pair_rows(normed_mid_here)
     (whole_up,) = gather_pair([after(up_weight, normed_mid_here)], 2)
     normed_mid = after(normed_mid, whole_up)
-    gate = dot(normed_mid, whole_gate)
-    upward = dot(normed_mid, whole_up)
-    (whole_down,) = gather_pair([after(down_weight, whole_up)], 3)
-    sigmoid_gate = jax.nn.sigmoid(gate)
-    hidden = (gate * sigmoid_gate * upward).astype(BF)
-    hidden_grad = dot(out_full, whole_down)
-    gate_rows = (
-        hidden_grad * upward * sigmoid_gate * (1.0 + gate * (1.0 - sigmoid_gate))
-    ).astype(BF)
-    up_rows = (hidden_grad * gate * sigmoid_gate).astype(BF)
-    mid_partial = (contract_cols(gate_rows, whole_gate) + contract_cols(up_rows, whole_up)).astype(BF)
-    normed_mid_grad = reduce_pair_rows(mid_partial)
-    (down_weight_grad,) = scatter_pair([out_full], [after(hidden, mid_partial)], [0], 4)
-    normed_mid_grad = after(normed_mid_grad, down_weight_grad)
+    whole_down, hidden, silu, slope = gather_down_and_hidden(
+        down_weight, normed_mid, whole_gate, whole_up, 3
+    )
+    result = middle + reduce_pair_product(hidden, whole_down)
+    normed_mid_grad, down_weight_grad, gate_weight_grad, up_rows = feed_forward_backward(
+        out_full, normed_mid, hidden, silu, slope, whole_gate, whole_up, whole_down, 4
+    )
     middle_norm_grad, gain_mid_grad = scale_backward(
         middle, norm2_gain, inverse_mid, normed_mid_grad
     )
     middle_grad = out_grad + middle_norm_grad
     branch_here = middle_grad.astype(BF)
     branch_full = lax.all_gather(branch_here, TP, axis=1, tiled=True)
-    ffn_partial = contract_cols(hidden, whole_down)
-    result = middle + reduce_pair_rows(after(ffn_partial, branch_here))
-    gate_weight_grad, up_weight_grad = scatter_pair(
-        [normed_mid], [after(gate_rows, branch_here), up_rows], [0, 0], 5
-    )
-    branch_full = after(branch_full, gate_weight_grad)
+    up_weight_grad = scatter_pair(normed_mid, after(up_rows, branch_here), 5)
+    branch_full = after(branch_full, up_weight_grad)
     gated_grad = dot(branch_full, whole_out)
     out_gate_grad = gated_grad * convolved
     conv_grad = gated_grad * out_gate

time: 993 us -> 884 us (0.89)
  local copies, waits for them, and re-layouts: 116 us -> 26.4 us
  matrix products: 118 us -> 50.3 us
  Pallas kernels: 616 us -> 669 us
    pallas_call x2 -> x3, Pallas kernels: 215 us -> 319 us  [the longest x1 169 us: feed_forward_backward(): pl.pallas_call(kernel, out_shape=[jax.ShapeDtypeStruct((tokens, local), F...]
    reshape x5 -> x0, local copies, waits for them, and re-layouts: 58.4 us -> none  [the longest x4 46.1 us: reduce_pair_rows(): partial_rows.astype(BF).reshape(pair, tokens, parts, local)]
    pallas_call x3 -> x2, Pallas kernels: 179 us -> 126 us  [gather_pair(): pl.pallas_call(kernel, out_shape=[jax.ShapeDtypeStruct((8 * rows, half),...]
    dot_general x5 -> x2, matrix products: 61.8 us -> 15.9 us  [dot(): return jnp.dot(left, right, preferred_element_type=F32)]
    dot_general x5 -> x10, matrix products: 56.7 us -> 34.4 us  [contract_cols(): lax.dot_general(left, right, (((1,), (1,)), ((), ())), preferred_element_...]
    pallas_call x1, Pallas kernels: 94.7 us -> 117 us  [gather_line(): pl.pallas_call(kernel, out_shape=[jax.ShapeDtypeStruct((8 * rows, w.shape...]
    unnamed x122 -> x70, local copies, waits for them, and re-layouts: 43.4 us -> 23.1 us
    pallas_call x1, Pallas kernels: 126 us -> 108 us  [scatter_line(): pl.pallas_call(kernel, out_shape=[jax.ShapeDtypeStruct((rows, r.shape[1])...]
  transfers between devices with their start and end apart: 11 -> 10, of which waited for: 4 -> 4; matrix products, arithmetic and copies ran while one was open for 8% -> 2% of each run, Pallas kernels for 63% -> 68%
where the time goes in v3:
time: 884 us; the launch traced here: 876 us
  Pallas kernels  669 us (76%)
  blocking collectives  61.2 us (7%)
  matrix products  50.3 us (6%)
  other arithmetic  40.9 us (5%)
  local copies, waits for them, and re-layouts  26.4 us (3%)
  between operations  14.8 us (2%)
    pallas_call x1, Pallas kernels, feed_forward_backward(): pl.pallas_call(kernel, out_shape=[jax.ShapeDtypeStruct((tokens, local), F...  169 us
    pallas_call x2, Pallas kernels, gather_pair(): pl.pallas_call(kernel, out_shape=[jax.ShapeDtypeStruct((8 * rows, half),...  126 us
    pallas_call x1, Pallas kernels, gather_line(): pl.pallas_call(kernel, out_shape=[jax.ShapeDtypeStruct((8 * rows, w.shape...  117 us
    pallas_call x1, Pallas kernels, scatter_line(): pl.pallas_call(kernel, out_shape=[jax.ShapeDtypeStruct((rows, r.shape[1])...  108 us
    pallas_call x1, Pallas kernels, gather_down_and_hidden(): pl.pallas_call(kernel, out_shape=[jax.ShapeDtypeStruct((8 * rows, half),...  76 us
    pallas_call x1, Pallas kernels, scatter_pair(): pl.pallas_call(kernel, out_shape=jax.ShapeDtypeStruct((rows, 2 * half), F...  73.8 us
    psum x1, blocking collectives, paired_on_device(): lax.psum((tap_grads, gain_in_grad, gain_mid_grad), SEQ)  35.7 us
    dot_general x10, matrix products, contract_cols(): lax.dot_general(left, right, (((1,), (1,)), ((), ())), preferred_element_...  34.4 us
  transfers between devices with their start and end apart: 10, of which 4 were waited for; matrix products, arithmetic and copies ran while one was open for 2% of the time, Pallas kernels for 68%

profile of v3, /device:TPU:0, one launch (start us, length us, event | category | flops | bytes accessed | tf_op | source)
XLA Modules:
  0.0 876.0 jit_solution(17076816442319446703)
XLA Ops:
  7.2 1.8 multiply_reduce_fusion.8
  9.1 8.5 psum.49
  17.6 2.7 convert_element_type.79
  20.3 1.2 multiply_convert_fusion.5
  21.6 0.7 all-gather.7.cloned.1.call-update
  23.0 116.6 %gather_line.1 = (bf16[2048,1536]{1,0:T(8,128)(2,1)S(1)}, bf16[2048,512]{1,0:T(8,128)(2,1)S(1)}) custom-call(bf16[256,1536]{1,0:T(8,128)(2,1)S(1)} %copy.29.refs_0_, bf16[256,512]{1,0:T(8,128)(2,1)S(1)} %copy-done.7), custom_call_target="tpu_custom_call" | custom-call | bytes 209715200 | tf_op jit(solution)/shard_map/gather_line/pallas_call | solution.py:576
  139.6 2.7 copy-done.8
  142.5 10.5 %fusion.44 = f32[1024,1536]{1,0:T(8,128)S(1)} fusion(bf16[1024,2048]{1,0:T(8,128)(2,1)} %all-gather.7.cloned.1.call-done.refs_0_, bf16[2048,1536]{1,0:T(8,128)(2,1)} %copy-done.8), kind=kOutput, calls=%fused_computation.94 | convolution fusion | flops 6442450944 | bytes 16777216 | tf_op jit(solution)/shard_map/dot_general | solution.py:198
  153.0 0.5 slice_multiply_fusion
  153.6 2.4 collective-permute-start
  156.0 1.3 collective-permute-done
  157.3 2.2 multiply_convert_fusion.4
  159.5 4.3 convolution_convert_fusion.1
  163.9 1.1 copy-done.4
  165.1 54.9 %gather_pair.2.refs_2_.refs_5_ = bf16[2048,1024]{1,0:T(8,128)(2,1)S(1)} custom-call(bf16[256,2048]{1,0:T(8,128)(2,1)S(1)} %copy-done.4), custom_call_target="tpu_custom_call" | custom-call | bytes 104857600 | tf_op jit(solution)/shard_map/gather_pair/pallas_call | solution.py:372
  220.0 1.9 copy-done
  222.0 1.6 convert_element_type.87
  223.9 1.7 multiply_reduce_fusion.7
  225.5 5.6 psum.50
  231.2 2.9 multiply_convert_fusion.3
  234.2 71.1 %gather_pair.3.refs_3_.refs_6_ = bf16[2048,1024]{1,0:T(8,128)(2,1)S(1)} custom-call(bf16[256,2048]{1,0:T(8,128)(2,1)S(1)} %copy-done.5), custom_call_target="tpu_custom_call" | custom-call | bytes 104857600 | tf_op jit(solution)/shard_map/gather_pair/pallas_call | solution.py:372
  305.4 1.9 copy-done.1
  307.3 0.3 all-gather.13.cloned.1.call-done
  307.6 76.0 %gather_down_and_hidden.1 = (bf16[2048,1024]{1,0:T(8,128)(2,1)S(1)}, bf16[2048,1024]{1,0:T(8,128)(2,1)}, bf16[2048,1024]{1,0:T(8,128)(2,1)}, bf16[2048,1024]{1,0:T(8,128)(2,1)}) custom-call(bf16[256,2048]{1,0:T(8,128)(2,1)S(1)} %copy-done.6, bf16[2,4,1024,512]{3,2,1,0:T(8,128)(2,1)} %bitcast.33, bf16[2048,1024]{1,0:T(8,128)(2,1)} %copy-done, ...), custom_call_target="tpu_custom_call" | custom-call | bytes 104857600 | tf_op jit(solution)/shard_map/gather_down_and_hidden/pallas_call | solution.py:459
  383.7 5.4 fusion.12
  389.1 2.3 fusion.11
  391.4 2.7 fusion.10
  394.0 2.3 fusion.9
  396.3 2.3 fusion.8
  398.6 2.3 fusion.7
  400.9 2.3 fusion.6
  403.2 2.3 fusion.5
  405.6 168.6 %feed_forward_backward.1 = (f32[1024,512]{1,0:T(8,128)}, f32[256,2048]{1,0:T(8,128)}, f32[256,2048]{1,0:T(8,128)}, bf16[2048,1024]{1,0:T(8,128)(2,1)}) custom-call(bf16[2,4,1024,512]{3,2,1,0:T(8,128)(2,1)} %bitcast.36, bf16[2,4,1024,512]{3,2,1,0:T(8,128)(2,1)} %bitcast.34, bf16[2048,1024]{1,0:T(8,128)(2,1)} %get-tuple-element.43.refs_2_, ...), custom_call_target="tpu_custom_call" | custom-call | bytes 314572800 | tf_op jit(solution)/shard_map/feed_forward_backward/pallas_call | solution.py:1134
  574.3 3.0 multiply_reduce_fusion
  577.2 5.8 psum.51
  583.0 4.5 fusion.41
  587.6 2.2 copy-done.2
  589.7 73.8 %scatter_pair.1 = f32[256,2048]{1,0:T(8,128)S(1)} custom-call(bf16[2,4,1024,512]{3,2,1,0:T(8,128)(2,1)} %bitcast.35, bf16[2048,1024]{1,0:T(8,128)(2,1)S(1)} %copy-done.2), custom_call_target="tpu_custom_call" | custom-call | bytes 157286400 | tf_op jit(solution)/shard_map/scatter_pair/pallas_call | solution.py:801
  663.6 5.3 fusion.45
  669.0 2.8 multiply_reduce_fusion.2
  671.9 1.3 collective-permute-start.2
  673.2 1.3 collective-permute-start.1
  674.5 3.2 collective-permute-done.2
  677.7 1.9 collective-permute-done.1
  679.6 2.9 multiply_convert_fusion.2
  682.5 2.3 multiply_convert_fusion
  684.8 1.0 copy-done.22
  685.8 8.2 convolution_convert_fusion
  694.1 0.6 pad_maximum_fusion.5
  694.7 3.0 pad_maximum_fusion.refs_3_
  697.7 108.3 %scatter_line.1 = (f32[256,512]{1,0:T(8,128)}, f32[256,1536]{1,0:T(8,128)}) custom-call(bf16[1024,2048]{1,0:T(8,128)(2,1)} %all-gather.7.cloned.1.call-done.refs_0_, bf16[1024,2048]{1,0:T(8,128)(2,1)} %all-gather.9.cloned.1.call-done.refs_1_, bf16[1024,512]{1,0:T(8,128)(2,1)} %copy-done.20, bf16[1024,1536]{1,0:T(8,128)(2,1)} %pad_maximum_fusion.refs_3_), custom_call_target="tpu_custom_call" | custom-call | bytes 335544320 | tf_op jit(solution)/shard_map/scatter_line/pallas_call | solution.py:926
  806.0 3.0 copy.30
  809.0 3.0 copy.31
  812.1 1.7 convert_element_type.100
  814.0 0.6 multiply_reduce_fusion.4
  814.6 0.7 copy-done.17
  815.3 5.6 psum.52
  820.9 4.7 subtract_add_fusion
  825.7 35.7 %all-reduce = (f32[512]{0:T(512)}, f32[3,512]{1,0:T(4,128)}, f32[512]{0:T(512)}) all-reduce(f32[512]{0:T(512)S(1)} %get-tuple-element.92, f32[3,512]{1,0:T(4,128)S(1)} %pad_maximum_fusion.4, f32[512]{0:T(512)S(1)} %get-tuple-element.90), channel_id=1, replica_groups=mesh['zh'=2,'zl'=2,'x'=2,'y'=2,'c'=2] {'zh','zl','x'}, use_global_device_ids=true, to_apply=%region_15.0 | all-reduce | flops 2560 | bytes 20480 | tf_op jit(solution)/shard_map/psum | solution.py:1315
  861.4 0.8 copy.43
  862.2 3.1 copy.44
  865.3 1.3 copy.45
  866.6 1.0 copy-done.23
  867.7 1.3 copy.46
  (91 shorter events, 1.8 us)
Async XLA Ops:
  7.2 135.3 %all-gather.11.cloned.1.call-start = ((), (), s32[]{:S(2)}) async-start(), calls=%async_computation.8 | async-start | bytes 9437184 | tf_op jit(solution)/shard_map/all_gather | solution.py:1180
  9.0 11.3 %copy-start.10 = (f32[1024,512]{1,0:T(8,128)S(1)}, f32[1024,512]{1,0:T(8,128)}, u32[]{:S(2)}) copy-start(f32[1024,512]{1,0:T(8,128)} %param.11) | copy-start | bytes 6291460
  9.0 11.2 %copy-start.26 = (f32[512]{0:T(512)S(1)}, f32[512]{0:T(512)}, u32[]{:S(2)}) copy-start(f32[512]{0:T(512)} %param.12) | copy-start | bytes 6148
  20.3 2.1 copy-start.24
  21.5 1.4 copy-start.7
  21.5 120.9 %all-gather.7.cloned.1.call-start = ((), (), s32[]{:S(2)}) async-start(), calls=%async_computation.3 | async-start | bytes 5242880 | tf_op jit(solution)/shard_map/all_gather | solution.py:1238
  22.3 199.7 %reduce-scatter.4.cloned.1.call-start = ((), (), s32[]{:S(2)}) async-start(), calls=%async_computation.4 | async-start | bytes 5242880 | tf_op jit(solution)/shard_map/reduce_scatter | solution.py:1200
  22.4 119.9 %copy-start.29 = (s32[4]{0:T(128)S(1)}, s32[4]{0:T(128)}, u32[]{:S(2)}) copy-start(s32[4]{0:T(128)} %param.20) | copy-start | bytes 52
  139.6 2.7 copy-start.8
  142.3 17.3 %copy-start.9 = (bf16[2048,512]{1,0:T(8,128)(2,1)}, bf16[2048,512]{1,0:T(8,128)(2,1)S(1)}, u32[]{:S(2)}) copy-start(bf16[2048,512]{1,0:T(8,128)(2,1)S(1)} %get-tuple-element.38) | copy-start | bytes 6291460
  153.0 4.3 copy-start.14
  153.0 3.0 copy-start.28
  153.5 6.0 copy-start.15
  153.6 3.8 collective-permute-start
  159.5 4.3 copy-start.20
  163.9 1.2 copy-start.4
  163.9 143.7 %all-gather.13.cloned.1.call-start = ((), (), s32[]{:S(2)}) async-start(), calls=%async_computation.9 | async-start | bytes 9437184 | tf_op jit(solution)/shard_map/all_gather | solution.py:1180
  220.0 1.9 copy-start
  222.0 1.9 copy-start.11
  223.9 7.3 copy-start.27
  231.2 3.0 copy-start.5
  234.1 73.5 %copy-start.6 = (bf16[256,2048]{1,0:T(8,128)(2,1)S(1)}, bf16[256,2048]{1,0:T(8,128)(2,1)}, u32[]{:S(2)}) copy-start(bf16[256,2048]{1,0:T(8,128)(2,1)} %refs_0_.3) | copy-start | bytes 3145732
  234.2 348.9 %reduce-scatter.6.cloned.1.call-start = ((), (), s32[]{:S(2)}) async-start(), calls=%async_computation.5 | async-start | bytes 9437184 | tf_op jit(solution)/shard_map/reduce_scatter | solution.py:1196
  305.4 1.9 copy-start.1
  383.7 19.5 %copy-start.3 = (bf16[2048,1024]{1,0:T(8,128)(2,1)}, bf16[2048,1024]{1,0:T(8,128)(2,1)S(1)}, u32[]{:S(2)}) copy-start(bf16[2048,1024]{1,0:T(8,128)(2,1)S(1)} %get-tuple-element.44.refs_7_) | copy-start | bytes 12582916
  383.7 5.4 copy-start.19
  405.5 258.1 %all-gather.9.cloned.1.call-start = ((), (), s32[]{:S(2)}) async-start(), calls=%async_computation.6 | async-start | bytes 5242880 | tf_op jit(solution)/shard_map/all_gather | solution.py:1278
  574.2 8.8 %copy-start.13 = (f32[1024,512]{1,0:T(8,128)S(1)}, f32[1024,512]{1,0:T(8,128)}, u32[]{:S(2)}) copy-start(f32[1024,512]{1,0:T(8,128)} %get-tuple-element.115) | copy-start | bytes 6291460
  587.5 224.6 %reduce-scatter.8.cloned.1.call-start = ((), (), s32[]{:S(2)}) async-start(), calls=%async_computation.7 | async-start | bytes 5242880 | tf_op jit(solution)/shard_map/reduce_scatter | solution.py:1200
  587.5 2.2 copy-start.2
  663.6 5.4 copy-start.16
  663.6 5.4 copy-start.18
  669.0 16.8 %slice-start = ((s8[6291456]{0:T(1024)(128)(4,1)}), s8[4194304]{0:T(1024)(128)(4,1)S(1)}, s32[]{:S(2)}) async-start(s8[6291456]{0:T(1024)(128)(4,1)} %bitcast.31), calls=%async_computation.10 | async-start | bytes 8388608
  671.9 5.8 collective-permute-start.2
  673.2 6.4 collective-permute-start.1
  679.6 6.2 slice-start.1
  682.5 2.3 copy-start.21
  684.8 1.0 copy-start.22
  812.1 1.9 copy-start.12
  814.0 1.3 copy-start.17
  820.9 40.5 %copy-start.25 = (f32[256,512]{1,0:T(8,128)S(1)}, f32[256,512]{1,0:T(8,128)}, u32[]{:S(2)}) copy-start(f32[256,512]{1,0:T(8,128)} %get-tuple-element.145) | copy-start | bytes 1572868
  865.3 2.3 copy-start.23
Sparse Core Ops, SparseCore 0:
  21.7 80.6 all-gather.10
  104.5 34.4 all-gather.6
  164.0 46.2 reduce-scatter.3
  234.3 73.3 all-gather.12
  405.7 127.2 reduce-scatter.5
  587.6 33.5 all-gather.8
  694.2 44.5 reduce-scatter.7

commit v4 on v3

--- a/solution.py
+++ b/solution.py
@@ -815,7 +815,7 @@
 
 def scatter_line(lefts, rights, which, collective):
     n, nx, ny = len(which), len(lefts), len(rights)
-    rows = lefts[0].shape[1] // 8
+    rows = lefts[-1].shape[1] // 8
     width = min(r.shape[1] for r in rights)
 
     def kernel(*refs):
@@ -826,10 +826,13 @@
 
         def product(i, k, x):
             a, b, group = which[i]
-            cols = pl.ds(pl.multiple_of(p.block(k, x) * rows, rows), rows)
-            return contract_tokens(
-                left[a][:, cols], right[b][:, group * width : (group + 1) * width]
-            )
+            start = p.block(k, x) * rows
+            if len(left[a].shape) == 2:
+                block = left[a][:, pl.ds(pl.multiple_of(start, rows), rows)]
+            else:
+                local = left[a].shape[2]
+                block = left[a][start // local, :, pl.ds(pl.multiple_of(start % local, rows), rows)]
+            return contract_tokens(block, right[b][:, group * width : (group + 1) * width])
 
         def across(i, k):
             return remote(sx.at[i, k], rx.at[i, k], ss.at[i, k], rs.at[i, k], p.across)
@@ -944,6 +947,420 @@
         cost_estimate=pl.CostEstimate(flops=0, bytes_accessed=n * (80 << 20), transcendentals=0),
         name="scatter_line",
     )(*lefts, *rights)
+
+
+class Spread:
+    def __init__(self, p, view, ss, rs):
+        self.p = p
+        self.view, self.ss, self.rs = view, ss, rs
+
+    def to_core(self):
+        block = self.view(self.p.me)
+        return remote(block, block, self.ss.at[0], self.rs.at[0], self.p.core)
+
+    def to_side(self):
+        block = self.view(self.p.me)
+        return remote(block, block, self.ss.at[1], self.rs.at[1], self.p.side)
+
+    def on_to_core(self):
+        block = self.view(self.p.side_owner)
+        return remote(block, block, self.ss.at[2], self.rs.at[2], self.p.core)
+
+    def start(self):
+        self.to_side().start()
+        self.to_core().start()
+
+    def forward(self):
+        self.to_side().wait_recv()
+        self.on_to_core().start()
+
+    def finish(self):
+        self.to_core().wait_recv()
+        self.on_to_core().wait_recv()
+        self.to_core().wait_send()
+        self.to_side().wait_send()
+        self.on_to_core().wait_send()
+
+
+def lanes_of(column):
+    return jnp.broadcast_to(column, (column.shape[0], 128)).T[:8]
+
+
+def column_of(lanes):
+    return jnp.broadcast_to(lanes[:1], (128, lanes.shape[1])).T[:, :1]
+
+
+def block_forward(
+    normed_here, stream, masks, conv_weight, gain, in_weight, out_weight, gate_weight, up_weight,
+    down_weight, collective,
+):
+    tokens, local = normed_here.shape
+    rows, width = gate_weight.shape
+    half = width // 2
+    three = in_weight.shape[1]
+    owners, pair = 4, 2
+    features = owners * local
+    tile = tokens // 4
+    plan = [("in", rows // 4)] * 4 + [("out", rows)]
+    plan += [(name, rows // 4) for name in ("gate", "up", "down") for _ in range(4)]
+    n_chunks = len(plan)
+
+    def kernel(*refs):
+        here_ref, stream_ref, masks_ref, conv_ref, gain_ref = refs[:5]
+        in_ref, out_ref, gate_ref, up_ref, down_ref = refs[5:10]
+        in_all, out_all, gate_all, up_all, down_all = refs[10:15]
+        normed_all, projected_all, convolved_all, gated_all, mid_all = refs[15:20]
+        hidden_all, silu_all, slope_all, middle, squares, halo = refs[20:26]
+        x, in_vm, out_vm, gate_vm, up_vm, projected, mixed, convolved, gated = refs[26:35]
+        to_core, sums, from_y, near_squares, mid, results, relay = refs[35:42]
+        chunk_ss, chunk_rs, x_ss, x_rs, mid_ss, mid_rs, move_ss, move_rs = refs[42:50]
+        square_ss, square_rs, halo_sem, store_sem, result_sem = refs[50:55]
+
+        p = Place()
+        p.core = (p.zh, p.zl, p.x, p.y, 1 - p.c)
+        p.side = (p.zh, p.zl, p.x, 1 - p.y, p.c)
+        diagonal = (p.zh, p.zl, p.x, 1 - p.y, 1 - p.c)
+        p.me, p.side_owner = 2 * p.y + p.c, 2 * (1 - p.y) + p.c
+        place = 2 * p.z + p.x
+        last = 2 * 4 - 1
+
+        def device_at(s):
+            return (s // 4, s // 2 % 2, s % 2, p.y, p.c)
+
+        following, previous = device_at(lax.rem(place + 1, 8)), device_at(lax.rem(place + 7, 8))
+        local_x = pltpu.make_async_copy(here_ref, x.at[p.me], store_sem.at[0])
+        local_x.start()
+        p.enter(p.core, p.side, diagonal, following, previous)
+
+        chunks = []
+        firsts = {}
+        targets = {
+            "in": (in_ref, in_vm), "out": (out_ref, out_vm), "gate": (gate_ref, gate_vm),
+            "up": (up_ref, up_vm), "down": (down_ref, down_all),
+        }
+        for c, (name, count) in enumerate(plan):
+            first = firsts.get(name, 0)
+            firsts[name] = first + count
+            source, target = targets[name]
+            if name in ("in", "out"):
+                chunk = line_gather_chunk(
+                    p, source, target, chunk_ss.at[c], chunk_rs.at[c], first, count, rows
+                )
+            else:
+                held = relay.at[("gate", "up", "down").index(name)]
+                chunk = pair_gather_chunk(
+                    p, source, target, held, chunk_ss.at[c], chunk_rs.at[c], first, count, rows
+                )
+            chunks.append(chunk)
+
+        def pump(step):
+            for stage in range(5):
+                if 0 <= step - stage < n_chunks:
+                    chunks[step - stage][stage]()
+
+        stores = []
+
+        def store(source, target):
+            copy = pltpu.make_async_copy(source, target, store_sem.at[1 + len(stores)])
+            copy.start()
+            stores.append(copy)
+
+        spread_x = Spread(p, lambda owner: x.at[owner], x_ss, x_rs)
+
+        def project(t):
+            here = pl.ds(t * tile, tile)
+            value = sum(
+                dot(x[j, here, :], in_vm[j * local : (j + 1) * local, :]) for j in range(owners)
+            )
+            projected[here, :] = value
+            mixed[pl.ds(8 + t * tile, tile), :] = value[:, :local] * value[:, 2 * local :]
+
+        def halo_copy():
+            return remote(
+                mixed.at[pl.ds(tokens, 8), :], halo, halo_sem.at[0], halo_sem.at[1], following
+            )
+
+        def send_halo():
+            @pl.when(place < last)
+            def _():
+                halo_copy().start()
+
+        def take_halo():
+            @pl.when(place > 0)
+            def _():
+                halo_copy().wait_recv()
+
+            @pl.when(place == 0)
+            def _():
+                halo[...] = jnp.zeros_like(halo)
+
+            mixed[:8, :] = halo[...]
+
+        def convolve(t):
+            here = pl.ds(t * tile, tile)
+            value = (
+                conv_ref[0:1, :] * mixed[pl.ds(8 + t * tile, tile), :]
+                + masks_ref[0, here, :] * conv_ref[1:2, :] * mixed[pl.ds(7 + t * tile, tile), :]
+                + masks_ref[1, here, :] * conv_ref[2:3, :] * mixed[pl.ds(6 + t * tile, tile), :]
+            )
+            convolved[here, :] = value
+            gated[here, :] = (projected[here, local : 2 * local] * value).astype(BF)
+
+        owner = [
+            2 * (1 - p.y) + 1 - p.c, 2 * (1 - p.y) + p.c, 2 * p.y + 1 - p.c, 2 * p.y + p.c
+        ]
+
+        def core_copy(b, t):
+            return remote(
+                to_core.at[b, t], sums.at[b, t], move_ss.at[b, t], move_rs.at[b, t], p.core
+            )
+
+        def side_copy(t):
+            return remote(sums.at[0, t], from_y.at[t], move_ss.at[2, t], move_rs.at[2, t], p.side)
+
+        def mixer_out(n):
+            out_rows = pl.ds(pl.multiple_of(owner[n] * local, local), local)
+            for t in range(4):
+                here = pl.ds(t * tile, tile)
+                value = contract_cols(gated[here, :], out_vm[out_rows, :])
+                b = n // 2
+                if n % 2 == 0:
+                    to_core[b, t] = value.astype(BF)
+                    core_copy(b, t).start()
+                else:
+                    core_copy(b, t).wait_recv()
+                    value = value + sums[b, t].astype(F32)
+                    if b == 0:
+                        sums[b, t] = value.astype(BF)
+                        side_copy(t).start()
+                    else:
+                        middle[here, :] = stream_ref[here, :] + value
+
+        def residual(t):
+            here = pl.ds(t * tile, tile)
+            side_copy(t).wait_recv()
+            value = middle[here, :] + from_y[t].astype(F32)
+            middle[here, :] = value
+            squares[:, here] = lanes_of(jnp.sum(value * value, axis=1, keepdims=True))
+
+        def square_copies():
+            return [
+                remote(
+                    squares, near_squares.at[i], square_ss.at[i], square_rs.at[i], device
+                )
+                for i, device in enumerate((p.core, p.side, diagonal))
+            ]
+
+        def sum_squares():
+            for copy in square_copies():
+                copy.wait_recv()
+                copy.wait_send()
+            squares[...] = (
+                squares[...] + near_squares[0] + near_squares[1] + near_squares[2]
+            )
+
+        def own_tile(t):
+            return lambda who: mid.at[p.zl, who, pl.ds(t * tile, tile), :]
+
+        def mate_tile(t):
+            return lambda who: mid.at[1 - p.zl, who, pl.ds(t * tile, tile), :]
+
+        spread_own = [Spread(p, own_tile(t), mid_ss.at[0, t], mid_rs.at[0, t]) for t in range(4)]
+        spread_mate = [Spread(p, mate_tile(t), mid_ss.at[1, t], mid_rs.at[1, t]) for t in range(4)]
+
+        def mate_send(t):
+            block = own_tile(t)(p.me)
+            return remote(block, block, mid_ss.at[0, t, 3], mid_rs.at[0, t, 3], p.mate)
+
+        def normalize_mid(t):
+            here = pl.ds(t * tile, tile)
+            inverse = lax.rsqrt(squares[:, here] / features + epsilon)
+            value = middle[here, :] * column_of(inverse) * gain_ref[...]
+            mid[p.zl, p.me, here, :] = value.astype(BF)
+            mate_send(t).start()
+            spread_own[t].start()
+
+        def pass_on(t):
+            spread_own[t].forward()
+            mate_send(t).wait_recv()
+            spread_mate[t].start()
+
+        def result_stores(m, act):
+            start = pl.multiple_of(tile_place(m) * tile, tile)
+            for i, ref in enumerate((hidden_all, silu_all, slope_all)):
+                copy = pltpu.make_async_copy(
+                    results.at[m % 2, i], ref.at[pl.ds(start, tile), :], result_sem.at[m % 2, i]
+                )
+                getattr(copy, act)()
+
+        def tile_place(m):
+            return (p.zl if m < 4 else 1 - p.zl) * 4 + m % 4
+
+        def hidden_units(m):
+            q = p.zl if m < 4 else 1 - p.zl
+            here = pl.ds(m % 4 * tile, tile)
+            (spread_own if m < 4 else spread_mate)[m % 4].finish()
+            if m >= 2:
+                result_stores(m - 2, "wait")
+            for part in range(2):
+                cols = pl.ds(part * half // 2, half // 2)
+                value = sum(
+                    dot(mid[q, j, here, :], gate_vm[j * local : (j + 1) * local, cols])
+                    for j in range(owners)
+                )
+                upward = sum(
+                    dot(mid[q, j, here, :], up_vm[j * local : (j + 1) * local, cols])
+                    for j in range(owners)
+                )
+                sigmoid = jax.nn.sigmoid(value)
+                silu = value * sigmoid
+                results[m % 2, 0, :, cols] = (silu * upward).astype(BF)
+                results[m % 2, 1, :, cols] = silu.astype(BF)
+                results[m % 2, 2, :, cols] = (upward * (sigmoid + silu * (1.0 - sigmoid))).astype(BF)
+            result_stores(m, "start")
+
+        pump(0)
+        local_x.wait()
+        spread_x.start()
+        pump(1)
+        pump(2)
+        spread_x.forward()
+        pump(3)
+        pump(4)
+        pump(5)
+        spread_x.finish()
+        pump(6)
+        pump(7)
+        store(x, normed_all)
+        store(in_vm, in_all)
+        project(3)
+        send_halo()
+        project(2)
+        pump(8)
+        project(1)
+        project(0)
+        store(projected, projected_all)
+        store(out_vm, out_all)
+        pump(9)
+        take_halo()
+        for t in range(4):
+            convolve(t)
+        store(convolved, convolved_all)
+        store(gated, gated_all)
+        mixer_out(0)
+        mixer_out(1)
+        pump(10)
+        mixer_out(2)
+        mixer_out(3)
+        pump(11)
+        residual(0)
+        residual(1)
+        pump(12)
+        store(gate_vm, gate_all)
+        residual(2)
+        residual(3)
+        for copy in square_copies():
+            copy.start()
+        pump(13)
+        sum_squares()
+        for t in range(4):
+            normalize_mid(t)
+        pump(14)
+        pass_on(0)
+        pass_on(1)
+        pump(15)
+        pass_on(2)
+        pass_on(3)
+        pump(16)
+        store(up_vm, up_all)
+        for t in range(4):
+            spread_mate[t].forward()
+        hidden_units(0)
+        hidden_units(1)
+        pump(17)
+        hidden_units(2)
+        hidden_units(3)
+        pump(18)
+        hidden_units(4)
+        hidden_units(5)
+        pump(19)
+        hidden_units(6)
+        hidden_units(7)
+        store(mid, mid_all)
+        pump(20)
+        result_stores(6, "wait")
+        result_stores(7, "wait")
+        for copy in stores:
+            copy.wait()
+        for t in range(4):
+            core_copy(0, t).wait_send()
+            core_copy(1, t).wait_send()
+            side_copy(t).wait_send()
+            mate_send(t).wait_send()
+
+        @pl.when(place < last)
+        def _():
+            halo_copy().wait_send()
+
+    def array(*shape, dtype=BF):
+        return jax.ShapeDtypeStruct(shape, dtype)
+
+    units = array(pair * tokens, half)
+    outs = [
+        (array(8 * rows, three), ANY), (array(8 * rows, local), ANY),
+        (array(8 * rows, half), ANY), (array(8 * rows, half), ANY), (array(8 * rows, half), ANY),
+        (array(owners, tokens, local), ANY), (array(tokens, three, dtype=F32), ANY),
+        (array(tokens, local, dtype=F32), ANY), (array(tokens, local), ANY),
+        (array(pair, owners, tokens, local), ANY),
+        (units, ANY), (units, ANY), (units, ANY),
+        (array(tokens, local, dtype=F32), VMEM), (array(8, tokens, dtype=F32), VMEM),
+        (array(8, local, dtype=F32), VMEM),
+    ]
+    return pl.pallas_call(
+        kernel,
+        out_shape=[o[0] for o in outs],
+        in_specs=[ANY, VMEM, VMEM, VMEM, VMEM] + [ANY] * 5,
+        out_specs=[o[1] for o in outs],
+        scratch_shapes=[
+            pltpu.VMEM((owners, tokens, local), BF),
+            pltpu.VMEM((8 * rows, three), BF),
+            pltpu.VMEM((8 * rows, local), BF),
+            pltpu.VMEM((8 * rows, half), BF),
+            pltpu.VMEM((8 * rows, half), BF),
+            pltpu.VMEM((tokens, three), F32),
+            pltpu.VMEM((8 + tokens, local), F32),
+            pltpu.VMEM((tokens, local), F32),
+            pltpu.VMEM((tokens, local), BF),
+            pltpu.VMEM((2, 4, tile, local), BF),
+            pltpu.VMEM((2, 4, tile, local), BF),
+            pltpu.VMEM((4, tile, local), BF),
+            pltpu.VMEM((3, 8, tokens), F32),
+            pltpu.VMEM((pair, owners, tokens, local), BF),
+            pltpu.VMEM((2, 3, tile, half), BF),
+            pltpu.VMEM((3, 3, rows, half), BF),
+            pltpu.SemaphoreType.DMA((n_chunks, 12)),
+            pltpu.SemaphoreType.DMA((n_chunks, 10)),
+            pltpu.SemaphoreType.DMA((3,)),
+            pltpu.SemaphoreType.DMA((3,)),
+            pltpu.SemaphoreType.DMA((2, 4, 4)),
+            pltpu.SemaphoreType.DMA((2, 4, 4)),
+            pltpu.SemaphoreType.DMA((3, 4)),
+            pltpu.SemaphoreType.DMA((3, 4)),
+            pltpu.SemaphoreType.DMA((3,)),
+            pltpu.SemaphoreType.DMA((3,)),
+            pltpu.SemaphoreType.DMA((2,)),
+            pltpu.SemaphoreType.DMA((12,)),
+            pltpu.SemaphoreType.DMA((2, 3)),
+        ],
+        compiler_params=pltpu.CompilerParams(
+            collective_id=collective, has_side_effects=True, vmem_limit_bytes=62 << 20
+        ),
+        cost_estimate=pl.CostEstimate(flops=0, bytes_accessed=600 << 20, transcendentals=0),
+        name="block_forward",
+    )(
+        normed_here, stream, masks, conv_weight, gain, in_weight, out_weight, gate_weight, up_weight,
+        down_weight,
+    )
 
 
 def feed_forward_backward(out_rows, normed, hidden, silu, slope, gate, up, down, collective):
@@ -1235,37 +1652,30 @@
     positions = lax.axis_index(SEQ) * tokens + jnp.arange(tokens, dtype=jnp.int32)
     mask_one, mask_two = lag_masks(doc_starts, positions)
     normed_here, inverse_in, rms_in = rms_scale(stream, norm1_gain)
-    normed_in = lax.all_gather(normed_here, TP, axis=1, tiled=True)
-    in_matrix, whole_out = gather_line(
-        [after(in_weight.reshape(rows_here, 3 * local), normed_here), out_weight], 0
+    (
+        in_matrix, whole_out, whole_gate, whole_up, whole_down, normed_in, projected, convolved, gated,
+        normed_mid, hidden, silu, slope, middle, squares, halo,
+    ) = block_forward(
+        normed_here,
+        stream,
+        jnp.stack([mask_one, mask_two]),
+        conv_weight,
+        norm2_gain[None],
+        in_weight.reshape(rows_here, 3 * local),
+        out_weight,
+        gate_weight,
+        up_weight,
+        down_weight,
+        0,
     )
     out_full = gather_pair_rows(after(out_grad.astype(BF), normed_here))
-    in_matrix = after(in_matrix, out_full)
-    projected = dot(normed_in, in_matrix)
+    mean_square = squares[0] / (local * lax.axis_size(TP)) + epsilon
+    rms_mid, inverse_mid = jnp.sqrt(mean_square), lax.rsqrt(mean_square)[:, None]
     in_gate = projected[:, :local]
     out_gate = projected[:, local : 2 * local]
     carried = projected[:, 2 * local :]
     mixed = in_gate * carried
-    previous = from_behind(mixed[-2:], SEQ, 1)
-    extended = jnp.concatenate([previous, mixed], axis=0)
-    convolved = (
-        conv_weight[0] * mixed
-        + mask_one * conv_weight[1] * extended[1:-1]
-        + mask_two * conv_weight[2] * extended[:-2]
-    )
-    gated = (out_gate * convolved).astype(BF)
-    mixer_partial = contract_cols(gated, whole_out).astype(BF)
-    mixer_out = reduce_features(mixer_partial)
-    (whole_gate,) = gather_pair([after(gate_weight, mixer_partial)], 1)
-    mixer_out = after(mixer_out, whole_gate)
-    middle = stream + mixer_out
-    normed_mid_here, inverse_mid, rms_mid = rms_scale(middle, norm2_gain)
-    normed_mid = gather_pair_rows(normed_mid_here)
-    (whole_up,) = gather_pair([after(up_weight, normed_mid_here)], 2)
-    normed_mid = after(normed_mid, whole_up)
-    whole_down, hidden, silu, slope = gather_down_and_hidden(
-        down_weight, normed_mid, whole_gate, whole_up, 3
-    )
+    extended = jnp.concatenate([halo[-2:], mixed], axis=0)
     result = middle + reduce_pair_product(hidden, whole_down)
     normed_mid_grad, down_weight_grad, gate_weight_grad, up_rows = feed_forward_backward(
         out_full, normed_mid, hidden, silu, slope, whole_gate, whole_up, whole_down, 4

time: 884 us -> 802 us (0.907)
  Pallas kernels: 669 us -> 626 us
  matrix products: 50.3 us -> 40.7 us
    pallas_call x4 -> x1, Pallas kernels: 319 us -> 276 us  [block_forward(): pl.pallas_call(kernel, out_shape=[o[0] for o in outs], in_specs=[ANY, VME...]
    unnamed x70 -> x38, local copies, waits for them, and re-layouts: 23.1 us -> 13.1 us
    dot_general x10 -> x9, matrix products: 34.4 us -> 31.4 us  [contract_cols(): lax.dot_general(left, right, (((1,), (1,)), ((), ())), preferred_element_...]
  transfers between devices with their start and end apart: 10 -> 6, of which waited for: 4 -> 2; matrix products, arithmetic and copies ran while one was open for 2% -> 5% of each run, Pallas kernels for 68% -> 79%
where the time goes in v4:
time: 802 us; the launch traced here: 796 us
  Pallas kernels  626 us (78%)
  blocking collectives  55.3 us (7%)
  matrix products  40.7 us (5%)
  other arithmetic  33.5 us (4%)
  local copies, waits for them, and re-layouts  18.1 us (2%)
  between operations  14.3 us (2%)
    pallas_call x1, Pallas kernels, block_forward(): pl.pallas_call(kernel, out_shape=[o[0] for o in outs], in_specs=[ANY, VME...  276 us
    pallas_call x1, Pallas kernels, feed_forward_backward(): pl.pallas_call(kernel, out_shape=[jax.ShapeDtypeStruct((tokens, local), F...  167 us
    pallas_call x1, Pallas kernels, scatter_line(): pl.pallas_call(kernel, out_shape=[jax.ShapeDtypeStruct((rows, r.shape[1])...  108 us
    pallas_call x1, Pallas kernels, scatter_pair(): pl.pallas_call(kernel, out_shape=jax.ShapeDtypeStruct((rows, 2 * half), F...  75 us
    psum x1, blocking collectives, paired_on_device(): lax.psum((tap_grads, gain_in_grad, gain_mid_grad), SEQ)  35.5 us
    dot_general x9, matrix products, contract_cols(): lax.dot_general(left, right, (((1,), (1,)), ((), ())), preferred_element_...  31.4 us
  transfers between devices with their start and end apart: 6, of which 2 were waited for; matrix products, arithmetic and copies ran while one was open for 5% of the time, Pallas kernels for 79%

profile of v4, /device:TPU:0, one launch (start us, length us, event | category | flops | bytes accessed | tf_op | source)
XLA Modules:
  0.0 795.5 jit_solution(6705300993131525152)
XLA Ops:
  7.2 0.0 all-gather.6.cloned.1.call-start
  7.2 2.8 convert_element_type.93
  10.1 0.2 multiply_reduce_fusion.5
  10.3 8.4 %psum.42 = f32[1024,1]{0,1:T(1,128)S(1)} all-reduce(f32[1024,1]{0,1:T(1,128)S(1)} %bitcast.38), channel_id=1, replica_groups=mesh['zh'=2,'zl'=2,'x'=2,'y'=2,'c'=2] {'y','c'}, use_global_device_ids=true, to_apply=%region_1.0 | all-reduce | flops 1024 | bytes 8192 | tf_op jit(solution)/shard_map/psum | solution.py:1624
  18.7 1.2 multiply_convert_fusion.3.refs_0_
  19.9 0.0 all-gather.6.cloned.1.call-update
  20.0 0.0 reduce-scatter.3.cloned.1.call-start
  20.0 0.3 copy.46
  20.3 1.2 copy.47.refs_5_
  21.5 0.1 convert_reduce_fusion.2
  21.6 0.3 fusion.35
  22.0 1.1 add_convert_fusion.refs_2_
  23.0 275.8 %block_forward.1 = (bf16[2048,1536]{1,0:T(8,128)(2,1)}, bf16[2048,512]{1,0:T(8,128)(2,1)}, bf16[2048,1024]{1,0:T(8,128)(2,1)}, bf16[2048,1024]{1,0:T(8,128)(2,1)...) custom-call(bf16[1024,512]{1,0:T(8,128)(2,1)} %multiply_convert_fusi, ...), custom_call_target="tpu_custom_call" | custom-call | bytes 629145600 | tf_op jit(solution)/shard_map/block_forward/pallas_call | solution.py:1319
  298.9 4.3 fusion.16
  303.1 0.3 copy-done.6
  303.4 2.3 fusion.15
  305.8 2.5 fusion.14
  308.2 2.3 fusion.13
  310.5 2.3 fusion.12
  312.7 2.3 fusion.11
  315.0 2.3 fusion.10
  317.3 2.3 fusion.9
  319.6 0.0 reduce-scatter.3.cloned.1.call-update
  319.6 0.0 all-gather.4.cloned.1.call-start
  319.7 0.8 fusion.46
  320.5 0.0 all-gather.6.cloned.1.call-done
  320.5 167.0 %feed_forward_backward.1 = (f32[1024,512]{1,0:T(8,128)}, f32[256,2048]{1,0:T(8,128)}, f32[256,2048]{1,0:T(8,128)}, bf16[2048,1024]{1,0:T(8,128)(2,1)}) custom-call(bf16[2,4,1024,512]{3,2,1,0:T(8,128)(2,1)} %bitcast.23, bf16[2,4,1024,512]{3,2,1,0:T(8,128)(2,1)} %get-tuple-element.43.refs_1_.left_ref, bf16[2048,1024]{1,0:T(8,128)(2,1)} %get-tuple-element.39.refs_2_, ...), custom_call_target="tpu_custom_call" | custom-call | bytes 314572800 | tf_op jit(solution)/shard_map/feed_forward_backward/pallas_call | solution.py:1551
  487.5 3.0 multiply_reduce_fusion
  490.5 5.8 psum.43
  496.3 0.0 reduce-scatter.3.cloned.1.call-done
  496.3 4.5 fusion.50
  500.8 0.0 all-gather.4.cloned.1.call-update
  500.8 0.0 reduce-scatter.5.cloned.1.call-start
  500.8 0.7 slice.87
  501.6 4.2 slice_multiply_fusion.1
  505.8 75.0 %scatter_pair.1 = f32[256,2048]{1,0:T(8,128)S(1)} custom-call(bf16[2,4,1024,512]{3,2,1,0:T(8,128)(2,1)} %get-tuple-element.43.refs_1_.left_ref, bf16[2048,1024]{1,0:T(8,128)(2,1)S(1)} %copy-done), custom_call_target="tpu_custom_call" | custom-call | bytes 157286400 | tf_op jit(solution)/shard_map/scatter_pair/pallas_call | solution.py:801
  580.8 0.0 all-gather.4.cloned.1.call-done.refs_1_
  580.8 9.3 %fusion.2 = (f32[512]{0:T(512)S(1)}, f32[512]{0:T(512)S(1)}, f32[512]{0:T(512)S(1)}, f32[1024,512]{1,0:T(8,128)S(1)}, f32[1024,512]{1,0:T(8,128)S(1)}, /*index=5...) fusion(f32[2,512]{1,0:T(2,128)S(1)} %slice.87, f32[1024,512]{1,0:T(8,128)} %slice_multiply_fusion.1, ...), kind=kOutput, calls=%fused_computation.6 | convolution fusion | flops 2154297856 | bytes 19941376 | tf_op jit(solution)/shard_map/dot_general | solution.py:198
  590.2 1.3 collective-permute-start.1
  591.5 1.3 collective-permute-start
  592.8 2.9 collective-permute-done.1
  595.7 1.9 collective-permute-done
  597.6 2.7 multiply_convert_fusion.2
  600.3 1.9 multiply_convert_fusion
  602.3 1.0 copy-done.7
  603.2 11.0 %convolution_convert_fusion = bf16[1024,2048]{1,0:T(8,128)(2,1)} fusion(bf16[2048,1536]{1,0:T(8,128)(2,1)} %get-tuple-element.55, bf16[1024,512]{1,0:T(8,128)(2,1)S(1)} %multiply_convert_fusion, bf16[1024,512]{1,0:T(8,128)(2,1)S(1)} %get-tuple-element.146, bf16[1024,512]{1,0:T(8,128)(2,1)S(1)} %get-tuple-element.138), kind=kOutput, calls=%fused_computation | convolution fusion | flops 6453985280 | bytes 13631488 | tf_op jit(solution)/shard_map/dot_general | solution.py:35
  614.2 0.0 reduce-scatter.5.cloned.1.call-update
  614.3 0.6 pad_maximum_fusion.5
  614.9 3.0 pad_maximum_fusion.refs_3_
  617.9 108.1 %scatter_line.1 = (f32[256,512]{1,0:T(8,128)}, f32[256,1536]{1,0:T(8,128)}) custom-call(bf16[4,1024,512]{2,1,0:T(8,128)(2,1)} %get-tuple-element.56.refs_0_, bf16[1024,2048]{1,0:T(8,128)(2,1)} %all-gather.4.cloned.1.call-done.refs_1_, bf16[1024,512]{1,0:T(8,128)(2,1)} %get-tuple-element.58.refs_2_, bf16[1024,1536]{1,0:T(8,128)(2,1)} %pad_maximum_fusion.refs_3_), custom_call_target="tpu_custom_call" | custom-call | bytes 335544320 | tf_op jit(solution)/shard_map/scatter_line/pallas_call | solution.py:929
  726.0 3.0 copy.48
  729.0 3.0 copy.49
  732.0 1.7 convert_element_type.98
  733.7 0.2 copy-done.2
  733.9 0.6 multiply_reduce_fusion.2
  734.5 0.7 copy-done.3
  735.2 5.7 psum.44
  741.0 4.7 subtract_add_fusion
  745.7 35.5 %all-reduce = (f32[512]{0:T(512)}, f32[3,512]{1,0:T(4,128)}, f32[512]{0:T(512)}) all-reduce(f32[512]{0:T(512)S(1)} %get-tuple-element.122, f32[3,512]{1,0:T(4,128)S(1)} %pad_maximum_fusion.4, f32[512]{0:T(512)S(1)} %get-tuple-element.120), channel_id=1, replica_groups=mesh['zh'=2,'zl'=2,'x'=2,'y'=2,'c'=2] {'zh','zl','x'}, use_global_device_ids=true, to_apply=%region_12.0 | all-reduce | flops 2560 | bytes 20480 | tf_op jit(solution)/shard_map/psum | solution.py:1725
  781.2 0.8 copy.61
  782.0 3.1 copy.62
  785.1 1.3 copy.63
  786.4 1.0 copy-done.8
  787.5 1.3 copy.64
  (40 shorter events, 0.2 us)
Async XLA Ops:
  7.2 2.9 copy-start.1
  7.2 11.5 %copy-start.13 = (f32[512]{0:T(512)S(1)}, f32[512]{0:T(512)}, u32[]{:S(2)}) copy-start(f32[512]{0:T(512)} %param.12) | copy-start | bytes 6148
  7.2 313.3 %all-gather.6.cloned.1.call-start = ((), (), s32[]{:S(2)}) async-start(), calls=%async_computation.5 | async-start | bytes 9437184 | tf_op jit(solution)/shard_map/all_gather | solution.py:1597
  18.7 1.3 copy-start.10
  19.9 1.5 copy-start.15
  20.0 476.3 %reduce-scatter.3.cloned.1.call-start = ((), (), s32[]{:S(2)}) async-start(), calls=%async_computation.2 | async-start | bytes 9437184 | tf_op jit(solution)/shard_map/reduce_scatter | solution.py:1613
  298.8 4.3 copy-start.5
  298.8 4.6 copy-start.6
  319.6 261.2 %all-gather.4.cloned.1.call-start = ((), (), s32[]{:S(2)}) async-start(), calls=%async_computation.3 | async-start | bytes 5242880 | tf_op jit(solution)/shard_map/all_gather | solution.py:1688
  320.5 167.0 %copy-start.14 = (f32[512]{0:T(512)S(1)}, f32[512]{0:T(512)}, u32[]{:S(2)}) copy-start(f32[512]{0:T(512)} %param.16) | copy-start | bytes 6148
  487.5 8.8 %copy-start.4 = (f32[1024,512]{1,0:T(8,128)S(1)}, f32[1024,512]{1,0:T(8,128)}, u32[]{:S(2)}) copy-start(f32[1024,512]{1,0:T(8,128)} %get-tuple-element.38) | copy-start | bytes 6291460
  500.8 231.2 %reduce-scatter.5.cloned.1.call-start = ((), (), s32[]{:S(2)}) async-start(), calls=%async_computation.4 | async-start | bytes 5242880 | tf_op jit(solution)/shard_map/reduce_scatter | solution.py:1617
  501.6 4.2 copy-start
  580.8 12.0 %copy-start.12 = (f32[3,512]{1,0:T(4,128)S(1)}, f32[3,512]{1,0:T(4,128)}, u32[]{:S(2)}) copy-start(f32[3,512]{1,0:T(4,128)} %refs_3_.1) | copy-start | bytes 18436
  590.2 12.1 %copy-start.9 = (bf16[1024,512]{1,0:T(8,128)(2,1)}, bf16[1024,512]{1,0:T(8,128)(2,1)S(1)}, u32[]{:S(2)}) copy-start(bf16[1024,512]{1,0:T(8,128)(2,1)S(1)} %get-tuple-element.146) | copy-start | bytes 3145732
  590.2 5.5 collective-permute-start.1
  591.5 6.1 collective-permute-start
  602.3 1.0 copy-start.7
  732.0 1.9 copy-start.2
  733.9 1.3 copy-start.3
  740.9 40.2 %copy-start.11 = (f32[256,512]{1,0:T(8,128)S(1)}, f32[256,512]{1,0:T(8,128)}, u32[]{:S(2)}) copy-start(f32[256,512]{1,0:T(8,128)} %get-tuple-element.174) | copy-start | bytes 1572868
  785.1 2.3 copy-start.8
Sparse Core Ops, SparseCore 0:
  20.1 67.9 all-gather.5
  319.7 128.3 reduce-scatter.2
  500.9 34.3 all-gather.3
  614.4 44.4 reduce-scatter.4

commit v5 on v4

--- a/solution.py
+++ b/solution.py
@@ -224,6 +224,12 @@
     def block(self, which, x):
         return self.rows[which] * 2 + x
 
+    def enter_all(self, devices):
+        barrier = pltpu.get_barrier_semaphore()
+        for device in devices:
+            pl.semaphore_signal(barrier, inc=1, device_id=device, device_id_type=MESH)
+        pl.semaphore_wait(barrier, len(devices))
+
     def enter(self, *others):
         barrier = pltpu.get_barrier_semaphore()
 
@@ -246,14 +252,6 @@
         @pl.when(self.outer)
         def _():
             pl.semaphore_wait(barrier, 2 + len(others))
-
-
-def in_stages(chunks):
-    stages = len(chunks[0])
-    for step in range(len(chunks) + stages - 1):
-        for stage in range(stages):
-            if 0 <= step - stage < len(chunks):
-                chunks[step - stage][stage]()
 
 
 def pair_gather_chunk(p, weight, out, relay, ss, rs, first, count, rows):
@@ -347,137 +345,6 @@
     return [begin, mate_here, near_here, far_here, finish]
 
 
-def gather_pair(weights, collective, split=4):
-    n = len(weights)
-    rows, width = weights[0].shape
-    half = width // 2
-    count = rows // split
-
-    def kernel(*refs):
-        ins, outs = refs[:n], refs[n : 2 * n]
-        relay, ss, rs = refs[2 * n :]
-        p = Place()
-        p.enter()
-        in_stages(
-            [
-                pair_gather_chunk(
-                    p, ins[i], outs[i], relay.at[i], ss.at[i * split + c], rs.at[i * split + c],
-                    c * count, count, rows,
-                )
-                for i in range(n)
-                for c in range(split)
-            ]
-        )
-
-    return pl.pallas_call(
-        kernel,
-        out_shape=[jax.ShapeDtypeStruct((8 * rows, half), BF)] * n,
-        in_specs=[ANY] * n,
-        out_specs=[ANY] * n,
-        scratch_shapes=[
-            pltpu.VMEM((n, 3, rows, half), BF),
-            pltpu.SemaphoreType.DMA((n * split, 12)),
-            pltpu.SemaphoreType.DMA((n * split, 10)),
-        ],
-        compiler_params=pltpu.CompilerParams(
-            collective_id=collective, has_side_effects=True, vmem_limit_bytes=32 << 20
-        ),
-        cost_estimate=pl.CostEstimate(flops=0, bytes_accessed=n * (100 << 20), transcendentals=0),
-        name="gather_pair",
-    )(*weights)
-
-
-def gather_down_and_hidden(weight, normed, gate, up, collective, split=4):
-    rows, width = weight.shape
-    half = width // 2
-    pair, owners, tokens, local = normed.shape
-    count = rows // split
-    tile = pair * tokens // 8
-
-    def kernel(*refs):
-        weight_ref, normed_ref, gate_ref, up_ref = refs[:4]
-        down_ref, hidden_ref, silu_ref, slope_ref = refs[4:8]
-        relay, x, results, ss, rs, x_sem, result_sem = refs[8:]
-
-        def loads(m, act):
-            start = m % (8 // pair) * tile
-            for j in range(owners):
-                copy = pltpu.make_async_copy(
-                    normed_ref.at[m // (8 // pair), j, pl.ds(start, tile), :],
-                    x.at[m % 2, :, pl.ds(j * local, local)],
-                    x_sem.at[m % 2, j],
-                )
-                getattr(copy, act)()
-
-        def stores(m, act):
-            for i, ref in enumerate((hidden_ref, silu_ref, slope_ref)):
-                copy = pltpu.make_async_copy(
-                    results.at[m % 2, i], ref.at[pl.ds(m * tile, tile), :], result_sem.at[m % 2, i]
-                )
-                getattr(copy, act)()
-
-        loads(0, "start")
-        loads(1, "start")
-        p = Place()
-        p.enter()
-        chunks = [
-            pair_gather_chunk(
-                p, weight_ref, down_ref, relay.at[0], ss.at[c], rs.at[c], c * count, count, rows
-            )
-            for c in range(split)
-        ]
-
-        def compute(m):
-            loads(m, "wait")
-            if m >= 2:
-                stores(m - 2, "wait")
-            for part in range(2):
-                here = pl.ds(part * half // 2, half // 2)
-                value = dot(x[m % 2], gate_ref[:, here])
-                upward = dot(x[m % 2], up_ref[:, here])
-                sigmoid = jax.nn.sigmoid(value)
-                silu = value * sigmoid
-                results[m % 2, 0, :, here] = (silu * upward).astype(BF)
-                results[m % 2, 1, :, here] = silu.astype(BF)
-                results[m % 2, 2, :, here] = (
-                    upward * (sigmoid + silu * (1.0 - sigmoid))
-                ).astype(BF)
-            stores(m, "start")
-            if m + 2 < 8:
-                loads(m + 2, "start")
-
-        for step in range(split + 4):
-            for stage in range(5):
-                if 0 <= step - stage < split:
-                    chunks[step - stage][stage]()
-            for m in range(step * 8 // (split + 4), (step + 1) * 8 // (split + 4)):
-                compute(m)
-        stores(6, "wait")
-        stores(7, "wait")
-
-    units = jax.ShapeDtypeStruct((pair * tokens, half), BF)
-    return pl.pallas_call(
-        kernel,
-        out_shape=[jax.ShapeDtypeStruct((8 * rows, half), BF), units, units, units],
-        in_specs=[ANY, ANY, VMEM, VMEM],
-        out_specs=[ANY] * 4,
-        scratch_shapes=[
-            pltpu.VMEM((1, 3, rows, half), BF),
-            pltpu.VMEM((2, tile, owners * local), BF),
-            pltpu.VMEM((2, 3, tile, half), BF),
-            pltpu.SemaphoreType.DMA((split, 12)),
-            pltpu.SemaphoreType.DMA((split, 10)),
-            pltpu.SemaphoreType.DMA((2, owners)),
-            pltpu.SemaphoreType.DMA((2, 3)),
-        ],
-        compiler_params=pltpu.CompilerParams(
-            collective_id=collective, has_side_effects=True, vmem_limit_bytes=48 << 20
-        ),
-        cost_estimate=pl.CostEstimate(flops=0, bytes_accessed=100 << 20, transcendentals=0),
-        name="gather_down_and_hidden",
-    )(weight, normed, gate, up)
-
-
 def line_gather_chunk(p, weight, out, ss, rs, first, count, rows):
     own = weight.at[pl.ds(first, count), :]
 
@@ -550,44 +417,6 @@
                 copy.wait_send()
 
     return [begin, mate_here, near_here, far_here, finish]
-
-
-def gather_line(weights, collective, split=2):
-    n = len(weights)
-    rows = weights[0].shape[0]
-    count = rows // split
-
-    def kernel(*refs):
-        ins, outs = refs[:n], refs[n : 2 * n]
-        ss, rs = refs[2 * n :]
-        p = Place()
-        p.enter()
-        in_stages(
-            [
-                line_gather_chunk(
-                    p, ins[i], outs[i], ss.at[i * split + c], rs.at[i * split + c],
-                    c * count, count, rows,
-                )
-                for i in range(n)
-                for c in range(split)
-            ]
-        )
-
-    return pl.pallas_call(
-        kernel,
-        out_shape=[jax.ShapeDtypeStruct((8 * rows, w.shape[1]), BF) for w in weights],
-        in_specs=[ANY] * n,
-        out_specs=[ANY] * n,
-        scratch_shapes=[
-            pltpu.SemaphoreType.DMA((n * split, 10)),
-            pltpu.SemaphoreType.DMA((n * split, 7)),
-        ],
-        compiler_params=pltpu.CompilerParams(
-            collective_id=collective, has_side_effects=True, vmem_limit_bytes=32 << 20
-        ),
-        cost_estimate=pl.CostEstimate(flops=0, bytes_accessed=n * (100 << 20), transcendentals=0),
-        name="gather_line",
-    )(*weights)
 
 
 def contract_tokens(left, right):
@@ -755,198 +584,21 @@
             getattr(copy, act)()
 
     def times(self, right):
-        n = self.at
-        self.at += 1
-        self.copies(n, "wait")
-        product = contract_tokens(self.buffer[n % 2], right)
-        if n + 2 < len(self.jobs):
+        return self.times_next(right, True, True)
+
+    def times_next(self, right, first, last):
+        if first:
+            self.at += 1
+            self.copies(self.at - 1, "wait")
+        n = self.at - 1
+        tokens = self.jobs[n][0].shape[0] * self.jobs[n][0].shape[2]
+        product = contract_tokens(self.buffer[n % 2, :tokens, :], right)
+        if last and n + 2 < len(self.jobs):
             self.copies(n + 2, "start")
         return product
 
 
 ORDER = (FAR, NEAR, MATE, OWN)
-
-
-def scatter_pair(left, right, collective):
-    tokens, half = right.shape
-    rows = left.shape[1] * left.shape[3] // 8
-
-    def kernel(left_ref, right_ref, out, *scratch):
-        sx, rx, sz, rz, rm, held, ss, rs, cols, cols_sem = scratch
-        p = Place()
-        p.enter()
-        feed = Columns(
-            p, [(left_ref, k, flip) for flip in (True, False) for k in ORDER], cols, cols_sem
-        )
-        m = PairScatter(
-            p, lambda k, x: feed.times(right_ref[...]), sx, rx.at[0], sz, rz.at[0], rm.at[0],
-            held, out, ss.at[0], rs.at[0],
-        )
-        m.send_across(FAR)
-        m.send_across(NEAR)
-        m.send_across(MATE, FAR)
-        m.send_across(OWN, NEAR)
-        m.send_on(FAR, 0)
-        m.send_on(NEAR, 1)
-        m.send_relay(0)
-        m.mate_rows()
-        m.send_relay(1)
-        m.send_forward()
-        m.own_rows()
-        m.send_back()
-        m.finish()
-        m.sent_on()
-        m.sent(MATE, OWN)
-
-    return pl.pallas_call(
-        kernel,
-        out_shape=jax.ShapeDtypeStruct((rows, 2 * half), F32),
-        in_specs=[ANY, VMEM],
-        out_specs=VMEM,
-        scratch_shapes=pair_scatter_scratch(1, rows, half)
-        + [pltpu.VMEM((2, tokens, rows), BF), pltpu.SemaphoreType.DMA((2, 2))],
-        compiler_params=pltpu.CompilerParams(
-            collective_id=collective, has_side_effects=True, vmem_limit_bytes=40 << 20
-        ),
-        cost_estimate=pl.CostEstimate(flops=0, bytes_accessed=150 << 20, transcendentals=0),
-        name="scatter_pair",
-    )(left, right)
-
-
-def scatter_line(lefts, rights, which, collective):
-    n, nx, ny = len(which), len(lefts), len(rights)
-    rows = lefts[-1].shape[1] // 8
-    width = min(r.shape[1] for r in rights)
-
-    def kernel(*refs):
-        left, right, out = refs[:nx], refs[nx : nx + ny], refs[nx + ny : nx + 2 * ny]
-        sx, rx, sz, rz, rm, own, ss, rs = refs[nx + 2 * ny :]
-        p = Place()
-        p.enter()
-
-        def product(i, k, x):
-            a, b, group = which[i]
-            start = p.block(k, x) * rows
-            if len(left[a].shape) == 2:
-                block = left[a][:, pl.ds(pl.multiple_of(start, rows), rows)]
-            else:
-                local = left[a].shape[2]
-                block = left[a][start // local, :, pl.ds(pl.multiple_of(start % local, rows), rows)]
-            return contract_tokens(block, right[b][:, group * width : (group + 1) * width])
-
-        def across(i, k):
-            return remote(sx.at[i, k], rx.at[i, k], ss.at[i, k], rs.at[i, k], p.across)
-
-        def outward(i, j):
-            return remote(sz.at[i, j], rz.at[i, j], ss.at[i, 4 + j], rs.at[i, 4 + j], p.mate)
-
-        def middle(i, j):
-            return remote(sz.at[i, j], rm.at[i, j], ss.at[i, 7 + j], rs.at[i, 7 + j], p.mid)
-
-        def back(i):
-            return remote(sz.at[i, 2], rz.at[i, 0], ss.at[i, 4], rs.at[i, 4], p.mate)
-
-        def send_across(i):
-            for k in (FAR, NEAR, MATE, OWN):
-                sx[i, k] = product(i, k, 1 - p.x).astype(BF)
-                across(i, k).start()
-
-        def summed(i, k):
-            total = product(i, k, p.x)
-            across(i, k).wait_recv()
-            return total + rx[i, k].astype(F32)
-
-        def send_on(i, k, j):
-            total = summed(i, k)
-
-            @pl.when(p.outer)
-            def _():
-                sz[i, j] = total.astype(BF)
-                outward(i, j).start()
-
-            @pl.when(p.inner)
-            def _():
-                outward(i, j).wait_recv()
-                sz[i, j] = (total + rz[i, j].astype(F32)).astype(BF)
-                middle(i, j).start()
-
-        def mate_rows(i):
-            total = summed(i, MATE)
-
-            @pl.when(p.outer)
-            def _():
-                sz[i, 2] = total.astype(BF)
-                outward(i, 2).start()
-
-            @pl.when(p.inner)
-            def _():
-                own[i, 0] = total
-
-        def own_rows(i):
-            own[i, 1] = summed(i, OWN)
-
-        def finish(i):
-            b, group = which[i][1:]
-            here = pl.ds(group * width, width)
-
-            @pl.when(p.inner)
-            def _():
-                middle(i, 0).wait_recv()
-                sz[i, 2] = (own[i, 0] + rm[i, 0].astype(F32)).astype(BF)
-                back(i).start()
-                outward(i, 2).wait_recv()
-                middle(i, 1).wait_recv()
-                out[b][:, here] = own[i, 1] + rz[i, 2].astype(F32) + rm[i, 1].astype(F32)
-
-            @pl.when(p.outer)
-            def _():
-                back(i).wait_recv()
-                out[b][:, here] = own[i, 1] + rz[i, 0].astype(F32)
-                for j in range(3):
-                    outward(i, j).wait_send()
-
-            for k in range(4):
-                across(i, k).wait_send()
-
-            @pl.when(p.inner)
-            def _():
-                for j in range(2):
-                    middle(i, j).wait_send()
-                back(i).wait_send()
-
-        send_across(0)
-        for i in range(n):
-            if i + 1 < n:
-                send_across(i + 1)
-            send_on(i, FAR, 0)
-            send_on(i, NEAR, 1)
-            mate_rows(i)
-            own_rows(i)
-            if i > 0:
-                finish(i - 1)
-        finish(n - 1)
-
-    return pl.pallas_call(
-        kernel,
-        out_shape=[jax.ShapeDtypeStruct((rows, r.shape[1]), F32) for r in rights],
-        in_specs=[VMEM] * (nx + ny),
-        out_specs=[VMEM] * ny,
-        scratch_shapes=[
-            pltpu.VMEM((n, 4, rows, width), BF),
-            pltpu.VMEM((n, 4, rows, width), BF),
-            pltpu.VMEM((n, 3, rows, width), BF),
-            pltpu.VMEM((n, 3, rows, width), BF),
-            pltpu.VMEM((n, 2, rows, width), BF),
-            pltpu.VMEM((n, 2, rows, width), F32),
-            pltpu.SemaphoreType.DMA((n, 9)),
-            pltpu.SemaphoreType.DMA((n, 9)),
-        ],
-        compiler_params=pltpu.CompilerParams(
-            collective_id=collective, has_side_effects=True, vmem_limit_bytes=60 << 20
-        ),
-        cost_estimate=pl.CostEstimate(flops=0, bytes_accessed=n * (80 << 20), transcendentals=0),
-        name="scatter_line",
-    )(*lefts, *rights)
 
 
 class Spread:
@@ -1010,9 +662,10 @@
         in_ref, out_ref, gate_ref, up_ref, down_ref = refs[5:10]
         in_all, out_all, gate_all, up_all, down_all = refs[10:15]
         normed_all, projected_all, convolved_all, gated_all, mid_all = refs[15:20]
-        hidden_all, silu_all, slope_all, middle, squares, halo = refs[20:26]
+        hidden_all, silu_all, slope_all, mixed_all, middle, squares = refs[20:26]
         x, in_vm, out_vm, gate_vm, up_vm, projected, mixed, convolved, gated = refs[26:35]
         to_core, sums, from_y, near_squares, mid, results, relay = refs[35:42]
+        halo = refs[55]
         chunk_ss, chunk_rs, x_ss, x_rs, mid_ss, mid_rs, move_ss, move_rs = refs[42:50]
         square_ss, square_rs, halo_sem, store_sem, result_sem = refs[50:55]
 
@@ -1246,6 +899,7 @@
         for t in range(4):
             convolve(t)
         store(convolved, convolved_all)
+        store(mixed, mixed_all)
         store(gated, gated_all)
         mixer_out(0)
         mixer_out(1)
@@ -1313,8 +967,8 @@
         (array(tokens, local, dtype=F32), ANY), (array(tokens, local), ANY),
         (array(pair, owners, tokens, local), ANY),
         (units, ANY), (units, ANY), (units, ANY),
+        (array(8 + tokens, local, dtype=F32), ANY),
         (array(tokens, local, dtype=F32), VMEM), (array(8, tokens, dtype=F32), VMEM),
-        (array(8, local, dtype=F32), VMEM),
     ]
     return pl.pallas_call(
         kernel,
@@ -1351,6 +1005,7 @@
             pltpu.SemaphoreType.DMA((2,)),
             pltpu.SemaphoreType.DMA((12,)),
             pltpu.SemaphoreType.DMA((2, 3)),
+            pltpu.VMEM((8, local), F32),
         ],
         compiler_params=pltpu.CompilerParams(
             collective_id=collective, has_side_effects=True, vmem_limit_bytes=62 << 20
@@ -1363,7 +1018,9 @@
     )
 
 
-def feed_forward_backward(out_rows, normed, hidden, silu, slope, gate, up, down, collective):
+def feed_forward_backward(
+    out_rows, normed, hidden, silu, slope, gate, up, down, middle, out_grad, squares, gain, collective
+):
     pair, owners, tokens, local = normed.shape
     total, half = hidden.shape
     rows = owners * local // 8
@@ -1372,57 +1029,79 @@
 
     def kernel(*refs):
         out_ref, normed_ref, hidden_ref, silu_ref, slope_ref, gate_ref, up_ref, down_ref = refs[:8]
-        normed_grad, down_grad, gate_grad, up_rows = refs[8:12]
-        gate_rows, weights, cols, outs, factors, to_core, sums, from_y, from_mate = refs[12:21]
-        cols_sem, outs_sem, factors_sem, weights_sem, move_ss, move_rs = refs[21:27]
-        sx, rx, sz, rz, rm, held, ss, rs = refs[27:]
+        middle_ref, out_grad_ref, squares_ref, gain_ref = refs[8:12]
+        middle_grad, branch_all, gain_grad, partials, down_grad_all, gate_grad_all, up_rows = refs[12:19]
+        gate_rows, weights, cols, early, to_core, sums, from_y, from_mate, lanes = refs[19:28]
+        near_lanes, residual, weight_grad, cols_sem, early_sem, weights_sem, move_ss, move_rs = refs[28:36]
+        lanes_ss, lanes_rs, branch_ss, branch_rs, tile_sem = refs[36:41]
+        sx, rx, sz, rz, rm, held, ss, rs = refs[41:]
         p = Place()
-        core = (p.zh, p.zl, p.x, p.y, 1 - p.c)
-        side = (p.zh, p.zl, p.x, 1 - p.y, p.c)
+        p.core = (p.zh, p.zl, p.x, p.y, 1 - p.c)
+        p.side = (p.zh, p.zl, p.x, 1 - p.y, p.c)
+        diagonal = (p.zh, p.zl, p.x, 1 - p.y, 1 - p.c)
+        p.me, p.side_owner = 2 * p.y + p.c, 2 * (1 - p.y) + p.c
 
         down_load = pltpu.make_async_copy(down_ref, weights, weights_sem.at[0])
         down_load.start()
 
         def tile_loads(m, act):
             start = m % (8 // pair) * tile
-            for j in range(owners):
-                copy = pltpu.make_async_copy(
+            copies = [
+                (
                     out_ref.at[m // (8 // pair), j, pl.ds(start, tile), :],
-                    outs.at[m % 2, :, pl.ds(j * local, local)],
-                    outs_sem.at[m % 2, j],
+                    early.at[m % 2, pl.ds(j * tile, tile), :],
                 )
-                getattr(copy, act)()
-            for i, ref in enumerate((silu_ref, slope_ref)):
-                copy = pltpu.make_async_copy(
-                    ref.at[pl.ds(m * tile, tile), :], factors.at[m % 2, i], factors_sem.at[m % 2, i]
+                for j in range(owners)
+            ]
+            copies += [
+                (
+                    ref.at[pl.ds(m * tile, tile), pl.ds(part * local, local)],
+                    early.at[2 + m % 2, pl.ds((2 * i + part) * tile, tile), :],
                 )
-                getattr(copy, act)()
-
+                for i, ref in enumerate((silu_ref, slope_ref))
+                for part in range(2)
+            ]
+            for i, (source, target) in enumerate(copies):
+                getattr(pltpu.make_async_copy(source, target, early_sem.at[m % 2, i]), act)()
+
+        quarter = tokens // 4
         D = (out_ref, normed_ref)
-        jobs = [(D[0], k, True) for k in ORDER] + [(D[0], FAR, False), (D[0], NEAR, False)]
-        jobs += [(D[1], FAR, True), (D[1], NEAR, True), (D[0], MATE, False), (D[0], OWN, False)]
+        jobs = [(D[0], k, True) for k in ORDER]
+        jobs += [(D[0], FAR, False), (D[0], NEAR, False), (D[0], MATE, False)]
+        jobs += [(D[1], FAR, True), (D[1], NEAR, True), (D[0], OWN, False)]
         jobs += [(D[1], MATE, True), (D[1], OWN, True)]
         jobs += [(D[1], k, False) for k in ORDER]
         feed = Columns(p, jobs, cols, cols_sem)
         tile_loads(0, "start")
         tile_loads(1, "start")
-        p.enter(core, side)
+        p.enter(p.core, p.side, diagonal)
 
         dm = PairScatter(
             p, lambda k, x: feed.times(hidden_ref[...]), sx, rx.at[0], sz, rz.at[0],
-            rm.at[0], held, down_grad, ss.at[0], rs.at[0],
+            rm.at[0], held, weight_grad, ss.at[0], rs.at[0],
         )
         gm = PairScatter(
             p, lambda k, x: feed.times(gate_rows[...]), sx, rx.at[1], sz, rz.at[1],
-            rm.at[1], held, gate_grad, ss.at[1], rs.at[1],
+            rm.at[1], held, weight_grad, ss.at[1], rs.at[1],
         )
 
         def rows_backward(m):
             tile_loads(m, "wait")
             here = pl.ds(m * tile, tile)
-            hidden_grad = dot(outs[m % 2], weights[...])
-            up_rows[here, :] = (hidden_grad * factors[m % 2, 0].astype(F32)).astype(BF)
-            gate_rows[here, :] = (hidden_grad * factors[m % 2, 1].astype(F32)).astype(BF)
+            hidden_grad = sum(
+                dot(
+                    early[m % 2, j * tile : (j + 1) * tile, :],
+                    weights[j * local : (j + 1) * local, :],
+                )
+                for j in range(owners)
+            )
+            for part in range(2):
+                units = pl.ds(part * local, local)
+                value = hidden_grad[:, part * local : (part + 1) * local]
+                for i, ref in enumerate((up_rows, gate_rows)):
+                    first = (2 * i + part) * tile
+                    factor = early[2 + m % 2, first : first + tile, :]
+                    ref[here, units] = (value * factor.astype(F32)).astype(BF)
             if m + 2 < 8:
                 tile_loads(m + 2, "start")
 
@@ -1446,11 +1125,11 @@
 
         def core_copy(b, t):
             return remote(
-                to_core.at[b, t], sums.at[b, t], move_ss.at[b, t], move_rs.at[b, t], core
+                to_core.at[t], sums.at[b, t], move_ss.at[b, t], move_rs.at[b, t], p.core
             )
 
         def side_copy(t):
-            return remote(sums.at[0, t], from_y.at[t], move_ss.at[2, t], move_rs.at[2, t], side)
+            return remote(sums.at[0, t], from_y.at[t], move_ss.at[2, t], move_rs.at[2, t], p.side)
 
         def mate_copy(t):
             return remote(sums.at[1, t], from_mate.at[t], move_ss.at[3, t], move_rs.at[3, t], p.mate)
@@ -1468,20 +1147,17 @@
                 value = partial_sum(n, t)
                 b = n // 2
                 if n % 2 == 0:
-                    to_core[b, t] = value.astype(BF)
+                    if b == 1:
+                        core_copy(0, t).wait_send()
+                    to_core[t] = value.astype(BF)
                     core_copy(b, t).start()
                 else:
                     core_copy(b, t).wait_recv()
                     sums[b, t] = (value + sums[b, t].astype(F32)).astype(BF)
-                    if b == 0 and t < 2:
+                    if b == 0:
                         side_copy(t).start()
             if n + 2 < 4:
                 weight_loads(n + 2, "start")
-
-        def side_next():
-            for t in range(2):
-                side_copy(t).wait_send()
-                side_copy(t + 2).start()
 
         def to_mate(t):
             side_copy(t).wait_recv()
@@ -1491,89 +1167,209 @@
         def final(t):
             side_copy(t).wait_recv()
             mate_copy(t - 2).wait_recv()
-            normed_grad[pl.ds((t - 2) * piece, piece), :] = (
+            middle_grad[pl.ds((t - 2) * piece, piece), :] = (
                 sums[1, t].astype(F32) + from_y[t].astype(F32) + from_mate[t - 2].astype(F32)
             )
 
-        dm.send_across(FAR)
-        dm.send_across(NEAR)
+        def lane_copies():
+            return [
+                remote(lanes, near_lanes.at[i], lanes_ss.at[i], lanes_rs.at[i], device)
+                for i, device in enumerate((p.core, p.side, diagonal))
+            ]
+
+        inverse_lanes = lax.rsqrt(squares_ref[...] / (owners * local) + epsilon)
+
+        def residual_loads(n, act):
+            here = pl.ds(n % 4 * quarter, quarter)
+            for i, ref in enumerate((middle_ref, out_grad_ref)):
+                copy = pltpu.make_async_copy(ref.at[here, :], residual.at[n % 2, i], tile_sem.at[n % 2, i])
+                getattr(copy, act)()
+
+        def row_sums():
+            total = jnp.zeros((1, local), F32)
+            for t in range(4):
+                here = pl.ds(t * quarter, quarter)
+                residual_loads(t, "wait")
+                product = middle_grad[here, :] * residual[t % 2, 0]
+                residual_loads(t + 2, "start")
+                lanes[:, here] = lanes_of(
+                    jnp.sum(product * gain_ref[...], axis=1, keepdims=True)
+                )
+                inverse = column_of(inverse_lanes[:, t * quarter : (t + 1) * quarter])
+                total = total + jnp.sum(product * inverse, axis=0, keepdims=True)
+            gain_grad[...] = total
+            for copy in lane_copies():
+                copy.start()
+
+        spreads = [
+            Spread(
+                p,
+                lambda who, t=t: early.at[who, pl.ds(t * quarter, quarter), :],
+                branch_ss.at[t],
+                branch_rs.at[t],
+            )
+            for t in range(4)
+        ]
+
+        def residual_grad():
+            for copy in lane_copies():
+                copy.wait_recv()
+            sums_all = (lanes[...] + near_lanes[0] + near_lanes[1] + near_lanes[2]) / (owners * local)
+            scale_all = inverse_lanes * inverse_lanes * inverse_lanes * sums_all
+            for t in range(4):
+                here = pl.ds(t * quarter, quarter)
+                part = slice(t * quarter, (t + 1) * quarter)
+                residual_loads(4 + t, "wait")
+                value = (
+                    residual[t % 2, 1]
+                    + column_of(inverse_lanes[:, part]) * gain_ref[...] * middle_grad[here, :]
+                    - residual[t % 2, 0] * column_of(scale_all[:, part])
+                )
+                middle_grad[here, :] = value
+                early[p.me, here, :] = value.astype(BF)
+                spreads[t].start()
+                if t + 2 < 4:
+                    residual_loads(6 + t, "start")
+
+        def out_store(m, j):
+            start = m % (8 // pair) * tile
+            return pltpu.make_async_copy(
+                to_core.at[j % 2, pl.ds(0, tile), :],
+                partials.at[m // (8 // pair), j, pl.ds(start, tile), :],
+                tile_sem.at[2, j % 2],
+            )
+
+        def out_partial(m):
+            for j in range(owners):
+                value = contract_cols(
+                    hidden_ref[pl.ds(m * tile, tile), :], weights[j * local : (j + 1) * local, :]
+                )
+                if m > 0 or j >= 2:
+                    out_store(m if j >= 2 else m - 1, (j - 2) % owners).wait()
+                to_core[j % 2, :tile, :] = value.astype(BF)
+                out_store(m, j).start()
+
+        for k in ORDER:
+            dm.send_across(k)
         down_load.wait()
-        for m in range(8):
+        for m in range(3):
             rows_backward(m)
+        dm.send_on(FAR, 0)
+        for m in range(3, 7):
+            rows_backward(m)
+        dm.send_on(NEAR, 1)
+        rows_backward(7)
         weight_loads(0, "start")
         weight_loads(1, "start")
-        dm.send_across(MATE, FAR)
-        dm.send_across(OWN, NEAR)
-        dm.send_on(FAR, 0)
-        dm.send_on(NEAR, 1)
+        dm.send_relay(0)
         partial_block(0)
         partial_block(1)
-        dm.send_relay(0)
-        partial_block(2)
-        dm.sent(MATE)
-        gm.send_across(FAR)
-        dm.sent(OWN)
-        gm.send_across(NEAR)
         dm.mate_rows()
         dm.send_relay(1)
         dm.send_forward()
+        dm.sent(FAR)
+        gm.send_across(FAR)
+        dm.sent(NEAR)
+        gm.send_across(NEAR)
+        partial_block(2)
         dm.own_rows()
+        dm.sent(MATE)
+        gm.send_across(MATE)
+        dm.sent(OWN)
+        gm.send_across(OWN)
+        dm.send_back()
         partial_block(3)
-        side_next()
-        dm.send_back()
+        down_again = pltpu.make_async_copy(down_ref, weights, weights_sem.at[0])
+        down_again.start()
         to_mate(0)
-        gm.send_across(MATE, FAR)
-        gm.send_across(OWN, NEAR)
-        to_mate(1)
         dm.sent_on()
         gm.send_on(FAR, 0)
+        down_again.wait()
+        for t in range(4):
+            core_copy(1, t).wait_send()
+        for m in range(4):
+            out_partial(m)
+        to_mate(1)
         gm.send_on(NEAR, 1)
         gm.send_relay(0)
+        for m in range(4, 8):
+            out_partial(m)
+        residual_loads(0, "start")
+        residual_loads(1, "start")
         final(2)
-        final(3)
         gm.mate_rows()
         gm.send_relay(1)
         gm.send_forward()
+        final(3)
+        row_sums()
+        dm.finish()
+        down_store = pltpu.make_async_copy(weight_grad, down_grad_all, weights_sem.at[1])
+        down_store.start()
+        residual_grad()
+        down_store.wait()
         gm.own_rows()
         gm.send_back()
-        dm.finish()
+        for t in range(4):
+            spreads[t].forward()
         gm.finish()
+        gate_store = pltpu.make_async_copy(weight_grad, gate_grad_all, weights_sem.at[1])
+        gate_store.start()
+        for t in range(4):
+            spreads[t].finish()
+        gather_done = pltpu.make_async_copy(early, branch_all, early_sem.at[0, 0])
+        gather_done.start()
         gm.sent_on()
-        gm.sent(MATE, OWN)
+        gm.sent(*ORDER)
         for t in range(4):
-            core_copy(0, t).wait_send()
-            core_copy(1, t).wait_send()
+            side_copy(t).wait_send()
         for t in range(2):
-            side_copy(t + 2).wait_send()
             mate_copy(t).wait_send()
-
-    grad = jax.ShapeDtypeStruct((rows, 2 * half), F32)
+        for copy in lane_copies():
+            copy.wait_send()
+        out_store(7, 2).wait()
+        out_store(7, 3).wait()
+        gather_done.wait()
+        gate_store.wait()
+
+    def array(*shape, dtype=F32):
+        return jax.ShapeDtypeStruct(shape, dtype)
+
     return pl.pallas_call(
         kernel,
         out_shape=[
-            jax.ShapeDtypeStruct((tokens, local), F32),
-            grad,
-            grad,
-            jax.ShapeDtypeStruct((total, half), BF),
+            array(tokens, local),
+            array(owners, tokens, local, dtype=BF),
+            array(1, local),
+            array(pair, owners, tokens, local, dtype=BF),
+            array(rows, 2 * half),
+            array(rows, 2 * half),
+            array(total, half, dtype=BF),
         ],
-        in_specs=[ANY, ANY, VMEM, ANY, ANY, ANY, ANY, ANY],
-        out_specs=[VMEM] * 4,
+        in_specs=[ANY, ANY, VMEM, ANY, ANY, ANY, ANY, ANY, ANY, ANY, VMEM, VMEM],
+        out_specs=[VMEM, ANY, VMEM, ANY, ANY, ANY, VMEM],
         scratch_shapes=[
             pltpu.VMEM((total, half), BF),
             pltpu.VMEM((owners * local, half), BF),
             pltpu.VMEM((2, total, rows), BF),
-            pltpu.VMEM((2, tile, owners * local), BF),
-            pltpu.VMEM((2, 2, tile, half), BF),
-            pltpu.VMEM((2, 4, piece, local), BF),
+            pltpu.VMEM((owners, tokens, local), BF),
+            pltpu.VMEM((4, piece, local), BF),
             pltpu.VMEM((2, 4, piece, local), BF),
             pltpu.VMEM((4, piece, local), BF),
             pltpu.VMEM((2, piece, local), BF),
+            pltpu.VMEM((8, tokens), F32),
+            pltpu.VMEM((3, 8, tokens), F32),
+            pltpu.VMEM((2, 2, tokens // 4, local), F32),
+            pltpu.VMEM((rows, 2 * half), F32),
             pltpu.SemaphoreType.DMA((2, pair)),
-            pltpu.SemaphoreType.DMA((2, owners)),
-            pltpu.SemaphoreType.DMA((2, 2)),
+            pltpu.SemaphoreType.DMA((2, 8)),
             pltpu.SemaphoreType.DMA((5,)),
             pltpu.SemaphoreType.DMA((4, 4)),
             pltpu.SemaphoreType.DMA((4, 4)),
+            pltpu.SemaphoreType.DMA((3,)),
+            pltpu.SemaphoreType.DMA((3,)),
+            pltpu.SemaphoreType.DMA((4, 3)),
+            pltpu.SemaphoreType.DMA((4, 3)),
+            pltpu.SemaphoreType.DMA((3, 2)),
         ]
         + pair_scatter_scratch(2, rows, half),
         compiler_params=pltpu.CompilerParams(
@@ -1581,7 +1377,512 @@
         ),
         cost_estimate=pl.CostEstimate(flops=0, bytes_accessed=300 << 20, transcendentals=0),
         name="feed_forward_backward",
-    )(out_rows, normed, hidden, silu, slope, gate, up, down)
+    )(
+        out_rows, normed, hidden, silu, slope, gate, up, down, middle, out_grad, squares, gain
+    )
+
+
+class LineScatter:
+    def __init__(self, p, product, sx, rx, sz, rz, rm, held, out, ss, rs):
+        self.p, self.product = p, product
+        self.sx, self.rx, self.sz, self.rz, self.rm = sx, rx, sz, rz, rm
+        self.held, self.out, self.ss, self.rs = held, out, ss, rs
+
+    def across(self, k):
+        return remote(self.sx.at[k], self.rx.at[k], self.ss.at[k], self.rs.at[k], self.p.across)
+
+    def outward(self, j):
+        return remote(self.sz.at[j], self.rz.at[j], self.ss.at[4 + j], self.rs.at[4 + j], self.p.mate)
+
+    def middle(self, j):
+        return remote(self.sz.at[j], self.rm.at[j], self.ss.at[7 + j], self.rs.at[7 + j], self.p.mid)
+
+    def back(self):
+        return remote(self.sz.at[2], self.rz.at[0], self.ss.at[4], self.rs.at[4], self.p.mate)
+
+    def send_across(self, k):
+        self.sx[k] = self.product(k, 1 - self.p.x).astype(BF)
+        self.across(k).start()
+
+    def summed(self, k):
+        total = self.product(k, self.p.x)
+        self.across(k).wait_recv()
+        return total + self.rx[k].astype(F32)
+
+    def send_on(self, k, j):
+        total = self.summed(k)
+
+        @pl.when(self.p.outer)
+        def _():
+            self.sz[j] = total.astype(BF)
+            self.outward(j).start()
+
+        @pl.when(self.p.inner)
+        def _():
+            self.outward(j).wait_recv()
+            self.sz[j] = (total + self.rz[j].astype(F32)).astype(BF)
+            self.middle(j).start()
+
+    def mate_rows(self):
+        total = self.summed(MATE)
+
+        @pl.when(self.p.outer)
+        def _():
+            self.sz[2] = total.astype(BF)
+            self.outward(2).start()
+
+        @pl.when(self.p.inner)
+        def _():
+            self.held[...] = total
+
+    def own_rows(self):
+        self.out[...] = self.summed(OWN)
+
+    def send_back(self):
+        @pl.when(self.p.inner)
+        def _():
+            self.middle(0).wait_recv()
+            self.sz[2] = (self.held[...] + self.rm[0].astype(F32)).astype(BF)
+            self.back().start()
+
+    def finish(self):
+        @pl.when(self.p.inner)
+        def _():
+            self.outward(2).wait_recv()
+            self.middle(1).wait_recv()
+            self.out[...] = self.out[...] + self.rz[2].astype(F32) + self.rm[1].astype(F32)
+            for j in range(2):
+                self.middle(j).wait_send()
+            self.back().wait_send()
+
+        @pl.when(self.p.outer)
+        def _():
+            self.back().wait_recv()
+            self.out[...] = self.out[...] + self.rz[0].astype(F32)
+            for j in range(3):
+                self.outward(j).wait_send()
+
+        for k in range(4):
+            self.across(k).wait_send()
+
+
+def mixer_backward(
+    normed_mid, up_rows, branch, whole_out, in_matrix, projected, convolved, mixed, gated, normed_in,
+    masks, conv_weight, stream, middle_grad, gain, inverse, gain_mid_grad, collective,
+):
+    pair, owners, tokens, local = normed_mid.shape
+    total, half = up_rows.shape
+    rows = owners * local // 8
+    three = in_matrix.shape[1]
+    tile = tokens // 4
+    groups = three // local
+
+    def kernel(*refs):
+        normed_mid_ref, up_rows_ref, branch_ref, out_ref, in_ref, projected_ref, convolved_ref = refs[:7]
+        mixed_ref, gated_ref, normed_in_ref, masks_ref, conv_ref, stream_ref = refs[7:13]
+        middle_ref, gain_ref, inverse_ref, gain_mid_ref = refs[13:17]
+        stream_grad, small_sums, up_grad, out_grad, in_grad = refs[17:22]
+        conv_grad, rows_grad, stage, stage_mixed, weights, to_core, sums, from_y, lanes, near_lanes = refs[22:32]
+        smalls, cols, stage_sem, in_sem, move_ss, move_rs, lanes_ss, lanes_rs = refs[32:40]
+        small_ss, small_rs, halo_sem, cols_sem = refs[40:44]
+        branch_sem = refs[59]
+        sx, rx, sz, rz, rm, held, ss, rs = refs[44:52]
+        lx, lrx, lz, lrz, lrm, lss, lrs = refs[52:59]
+        lheld = held.at[:, pl.ds(0, local)]
+
+        p = Place()
+        p.core = (p.zh, p.zl, p.x, p.y, 1 - p.c)
+        p.side = (p.zh, p.zl, p.x, 1 - p.y, p.c)
+        diagonal = (p.zh, p.zl, p.x, 1 - p.y, 1 - p.c)
+        place = 2 * p.z + p.x
+        last = 7
+
+        def device_at(s):
+            return (s // 4, s // 2 % 2, s % 2, p.y, p.c)
+
+        others = [lax.rem(place + d, 8) for d in range(1, 8)]
+
+        jobs = []
+        for t in range(4):
+            jobs.append(((projected_ref, 1), (convolved_ref, 0), t))
+        for t in range(4):
+            jobs.append(((projected_ref, 0), (projected_ref, 2), t))
+        for _ in range(2):
+            for t in range(4):
+                jobs.append(((stream_ref, 0), (middle_ref, 0), t))
+        taken = []
+
+        def stage_copies(n, act):
+            for i, (ref, group) in enumerate(jobs[n][:2]):
+                copy = pltpu.make_async_copy(
+                    ref.at[pl.ds(jobs[n][2] * tile, tile), pl.ds(group * local, local)],
+                    stage.at[n % 2, i],
+                    stage_sem.at[n % 2, i],
+                )
+                getattr(copy, act)()
+
+        def mixed_load(t):
+            return pltpu.make_async_copy(
+                mixed_ref.at[pl.ds(t * tile, tile + 8), :], stage_mixed.at[t % 2], stage_sem.at[t % 2, 2]
+            )
+
+        def branch_slot(t, j):
+            return to_core.at[j] if t % 2 == 0 else lz.at[j // 3, j % 3]
+
+        def branch_loads(t, act):
+            for j in range(owners):
+                copy = pltpu.make_async_copy(
+                    branch_ref.at[0, j, pl.ds(t * tile, tile), :], branch_slot(t, j), branch_sem.at[t % 2, j]
+                )
+                getattr(copy, act)()
+
+        def staged():
+            n = len(taken)
+            taken.append(n)
+            stage_copies(n, "wait")
+            values = stage[n % 2, 0], stage[n % 2, 1]
+            return values
+
+        def staged_done():
+            n = len(taken) - 1
+            if n + 2 < len(jobs):
+                stage_copies(n + 2, "start")
+
+        def out_loads(act):
+            for j in range(owners):
+                copy = pltpu.make_async_copy(
+                    out_ref.at[pl.ds(j * local, local), :], weights.at[j], in_sem.at[j]
+                )
+                getattr(copy, act)()
+
+        out_loads("start")
+        stage_copies(0, "start")
+        stage_copies(1, "start")
+        branch_loads(0, "start")
+        branch_loads(1, "start")
+        mixed_load(0).start()
+        mixed_load(1).start()
+        feed_jobs = [(normed_mid_ref, k, True) for k in ORDER]
+        feed_jobs += [(normed_mid_ref, FAR, False)]
+        feed_jobs += [(branch_ref, k, True) for k in ORDER]
+        feed_jobs += [(normed_mid_ref, NEAR, False)]
+        feed_jobs += [(normed_in_ref, FAR, True), (normed_in_ref, NEAR, True)]
+        feed_jobs += [(normed_mid_ref, MATE, False)]
+        feed_jobs += [(normed_in_ref, MATE, True), (normed_in_ref, OWN, True)]
+        feed_jobs += [(normed_mid_ref, OWN, False)]
+        feed_jobs += [(branch_ref, k, False) for k in ORDER]
+        feed_jobs += [(normed_in_ref, k, False) for k in ORDER]
+        feed = Columns(p, feed_jobs, cols, cols_sem)
+        owner = [
+            2 * (1 - p.y) + 1 - p.c, 2 * (1 - p.y) + p.c, 2 * p.y + 1 - p.c, 2 * p.y + p.c
+        ]
+        p.enter_all([device_at(s) for s in others] + [p.core, p.side, diagonal])
+
+        um = PairScatter(
+            p, lambda k, x: feed.times(up_rows_ref[...]), sx, rx.at[0], sz, rz.at[0], rm.at[0], held,
+            up_grad, ss.at[0], rs.at[0],
+        )
+
+        om = LineScatter(
+            p, lambda k, x: feed.times(gated_ref[...]), lx.at[0], lrx.at[0], lz.at[0], lrz.at[0], lrm.at[0], lheld,
+            out_grad, lss.at[0], lrs.at[0],
+        )
+        ims = [
+            LineScatter(
+                p, lambda k, x, g=g: feed.times_next(rows_grad[g], g == 0, g == groups - 1),
+                lx.at[1 + g], lrx.at[1 + g], lz.at[1 + g], lrz.at[1 + g], lrm.at[1 + g],
+                lheld, in_grad.at[:, pl.ds(g * local, local)], lss.at[1 + g], lrs.at[1 + g],
+            )
+            for g in range(groups)
+        ]
+
+        def halo_copy():
+            return remote(
+                conv_grad.at[pl.ds(0, 8), :],
+                conv_grad.at[pl.ds(tokens, 8), :],
+                halo_sem.at[0],
+                halo_sem.at[1],
+                device_at(others[6]),
+            )
+
+        taps = [jnp.zeros((1, local), F32) for _ in range(3)]
+
+        def gated_backward(t):
+            here = pl.ds(t * tile, tile)
+            branch_loads(t, "wait")
+            gated_grad = sum(
+                dot(branch_slot(t, j)[...], weights[j])
+                for j in range(owners)
+            )
+            if t + 2 < 4:
+                branch_loads(t + 2, "start")
+            out_gate, conv = staged()
+            mixed_load(t).wait()
+            near = stage_mixed.at[t % 2]
+            rows_grad[1, here, :] = (gated_grad * conv).astype(BF)
+            value = gated_grad * out_gate
+            conv_grad[here, :] = value
+            staged_done()
+            taps[0] += jnp.sum(value * near[pl.ds(8, tile), :], axis=0, keepdims=True)
+            taps[1] += jnp.sum(
+                masks_ref[here, 0:1] * value * near[pl.ds(7, tile), :],
+                axis=0, keepdims=True,
+            )
+            taps[2] += jnp.sum(
+                masks_ref[here, 1:2] * value * near[pl.ds(6, tile), :],
+                axis=0, keepdims=True,
+            )
+            if t + 2 < 4:
+                mixed_load(t + 2).start()
+
+        def send_halo():
+            @pl.when(place > 0)
+            def _():
+                halo_copy().start()
+
+        def take_halo():
+            @pl.when(place < last)
+            def _():
+                halo_copy().wait_recv()
+
+            @pl.when(place == last)
+            def _():
+                conv_grad[tokens:, :] = jnp.zeros((8, local), F32)
+
+        def conv_backward(t):
+            here = pl.ds(t * tile, tile)
+            in_gate, carried = staged()
+            value = (
+                conv_ref[0:1, :] * conv_grad[here, :]
+                + masks_ref[here, 2:3] * conv_ref[1:2, :] * conv_grad[pl.ds(1 + t * tile, tile), :]
+                + masks_ref[here, 3:4] * conv_ref[2:3, :] * conv_grad[pl.ds(2 + t * tile, tile), :]
+            )
+            rows_grad[0, here, :] = (value * carried).astype(BF)
+            rows_grad[2, here, :] = (value * in_gate).astype(BF)
+            staged_done()
+
+        def in_loads(n, act):
+            start = pl.multiple_of(owner[n] * local, local)
+            for g in range(groups):
+                copy = pltpu.make_async_copy(
+                    in_ref.at[pl.ds(start, local), pl.ds(g * local, local)], weights.at[g], in_sem.at[g]
+                )
+                getattr(copy, act)()
+
+        def core_copy(b, t):
+            return remote(to_core.at[t], sums.at[b, t], move_ss.at[b, t], move_rs.at[b, t], p.core)
+
+        def side_copy(t):
+            return remote(sums.at[0, t], from_y.at[t], move_ss.at[2, t], move_rs.at[2, t], p.side)
+
+        def partial_block(n):
+            in_loads(n, "wait")
+            b = n // 2
+            for t in range(4):
+                here = pl.ds(t * tile, tile)
+                value = sum(
+                    contract_cols(rows_grad[g, here, :], weights[g])
+                    for g in range(groups)
+                )
+                if n % 2 == 0:
+                    if b == 1:
+                        core_copy(0, t).wait_send()
+                    to_core[t] = value.astype(BF)
+                    core_copy(b, t).start()
+                else:
+                    core_copy(b, t).wait_recv()
+                    value = value + sums[b, t].astype(F32)
+                    if b == 0:
+                        sums[b, t] = value.astype(BF)
+                        side_copy(t).start()
+                    else:
+                        stream_grad[here, :] = value
+            if n + 1 < 4:
+                in_loads(n + 1, "start")
+
+        def lane_copies():
+            return [
+                remote(lanes, near_lanes.at[i], lanes_ss.at[i], lanes_rs.at[i], device)
+                for i, device in enumerate((p.core, p.side, diagonal))
+            ]
+
+        def small_copies():
+            return [
+                remote(
+                    smalls.at[place], smalls.at[place], small_ss.at[d], small_rs.at[place], device_at(s)
+                )
+                for d, s in enumerate(others)
+            ]
+
+        def row_sums():
+            total_gain = jnp.zeros((1, local), F32)
+            for t in range(4):
+                here = pl.ds(t * tile, tile)
+                side_copy(t).wait_recv()
+                value = stream_grad[here, :] + from_y[t].astype(F32)
+                stream_grad[here, :] = value
+                values = staged()[0]
+                staged_done()
+                product = value * values
+                lanes[:, here] = lanes_of(jnp.sum(product * gain_ref[...], axis=1, keepdims=True))
+                inverse_here = column_of(inverse_ref[:, here])
+                total_gain = total_gain + jnp.sum(product * inverse_here, axis=0, keepdims=True)
+            for copy in lane_copies():
+                copy.start()
+            smalls[place] = jnp.concatenate(
+                taps + [total_gain, gain_mid_ref[...], jnp.zeros((3, local), F32)], axis=0
+            )
+            for copy in small_copies():
+                copy.start()
+
+        def input_grad():
+            for copy in lane_copies():
+                copy.wait_recv()
+            sums_all = (lanes[...] + near_lanes[0] + near_lanes[1] + near_lanes[2]) / (owners * local)
+            scale_all = inverse_ref[...] * inverse_ref[...] * inverse_ref[...] * sums_all
+            for t in range(4):
+                here = pl.ds(t * tile, tile)
+                values, residual = staged()
+                stream_grad[here, :] = (
+                    residual
+                    + column_of(inverse_ref[:, here]) * gain_ref[...] * stream_grad[here, :]
+                    - values * column_of(scale_all[:, t * tile : (t + 1) * tile])
+                )
+                staged_done()
+
+        def sum_smalls():
+            for s in others:
+                block = smalls.at[s]
+                remote(block, block, small_ss.at[0], small_rs.at[s], p.mate).wait_recv()
+            value = smalls[0]
+            for s in range(1, 8):
+                value = value + smalls[s]
+            small_sums[...] = value
+
+        for k in ORDER:
+            um.send_across(k)
+        out_loads("wait")
+        for t in range(4):
+            gated_backward(t)
+            if t == 0:
+                send_halo()
+        in_loads(0, "start")
+        um.send_on(FAR, 0)
+        take_halo()
+        for t in range(4):
+            conv_backward(t)
+        for k in ORDER:
+            om.send_across(k)
+        um.send_on(NEAR, 1)
+        um.send_relay(0)
+        partial_block(0)
+        partial_block(1)
+        for k in (FAR, NEAR):
+            for m in ims:
+                m.send_across(k)
+        um.mate_rows()
+        um.send_relay(1)
+        um.send_forward()
+        partial_block(2)
+        partial_block(3)
+        for k in (MATE, OWN):
+            for m in ims:
+                m.send_across(k)
+        um.own_rows()
+        um.send_back()
+        row_sums()
+        om.send_on(FAR, 0)
+        om.send_on(NEAR, 1)
+        input_grad()
+        um.finish()
+        om.mate_rows()
+        om.own_rows()
+        om.send_back()
+        for m in ims:
+            m.send_on(FAR, 0)
+        sum_smalls()
+        for m in ims:
+            m.send_on(NEAR, 1)
+        om.finish()
+        for m in ims:
+            m.mate_rows()
+            m.send_back()
+        for m in ims:
+            m.own_rows()
+        for m in ims:
+            m.finish()
+        um.sent_on()
+        um.sent(*ORDER)
+        for t in range(4):
+            core_copy(1, t).wait_send()
+            side_copy(t).wait_send()
+        for copy in lane_copies() + small_copies():
+            copy.wait_send()
+
+        @pl.when(place > 0)
+        def _():
+            halo_copy().wait_send()
+
+    def array(*shape):
+        return jax.ShapeDtypeStruct(shape, F32)
+
+    n = 1 + groups
+    return pl.pallas_call(
+        kernel,
+        out_shape=[
+            array(tokens, local),
+            array(8, local),
+            array(rows, 2 * half),
+            array(rows, local),
+            array(rows, three),
+        ],
+        in_specs=[ANY, VMEM, ANY, ANY, ANY, ANY, ANY, ANY, VMEM, ANY, VMEM, VMEM, ANY, ANY]
+        + [VMEM] * 3,
+        out_specs=[VMEM] * 5,
+        scratch_shapes=[
+            pltpu.VMEM((tokens + 8, local), F32),
+            pltpu.VMEM((groups, tokens, local), BF),
+            pltpu.VMEM((2, 2, tile, local), F32),
+            pltpu.VMEM((2, tile + 8, local), F32),
+            pltpu.VMEM((owners, local, local), BF),
+            pltpu.VMEM((4, tile, local), BF),
+            pltpu.VMEM((2, 4, tile, local), BF),
+            pltpu.VMEM((4, tile, local), BF),
+            pltpu.VMEM((8, tokens), F32),
+            pltpu.VMEM((3, 8, tokens), F32),
+            pltpu.VMEM((8, 8, local), F32),
+            pltpu.VMEM((2, total, rows), BF),
+            pltpu.SemaphoreType.DMA((2, 3)),
+            pltpu.SemaphoreType.DMA((owners,)),
+            pltpu.SemaphoreType.DMA((3, 4)),
+            pltpu.SemaphoreType.DMA((3, 4)),
+            pltpu.SemaphoreType.DMA((3,)),
+            pltpu.SemaphoreType.DMA((3,)),
+            pltpu.SemaphoreType.DMA((7,)),
+            pltpu.SemaphoreType.DMA((8,)),
+            pltpu.SemaphoreType.DMA((2,)),
+            pltpu.SemaphoreType.DMA((2, pair)),
+        ]
+        + pair_scatter_scratch(1, rows, half)
+        + [
+            pltpu.VMEM((n, 4, rows, local), BF),
+            pltpu.VMEM((n, 4, rows, local), BF),
+            pltpu.VMEM((n, 3, rows, local), BF),
+            pltpu.VMEM((n, 3, rows, local), BF),
+            pltpu.VMEM((n, 2, rows, local), BF),
+            pltpu.SemaphoreType.DMA((n, 9)),
+            pltpu.SemaphoreType.DMA((n, 9)),
+            pltpu.SemaphoreType.DMA((2, owners)),
+        ],
+        compiler_params=pltpu.CompilerParams(
+            collective_id=collective, has_side_effects=True, vmem_limit_bytes=62 << 20
+        ),
+        cost_estimate=pl.CostEstimate(flops=0, bytes_accessed=300 << 20, transcendentals=0),
+        name="mixer_backward",
+    )(
+        normed_mid, up_rows, branch[None], whole_out, in_matrix, projected, convolved, mixed, gated,
+        normed_in[None], masks, conv_weight, stream, middle_grad, gain, inverse, gain_mid_grad,
+    )
 
 
 SEQ = ("zh", "zl", "x")
@@ -1596,27 +1897,6 @@
 def gather_pair_rows(rows):
     blocks = lax.all_gather(rows, PAIR, axis=0)
     return blocks.reshape(lax.axis_size("zl"), lax.axis_size(TP), *rows.shape)
-
-
-def reduce_pair_product(left, right):
-    pair, parts = lax.axis_size("zl"), lax.axis_size(TP)
-    tokens, local = left.shape[0] // pair, right.shape[0] // parts
-    blocks = jnp.concatenate(
-        [
-            contract_cols(
-                left[q * tokens : (q + 1) * tokens], right[j * local : (j + 1) * local]
-            ).astype(BF)
-            for q in range(pair)
-            for j in range(parts)
-        ]
-    )
-    return lax.psum_scatter(blocks, PAIR, scatter_dimension=0, tiled=True).astype(F32)
-
-
-def reduce_features(partial_rows):
-    return lax.psum_scatter(
-        partial_rows.astype(BF), TP, scatter_dimension=1, tiled=True
-    ).astype(F32)
 
 
 def rms_scale(values, gain):
@@ -1624,14 +1904,6 @@
     squares = lax.psum(jnp.sum(values * values, axis=1, keepdims=True), TP)
     inverse = lax.rsqrt(squares / width + epsilon)
     return (values * inverse * gain).astype(BF), inverse, jnp.sqrt(squares[:, 0] / width + epsilon)
-
-
-def scale_backward(values, gain, inverse, grad_rows):
-    width = gain.shape[0] * lax.axis_size(TP)
-    gained = gain * grad_rows
-    total = lax.psum(jnp.sum(values * gained, axis=1, keepdims=True), TP)
-    grad_values = inverse * gained - values * inverse**3 * (total / width)
-    return grad_values, jnp.sum(grad_rows * values * inverse, axis=0)
 
 
 def paired_on_device(
@@ -1654,7 +1926,7 @@
     normed_here, inverse_in, rms_in = rms_scale(stream, norm1_gain)
     (
         in_matrix, whole_out, whole_gate, whole_up, whole_down, normed_in, projected, convolved, gated,
-        normed_mid, hidden, silu, slope, middle, squares, halo,
+        normed_mid, hidden, silu, slope, mixed, middle, squares,
     ) = block_forward(
         normed_here,
         stream,
@@ -1671,60 +1943,32 @@
     out_full = gather_pair_rows(after(out_grad.astype(BF), normed_here))
     mean_square = squares[0] / (local * lax.axis_size(TP)) + epsilon
     rms_mid, inverse_mid = jnp.sqrt(mean_square), lax.rsqrt(mean_square)[:, None]
-    in_gate = projected[:, :local]
-    out_gate = projected[:, local : 2 * local]
-    carried = projected[:, 2 * local :]
-    mixed = in_gate * carried
-    extended = jnp.concatenate([halo[-2:], mixed], axis=0)
-    result = middle + reduce_pair_product(hidden, whole_down)
-    normed_mid_grad, down_weight_grad, gate_weight_grad, up_rows = feed_forward_backward(
-        out_full, normed_mid, hidden, silu, slope, whole_gate, whole_up, whole_down, 4
-    )
-    middle_norm_grad, gain_mid_grad = scale_backward(
-        middle, norm2_gain, inverse_mid, normed_mid_grad
-    )
-    middle_grad = out_grad + middle_norm_grad
-    branch_here = middle_grad.astype(BF)
-    branch_full = lax.all_gather(branch_here, TP, axis=1, tiled=True)
-    up_weight_grad = scatter_pair(normed_mid, after(up_rows, branch_here), 5)
-    branch_full = after(branch_full, up_weight_grad)
-    gated_grad = dot(branch_full, whole_out)
-    out_gate_grad = gated_grad * convolved
-    conv_grad = gated_grad * out_gate
-    lag_one = mask_one * conv_grad
-    lag_two = mask_two * conv_grad
-    next_one, next_two = from_behind((lag_one[:2], lag_two[:2]), SEQ, -1)
-    after_one = jnp.concatenate([lag_one, next_one], axis=0)
-    after_two = jnp.concatenate([lag_two, next_two], axis=0)
-    mixed_grad = (
-        conv_weight[0] * conv_grad
-        + conv_weight[1] * after_one[1 : tokens + 1]
-        + conv_weight[2] * after_two[2:]
-    )
-    tap_grads = jnp.stack(
+    middle_grad, branch_blocks, gain_mid_grad, ffn_partial, down_weight_grad, gate_weight_grad, up_rows = (
+        feed_forward_backward(
+            out_full, normed_mid, hidden, silu, slope, whole_gate, whole_up, whole_down, middle, out_grad,
+            squares, norm2_gain[None], 4,
+        )
+    )
+    result = middle + lax.psum_scatter(
+        ffn_partial.reshape(-1, local), PAIR, scatter_dimension=0, tiled=True
+    ).astype(F32)
+    next_one, next_two = lag_masks(doc_starts, positions + 1)[0], lag_masks(doc_starts, positions + 2)[1]
+    count = tokens * lax.axis_size(SEQ)
+    masks = jnp.concatenate(
         [
-            jnp.sum(conv_grad * mixed, axis=0),
-            jnp.sum(lag_one * extended[1:-1], axis=0),
-            jnp.sum(lag_two * extended[:-2], axis=0),
-        ]
-    )
-    projected_grad = jnp.concatenate(
-        [mixed_grad * carried, out_gate_grad, mixed_grad * in_gate], axis=1
-    ).astype(BF)
-    in_partial = contract_cols(projected_grad, in_matrix).astype(BF)
-    normed_in_grad = reduce_features(in_partial)
-    out_weight_grad, in_weight_grad = scatter_line(
-        [normed_in, branch_full],
-        [after(gated, in_partial), projected_grad],
-        [(1, 0, 0), (0, 1, 0), (0, 1, 1), (0, 1, 2)],
-        6,
-    )
-    normed_in_grad = after(normed_in_grad, in_weight_grad)
-    stream_norm_grad, gain_in_grad = scale_backward(stream, norm1_gain, inverse_in, normed_in_grad)
-    stream_grad = middle_grad + stream_norm_grad
-    conv_total, gain_in_total, gain_mid_total = lax.psum(
-        (tap_grads, gain_in_grad, gain_mid_grad), SEQ
-    )
+            mask_one,
+            mask_two,
+            jnp.where(positions[:, None] + 1 < count, next_one, 0.0),
+            jnp.where(positions[:, None] + 2 < count, next_two, 0.0),
+        ],
+        axis=1,
+    )
+    stream_grad, small_sums, up_weight_grad, out_weight_grad, in_weight_grad = mixer_backward(
+        normed_mid, up_rows, branch_blocks, whole_out, in_matrix, projected, convolved, mixed, gated,
+        normed_in, masks, conv_weight, stream, middle_grad, norm1_gain[None],
+        jnp.broadcast_to(inverse_in.reshape(1, tokens), (8, tokens)), gain_mid_grad, 5,
+    )
+    conv_total, gain_in_total, gain_mid_total = small_sums[:3], small_sums[3], small_sums[4]
     return (
         result,
         stream_grad,

time: 802 us -> 677 us (0.84)
  blocking collectives: 55.3 us -> 8.51 us
  matrix products: 40.7 us -> 0 us
  other arithmetic: 33.5 us -> 11.8 us
  Pallas kernels: 626 us -> 616 us
    psum x3 -> x0, blocking collectives: 46.9 us -> none  [the longest x1 35.5 us: paired_on_device(): lax.psum((tap_grads, gain_in_grad, gain_mid_grad), SEQ)]
    dot_general x10 -> x0, matrix products: 40.7 us -> none  [the longest x9 31.4 us: contract_cols(): lax.dot_general(left, right, (((1,), (1,)), ((), ())), preferred_element_...]
    pallas_call x3 -> x2, Pallas kernels: 350 us -> 341 us  [the longest x1 197 us: mixer_backward(): pl.pallas_call(kernel, out_shape=[array(tokens, local), array(8, local),...]
  transfers between devices with their start and end apart: 6 -> 2, of which waited for: 2 -> 0; matrix products, arithmetic and copies ran while one was open for 5% -> 2% of each run, Pallas kernels for 79% -> 70%
where the time goes in v5:
time: 677 us; the launch traced here: 670 us
  Pallas kernels  616 us (91%)
  local copies, waits for them, and re-layouts  19.2 us (3%)
  between operations  14.4 us (2%)
  other arithmetic  11.8 us (2%)
  blocking collectives  8.51 us (1%)
    pallas_call x1, Pallas kernels, block_forward(): pl.pallas_call(kernel, out_shape=[o[0] for o in outs], in_specs=[ANY, VME...  275 us
    pallas_call x1, Pallas kernels, mixer_backward(): pl.pallas_call(kernel, out_shape=[array(tokens, local), array(8, local),...  197 us
    pallas_call x1, Pallas kernels, feed_forward_backward(): pl.pallas_call(kernel, out_shape=[array(tokens, local), array(owners, tok...  144 us
  transfers between devices with their start and end apart: 2, of which 0 were waited for; matrix products, arithmetic and copies ran while one was open for 2% of the time, Pallas kernels for 70%

profile of v5, /device:TPU:0, one launch (start us, length us, event | category | flops | bytes accessed | tf_op | source)
XLA Modules:
  0.0 670.1 jit_solution(11772272298611777438)
XLA Ops:
  7.2 0.0 all-gather.3.cloned.1.call-start
  7.2 1.8 multiply_reduce_fusion
  9.0 0.0 copy-start
  9.0 0.0 copy-start.9
  9.1 8.5 %psum.7 = f32[1024,1]{0,1:T(1,128)S(1)} all-reduce(f32[1024,1]{0,1:T(1,128)S(1)} %bitcast.22), channel_id=1, replica_groups=mesh['zh'=2,'zl'=2,'x'=2,'y'=2,'c'=2] {'y','c'}, use_global_device_ids=true, to_apply=%region_1.0 | all-reduce | flops 1024 | bytes 8192 | tf_op jit(solution)/shard_map/psum | solution.py:1904
  17.6 2.7 convert_element_type.84
  20.3 0.0 copy-done
  20.3 0.0 copy-done.9
  20.3 0.0 copy-start.6
  20.3 1.2 multiply_convert_fusion.refs_0_
  21.5 0.0 copy-start.10
  21.5 0.0 all-gather.3.cloned.1.call-update
  21.5 0.0 reduce-scatter.2.cloned.1.call-start
  21.6 0.0 copy-done.6
  21.6 0.3 copy.52
  21.9 1.2 copy.53.refs_5_
  23.1 0.0 copy-done.10
  23.1 0.1 convert_reduce_fusion.1
  23.2 0.3 fusion.2
  23.6 1.1 add_convert_fusion.refs_2_
  24.6 275.4 %block_forward.1 = (bf16[2048,1536]{1,0:T(8,128)(2,1)}, bf16[2048,512]{1,0:T(8,128)(2,1)}, bf16[2048,1024]{1,0:T(8,128)(2,1)}, bf16[2048,1024]{1,0:T(8,128)(2,1)...) custom-call(bf16[1024,512]{1,0:T(8,128)(2,1)} %multiply_convert_fusi, ...), custom_call_target="tpu_custom_call" | custom-call | bytes 629145600 | tf_op jit(solution)/shard_map/block_forward/pallas_call | solution.py:973
  300.0 0.0 all-gather.3.cloned.1.call-done
  300.1 143.8 %feed_forward_backward.1 = (f32[1024,512]{1,0:T(8,128)}, bf16[4,1024,512]{2,1,0:T(8,128)(2,1)}, f32[1,512]{1,0:T(1,128)}, bf16[2,4,1024,512]{3,2,1,0:T(8,128)(2,...) custom-call(bf16[2,4,1024,512]{3,2,1,0:T(8,128)(2,1)} %bitcast.14, ...), custom_call_target="tpu_custom_call" | custom-call | bytes 314572800 | tf_op jit(solution)/shard_map/feed_forward_backward/pallas_call | solution.py:1337
  443.9 0.0 reduce-scatter.2.cloned.1.call-update
  444.0 1.0 copy.54.refs_10_
  445.1 0.8 add_sqrt_fusion
  445.8 0.6 pad_maximum_fusion.1
  446.4 0.6 broadcast_in_dim.22.refs_15_
  447.1 196.8 %mixer_backward.1 = (f32[1024,512]{1,0:T(8,128)}, f32[8,512]{1,0:T(8,128)}, f32[256,2048]{1,0:T(8,128)}, f32[256,512]{1,0:T(8,128)}, f32[256,1536]{1,0:T(8,128)}) custom-call(bf16[2,4,1024,512]{3,2,1,0:T(8,128)(2,1)} %get-tuple-element.42.refs_1_.refs_0_, bf16[2048,1024]{1,0:T(8,128)(2,1)} %get-tuple-element.51.refs_1_, bf16[1,4,1024,512]{3,2,1,0:T(8,128)(2,1)} %bitcast.18, ...), custom_call_target="tpu_custom_call" | custom-call | bytes 314572800 | tf_op jit(solution)/shard_map/mixer_backward/pallas_call | solution.py:1830
  643.9 3.0 copy.55
  646.9 0.0 copy-start.8
  646.9 0.0 copy-start.1
  646.9 3.2 copy.56
  650.1 0.0 copy-done.8
  650.1 0.6 slice.13
  650.7 0.6 fusion.9
  651.2 0.0 reduce-scatter.2.cloned.1.call-done
  651.2 0.0 copy-done.1
  651.3 0.0 copy-start.5
  651.3 3.0 convert_add_fusion
  654.3 0.0 copy-done.5
  654.3 0.0 copy-start.7
  654.3 0.0 copy-start.3
  654.3 1.3 copy.62
  655.6 0.1 copy-done.7
  655.6 0.8 copy.63
  656.4 0.5 copy-done.3
  657.0 0.0 copy-start.4
  657.0 1.3 copy.64
  658.3 1.0 copy-done.4
  659.3 0.0 copy-start.2
  659.3 1.3 copy.65
  660.7 1.0 copy-done.2
  661.7 1.3 copy.66
  (10 shorter events, 0.1 us)
Async XLA Ops:
  7.2 292.9 %all-gather.3.cloned.1.call-start = ((), (), s32[]{:S(2)}) async-start(), calls=%async_computation.2 | async-start | bytes 9437184 | tf_op jit(solution)/shard_map/all_gather | solution.py:1898
  9.0 11.3 %copy-start = (f32[1024,512]{1,0:T(8,128)S(1)}, f32[1024,512]{1,0:T(8,128)}, u32[]{:S(2)}) copy-start(f32[1024,512]{1,0:T(8,128)} %refs_12_.1) | copy-start | bytes 6291460
  9.0 11.2 %copy-start.9 = (f32[512]{0:T(512)S(1)}, f32[512]{0:T(512)}, u32[]{:S(2)}) copy-start(f32[512]{0:T(512)} %param.12) | copy-start | bytes 6148
  20.3 1.3 copy-start.6
  21.5 1.6 copy-start.10
  21.5 629.7 %reduce-scatter.2.cloned.1.call-start = ((), (), s32[]{:S(2)}) async-start(), calls=%async_computation.1 | async-start | bytes 9437184 | tf_op jit(solution)/shard_map/reduce_scatter | solution.py:1952
  646.9 3.2 copy-start.8
  646.9 4.4 copy-start.1
  651.3 3.0 copy-start.5
  654.3 1.4 copy-start.7
  654.3 2.7 copy-start.3
  657.0 2.3 copy-start.4
  659.3 2.3 copy-start.2
Sparse Core Ops, SparseCore 0:
  21.7 67.9 all-gather.2
  444.1 104.2 reduce-scatter.1

commit v6 on v5

--- a/solution.py
+++ b/solution.py
@@ -533,17 +533,14 @@
                 self.relay(j).wait_send()
             self.forward().wait_send()
 
-    def sent_on(self):
+    def sent_on(self, j):
         @pl.when(self.p.outer)
         def _():
-            for j in range(3):
-                self.outward(j).wait_send()
+            self.outward(j).wait_send()
 
         @pl.when(self.p.inner)
         def _():
-            for j in range(2):
-                self.middle(j).wait_send()
-            self.back().wait_send()
+            (self.back() if j == 2 else self.middle(j)).wait_send()
 
     def sent(self, *which):
         for k in which:
@@ -643,10 +640,10 @@
 
 
 def block_forward(
-    normed_here, stream, masks, conv_weight, gain, in_weight, out_weight, gate_weight, up_weight,
+    stream, masks, conv_weight, first_gain, gain, in_weight, out_weight, gate_weight, up_weight,
     down_weight, collective,
 ):
-    tokens, local = normed_here.shape
+    tokens, local = stream.shape
     rows, width = gate_weight.shape
     half = width // 2
     three = in_weight.shape[1]
@@ -658,14 +655,15 @@
     n_chunks = len(plan)
 
     def kernel(*refs):
-        here_ref, stream_ref, masks_ref, conv_ref, gain_ref = refs[:5]
+        stream_ref, masks_ref, conv_ref, first_gain_ref, gain_ref = refs[:5]
         in_ref, out_ref, gate_ref, up_ref, down_ref = refs[5:10]
         in_all, out_all, gate_all, up_all, down_all = refs[10:15]
         normed_all, projected_all, convolved_all, gated_all, mid_all = refs[15:20]
         hidden_all, silu_all, slope_all, mixed_all, middle, squares = refs[20:26]
+        first_squares, refs = refs[26], refs[:26] + refs[27:]
         x, in_vm, out_vm, gate_vm, up_vm, projected, mixed, convolved, gated = refs[26:35]
         to_core, sums, from_y, near_squares, mid, results, relay = refs[35:42]
-        halo = refs[55]
+        halo, first_near, first_ss, first_rs = refs[55:]
         chunk_ss, chunk_rs, x_ss, x_rs, mid_ss, mid_rs, move_ss, move_rs = refs[42:50]
         square_ss, square_rs, halo_sem, store_sem, result_sem = refs[50:55]
 
@@ -681,8 +679,6 @@
             return (s // 4, s // 2 % 2, s % 2, p.y, p.c)
 
         following, previous = device_at(lax.rem(place + 1, 8)), device_at(lax.rem(place + 7, 8))
-        local_x = pltpu.make_async_copy(here_ref, x.at[p.me], store_sem.at[0])
-        local_x.start()
         p.enter(p.core, p.side, diagonal, following, previous)
 
         chunks = []
@@ -707,7 +703,10 @@
             chunks.append(chunk)
 
         def pump(step):
-            for stage in range(5):
+            for c in range(3) if step == 0 else [step + 2]:
+                if c < n_chunks:
+                    chunks[c][0]()
+            for stage in range(1, 5):
                 if 0 <= step - stage < n_chunks:
                     chunks[step - stage][stage]()
 
@@ -796,21 +795,36 @@
             middle[here, :] = value
             squares[:, here] = lanes_of(jnp.sum(value * value, axis=1, keepdims=True))
 
-        def square_copies():
+        def square_copies(mine, near, send_sems, recv_sems):
             return [
-                remote(
-                    squares, near_squares.at[i], square_ss.at[i], square_rs.at[i], device
-                )
+                remote(mine, near.at[i], send_sems.at[i], recv_sems.at[i], device)
                 for i, device in enumerate((p.core, p.side, diagonal))
             ]
 
-        def sum_squares():
-            for copy in square_copies():
+        def sum_squares(mine, near, *sems):
+            for copy in square_copies(mine, near, *sems):
                 copy.wait_recv()
                 copy.wait_send()
-            squares[...] = (
-                squares[...] + near_squares[0] + near_squares[1] + near_squares[2]
-            )
+            mine[...] = mine[...] + near[0] + near[1] + near[2]
+
+        first = (first_squares, first_near, first_ss, first_rs)
+        second = (squares, near_squares, square_ss, square_rs)
+
+        def first_sums():
+            for t in range(4):
+                here = pl.ds(t * tile, tile)
+                value = stream_ref[here, :]
+                first_squares[:, here] = lanes_of(jnp.sum(value * value, axis=1, keepdims=True))
+            for copy in square_copies(*first):
+                copy.start()
+
+        def first_norm():
+            sum_squares(*first)
+            for t in range(4):
+                here = pl.ds(t * tile, tile)
+                inverse = lax.rsqrt(first_squares[:, here] / features + epsilon)
+                value = stream_ref[here, :] * column_of(inverse) * first_gain_ref[...]
+                x[p.me, here, :] = value.astype(BF)
 
         def own_tile(t):
             return lambda who: mid.at[p.zl, who, pl.ds(t * tile, tile), :]
@@ -873,7 +887,8 @@
             result_stores(m, "start")
 
         pump(0)
-        local_x.wait()
+        first_sums()
+        first_norm()
         spread_x.start()
         pump(1)
         pump(2)
@@ -913,10 +928,10 @@
         store(gate_vm, gate_all)
         residual(2)
         residual(3)
-        for copy in square_copies():
+        for copy in square_copies(*second):
             copy.start()
         pump(13)
-        sum_squares()
+        sum_squares(*second)
         for t in range(4):
             normalize_mid(t)
         pump(14)
@@ -927,14 +942,14 @@
         pass_on(3)
         pump(16)
         store(up_vm, up_all)
-        for t in range(4):
-            spread_mate[t].forward()
         hidden_units(0)
         hidden_units(1)
         pump(17)
         hidden_units(2)
+        for t in range(4):
+            spread_mate[t].forward()
+        pump(18)
         hidden_units(3)
-        pump(18)
         hidden_units(4)
         hidden_units(5)
         pump(19)
@@ -969,11 +984,12 @@
         (units, ANY), (units, ANY), (units, ANY),
         (array(8 + tokens, local, dtype=F32), ANY),
         (array(tokens, local, dtype=F32), VMEM), (array(8, tokens, dtype=F32), VMEM),
+        (array(8, tokens, dtype=F32), VMEM),
     ]
     return pl.pallas_call(
         kernel,
         out_shape=[o[0] for o in outs],
-        in_specs=[ANY, VMEM, VMEM, VMEM, VMEM] + [ANY] * 5,
+        in_specs=[VMEM] * 5 + [ANY] * 5,
         out_specs=[o[1] for o in outs],
         scratch_shapes=[
             pltpu.VMEM((owners, tokens, local), BF),
@@ -1006,6 +1022,9 @@
             pltpu.SemaphoreType.DMA((12,)),
             pltpu.SemaphoreType.DMA((2, 3)),
             pltpu.VMEM((8, local), F32),
+            pltpu.VMEM((3, 8, tokens), F32),
+            pltpu.SemaphoreType.DMA((3,)),
+            pltpu.SemaphoreType.DMA((3,)),
         ],
         compiler_params=pltpu.CompilerParams(
             collective_id=collective, has_side_effects=True, vmem_limit_bytes=62 << 20
@@ -1013,7 +1032,7 @@
         cost_estimate=pl.CostEstimate(flops=0, bytes_accessed=600 << 20, transcendentals=0),
         name="block_forward",
     )(
-        normed_here, stream, masks, conv_weight, gain, in_weight, out_weight, gate_weight, up_weight,
+        stream, masks, conv_weight, first_gain, gain, in_weight, out_weight, gate_weight, up_weight,
         down_weight,
     )
 
@@ -1272,40 +1291,40 @@
         dm.sent(NEAR)
         gm.send_across(NEAR)
         partial_block(2)
+        partial_block(3)
+        down_again = pltpu.make_async_copy(down_ref, weights, weights_sem.at[0])
+        down_again.start()
+        to_mate(0)
         dm.own_rows()
         dm.sent(MATE)
         gm.send_across(MATE)
         dm.sent(OWN)
         gm.send_across(OWN)
+        to_mate(1)
         dm.send_back()
-        partial_block(3)
-        down_again = pltpu.make_async_copy(down_ref, weights, weights_sem.at[0])
-        down_again.start()
-        to_mate(0)
-        dm.sent_on()
+        dm.sent_on(0)
         gm.send_on(FAR, 0)
+        dm.sent_on(1)
+        gm.send_on(NEAR, 1)
+        residual_loads(0, "start")
+        residual_loads(1, "start")
         down_again.wait()
         for t in range(4):
             core_copy(1, t).wait_send()
-        for m in range(4):
+        for m in range(8):
             out_partial(m)
-        to_mate(1)
-        gm.send_on(NEAR, 1)
-        gm.send_relay(0)
-        for m in range(4, 8):
-            out_partial(m)
-        residual_loads(0, "start")
-        residual_loads(1, "start")
+        dm.sent_on(2)
+        gm.mate_rows()
         final(2)
-        gm.mate_rows()
-        gm.send_relay(1)
-        gm.send_forward()
         final(3)
         row_sums()
+        gm.send_relay(0)
+        residual_grad()
         dm.finish()
         down_store = pltpu.make_async_copy(weight_grad, down_grad_all, weights_sem.at[1])
         down_store.start()
-        residual_grad()
+        gm.send_relay(1)
+        gm.send_forward()
         down_store.wait()
         gm.own_rows()
         gm.send_back()
@@ -1318,7 +1337,8 @@
             spreads[t].finish()
         gather_done = pltpu.make_async_copy(early, branch_all, early_sem.at[0, 0])
         gather_done.start()
-        gm.sent_on()
+        for j in range(3):
+            gm.sent_on(j)
         gm.sent(*ORDER)
         for t in range(4):
             side_copy(t).wait_send()
@@ -1790,28 +1810,29 @@
                 m.send_across(k)
         um.own_rows()
         um.send_back()
-        row_sums()
         om.send_on(FAR, 0)
         om.send_on(NEAR, 1)
-        input_grad()
-        um.finish()
         om.mate_rows()
         om.own_rows()
         om.send_back()
+        um.finish()
         for m in ims:
             m.send_on(FAR, 0)
-        sum_smalls()
+        row_sums()
         for m in ims:
             m.send_on(NEAR, 1)
+        input_grad()
         om.finish()
         for m in ims:
             m.mate_rows()
             m.send_back()
+        sum_smalls()
         for m in ims:
             m.own_rows()
         for m in ims:
             m.finish()
-        um.sent_on()
+        for j in range(3):
+            um.sent_on(j)
         um.sent(*ORDER)
         for t in range(4):
             core_copy(1, t).wait_send()
@@ -1899,13 +1920,6 @@
     return blocks.reshape(lax.axis_size("zl"), lax.axis_size(TP), *rows.shape)
 
 
-def rms_scale(values, gain):
-    width = gain.shape[0] * lax.axis_size(TP)
-    squares = lax.psum(jnp.sum(values * values, axis=1, keepdims=True), TP)
-    inverse = lax.rsqrt(squares / width + epsilon)
-    return (values * inverse * gain).astype(BF), inverse, jnp.sqrt(squares[:, 0] / width + epsilon)
-
-
 def paired_on_device(
     stream,
     norm1_gain,
@@ -1923,15 +1937,14 @@
     rows_here = in_weight.shape[0]
     positions = lax.axis_index(SEQ) * tokens + jnp.arange(tokens, dtype=jnp.int32)
     mask_one, mask_two = lag_masks(doc_starts, positions)
-    normed_here, inverse_in, rms_in = rms_scale(stream, norm1_gain)
     (
         in_matrix, whole_out, whole_gate, whole_up, whole_down, normed_in, projected, convolved, gated,
-        normed_mid, hidden, silu, slope, mixed, middle, squares,
+        normed_mid, hidden, silu, slope, mixed, middle, squares, first_squares,
     ) = block_forward(
-        normed_here,
         stream,
         jnp.stack([mask_one, mask_two]),
         conv_weight,
+        norm1_gain[None],
         norm2_gain[None],
         in_weight.reshape(rows_here, 3 * local),
         out_weight,
@@ -1940,9 +1953,11 @@
         down_weight,
         0,
     )
-    out_full = gather_pair_rows(after(out_grad.astype(BF), normed_here))
+    out_full = gather_pair_rows(out_grad.astype(BF))
     mean_square = squares[0] / (local * lax.axis_size(TP)) + epsilon
-    rms_mid, inverse_mid = jnp.sqrt(mean_square), lax.rsqrt(mean_square)[:, None]
+    rms_mid = jnp.sqrt(mean_square)
+    first_mean = first_squares / (local * lax.axis_size(TP)) + epsilon
+    rms_in, inverse_in = jnp.sqrt(first_mean[0]), lax.rsqrt(first_mean)
     middle_grad, branch_blocks, gain_mid_grad, ffn_partial, down_weight_grad, gate_weight_grad, up_rows = (
         feed_forward_backward(
             out_full, normed_mid, hidden, silu, slope, whole_gate, whole_up, whole_down, middle, out_grad,
@@ -1966,7 +1981,7 @@
     stream_grad, small_sums, up_weight_grad, out_weight_grad, in_weight_grad = mixer_backward(
         normed_mid, up_rows, branch_blocks, whole_out, in_matrix, projected, convolved, mixed, gated,
         normed_in, masks, conv_weight, stream, middle_grad, norm1_gain[None],
-        jnp.broadcast_to(inverse_in.reshape(1, tokens), (8, tokens)), gain_mid_grad, 5,
+        inverse_in, gain_mid_grad, 5,
     )
     conv_total, gain_in_total, gain_mid_total = small_sums[:3], small_sums[3], small_sums[4]
     return (

time: 677 us -> 626 us (0.925)
  Pallas kernels: 616 us -> 577 us
  blocking collectives: 8.51 us -> 0 us
    pallas_call x1, Pallas kernels: 197 us -> 167 us  [mixer_backward(): pl.pallas_call(kernel, out_shape=[array(tokens, local), array(8, local),...]
    pallas_call x1, Pallas kernels: 144 us -> 135 us  [feed_forward_backward(): pl.pallas_call(kernel, out_shape=[array(tokens, local), array(owners, tok...]
    psum x1 -> x0, blocking collectives: 8.51 us -> none  [rms_scale(): squares = lax.psum(jnp.sum(values * values, axis=1, keepdims=True), TP)]
  transfers between devices with their start and end apart: 2 -> 2, of which waited for: 0 -> 0; matrix products, arithmetic and copies ran while one was open for 2% -> 2% of each run, Pallas kernels for 70% -> 71%
where the time goes in v6:
time: 626 us; the launch traced here: 619 us
  Pallas kernels  577 us (92%)
  local copies, waits for them, and re-layouts  18.6 us (3%)
  between operations  14.5 us (2%)
  other arithmetic  9.42 us (2%)
    pallas_call x1, Pallas kernels, block_forward(): pl.pallas_call(kernel, out_shape=[o[0] for o in outs], in_specs=[VMEM] *...  274 us
    pallas_call x1, Pallas kernels, mixer_backward(): pl.pallas_call(kernel, out_shape=[array(tokens, local), array(8, local),...  167 us
    pallas_call x1, Pallas kernels, feed_forward_backward(): pl.pallas_call(kernel, out_shape=[array(tokens, local), array(owners, tok...  135 us
  transfers between devices with their start and end apart: 2, of which 0 were waited for; matrix products, arithmetic and copies ran while one was open for 2% of the time, Pallas kernels for 71%

profile of v6, /device:TPU:0, one launch (start us, length us, event | category | flops | bytes accessed | tf_op | source)
XLA Modules:
  0.0 619.3 jit_solution(12268998035483694776)
XLA Ops:
  7.2 0.0 copy-start.5
  7.2 0.0 all-gather.3.cloned.1.call-start
  7.2 2.8 convert_element_type.80
  10.0 0.0 copy-start.9
  10.0 0.0 all-gather.3.cloned.1.call-update
  10.0 0.0 reduce-scatter.2.cloned.1.call-start
  10.1 0.0 copy-done.5
  10.1 0.3 copy.52
  10.4 1.2 copy.53.refs_5_
  11.6 0.0 copy-done.9
  11.6 0.1 convert_reduce_fusion.1
  11.7 0.3 fusion.2
  12.1 1.1 add_convert_fusion.refs_1_
  13.1 274.5 %block_forward.1 = (bf16[2048,1536]{1,0:T(8,128)(2,1)}, bf16[2048,512]{1,0:T(8,128)(2,1)}, bf16[2048,1024]{1,0:T(8,128)(2,1)}, bf16[2048,1024]{1,0:T(8,128)(2,1)...) custom-call(f32[1024,512]{1,0:T(8,128)} %refs_12_.1, ...), custom_call_target="tpu_custom_call" | custom-call | bytes 629145600 | tf_op jit(solution)/shard_map/block_forward/pallas_call | solution.py:989
  287.6 0.0 all-gather.3.cloned.1.call-done
  287.6 135.3 %feed_forward_backward.1 = (f32[1024,512]{1,0:T(8,128)}, bf16[4,1024,512]{2,1,0:T(8,128)(2,1)}, f32[1,512]{1,0:T(1,128)}, bf16[2,4,1024,512]{3,2,1,0:T(8,128)(2,...) custom-call(bf16[2,4,1024,512]{3,2,1,0:T(8,128)(2,1)} %bitcast.10, ...), custom_call_target="tpu_custom_call" | custom-call | bytes 314572800 | tf_op jit(solution)/shard_map/feed_forward_backward/pallas_call | solution.py:1357
  422.9 0.0 copy-start.7
  422.9 0.0 reduce-scatter.2.cloned.1.call-update
  423.1 1.0 copy.54.refs_10_
  424.1 0.8 add_sqrt_fusion
  424.9 0.0 copy-done.7
  424.9 0.6 multiply_add_fusion
  425.5 0.6 pad_maximum_fusion.1
  426.1 166.9 %mixer_backward.1 = (f32[1024,512]{1,0:T(8,128)}, f32[8,512]{1,0:T(8,128)}, f32[256,2048]{1,0:T(8,128)}, f32[256,512]{1,0:T(8,128)}, f32[256,1536]{1,0:T(8,128)}) custom-call(bf16[2,4,1024,512]{3,2,1,0:T(8,128)(2,1)} %get-tuple-element.41.refs_1_.refs_0_, bf16[2048,1024]{1,0:T(8,128)(2,1)} %get-tuple-element.50.refs_1_, bf16[1,4,1024,512]{3,2,1,0:T(8,128)(2,1)} %bitcast.14, ...), custom_call_target="tpu_custom_call" | custom-call | bytes 314572800 | tf_op jit(solution)/shard_map/mixer_backward/pallas_call | solution.py:1851
  593.1 3.0 copy.55
  596.1 0.0 copy-start.8
  596.1 0.0 copy-start
  596.1 3.2 copy.56
  599.3 0.0 copy-done.8
  599.3 0.6 slice.16
  599.9 0.6 fusion.9
  600.5 0.0 reduce-scatter.2.cloned.1.call-done
  600.5 0.0 copy-done
  600.5 0.0 copy-start.4
  600.5 3.0 convert_add_fusion
  603.5 0.0 copy-done.4
  603.5 0.0 copy-start.6
  603.5 0.0 copy-start.2
  603.5 1.3 copy.62
  604.8 0.1 copy-done.6
  604.9 0.8 copy.63
  605.7 0.5 copy-done.2
  606.2 0.0 copy-start.3
  606.2 1.3 copy.64
  607.5 1.0 copy-done.3
  608.5 0.0 copy-start.1
  608.5 1.3 copy.65
  609.9 1.0 copy-done.1
  610.9 1.3 copy.66
  (10 shorter events, 0.1 us)
Async XLA Ops:
  7.2 2.9 copy-start.5
  7.2 280.4 %all-gather.3.cloned.1.call-start = ((), (), s32[]{:S(2)}) async-start(), calls=%async_computation.2 | async-start | bytes 9437184 | tf_op jit(solution)/shard_map/all_gather | solution.py:1919
  10.0 1.6 copy-start.9
  10.0 590.4 %reduce-scatter.2.cloned.1.call-start = ((), (), s32[]{:S(2)}) async-start(), calls=%async_computation.1 | async-start | bytes 9437184 | tf_op jit(solution)/shard_map/reduce_scatter | solution.py:1967
  422.9 1.9 copy-start.7
  596.1 3.2 copy-start.8
  596.1 4.4 copy-start
  600.5 3.0 copy-start.4
  603.5 1.4 copy-start.6
  603.5 2.7 copy-start.2
  606.2 2.3 copy-start.3
  608.5 2.3 copy-start.1
Sparse Core Ops, SparseCore 0:
  10.2 82.3 all-gather.2
  423.1 100.3 reduce-scatter.1

commit v7 on v6

--- a/solution.py
+++ b/solution.py
@@ -428,7 +428,7 @@
         self.p, self.product = p, product
         self.sx, self.rx, self.sz, self.rz, self.rm = sx, rx, sz, rz, rm
         self.held, self.out, self.ss, self.rs = held, out, ss, rs
-        self.half = held.shape[1]
+        self.half = sz.shape[2]
 
     def across(self, k):
         return remote(self.sx.at[k], self.rx.at[k], self.ss.at[k], self.rs.at[k], self.p.across)
@@ -1049,11 +1049,12 @@
     def kernel(*refs):
         out_ref, normed_ref, hidden_ref, silu_ref, slope_ref, gate_ref, up_ref, down_ref = refs[:8]
         middle_ref, out_grad_ref, squares_ref, gain_ref = refs[8:12]
-        middle_grad, branch_all, gain_grad, partials, down_grad_all, gate_grad_all, up_rows = refs[12:19]
+        middle_grad, branch_all, gain_grad, partials, down_grad_all, gate_grad_all, up_blocks = refs[12:19]
         gate_rows, weights, cols, early, to_core, sums, from_y, from_mate, lanes = refs[19:28]
         near_lanes, residual, weight_grad, cols_sem, early_sem, weights_sem, move_ss, move_rs = refs[28:36]
         lanes_ss, lanes_rs, branch_ss, branch_rs, tile_sem = refs[36:41]
-        sx, rx, sz, rz, rm, held, ss, rs = refs[41:]
+        up_rows, up_ss, up_rs, free_sem = refs[41:45]
+        sx, rx, sz, rz, rm, held, ss, rs = refs[45:]
         p = Place()
         p.core = (p.zh, p.zl, p.x, p.y, 1 - p.c)
         p.side = (p.zh, p.zl, p.x, 1 - p.y, p.c)
@@ -1089,6 +1090,8 @@
         jobs += [(D[0], FAR, False), (D[0], NEAR, False), (D[0], MATE, False)]
         jobs += [(D[1], FAR, True), (D[1], NEAR, True), (D[0], OWN, False)]
         jobs += [(D[1], MATE, True), (D[1], OWN, True)]
+        jobs += [(D[1], FAR, False), (D[1], NEAR, False), (D[1], FAR, True), (D[1], NEAR, True)]
+        jobs += [(D[1], MATE, False), (D[1], MATE, True), (D[1], OWN, True), (D[1], OWN, False)]
         jobs += [(D[1], k, False) for k in ORDER]
         feed = Columns(p, jobs, cols, cols_sem)
         tile_loads(0, "start")
@@ -1103,6 +1106,14 @@
             p, lambda k, x: feed.times(gate_rows[...]), sx, rx.at[1], sz, rz.at[1],
             rm.at[1], held, weight_grad, ss.at[1], rs.at[1],
         )
+
+        um = PairScatter(
+            p, lambda k, x: feed.times(up_rows[...]), sx, rx.at[0], sz, None, None, None, None,
+            up_ss, up_rs,
+        )
+
+        def up_store(k):
+            return pltpu.make_async_copy(rx.at[0, k], up_blocks.at[k], up_ss.at[4 + k])
 
         def rows_backward(m):
             tile_loads(m, "wait")
@@ -1296,6 +1307,7 @@
         down_again.start()
         to_mate(0)
         dm.own_rows()
+        pl.semaphore_signal(free_sem, inc=1, device_id=p.across, device_id_type=MESH)
         dm.sent(MATE)
         gm.send_across(MATE)
         dm.sent(OWN)
@@ -1306,6 +1318,11 @@
         gm.send_on(FAR, 0)
         dm.sent_on(1)
         gm.send_on(NEAR, 1)
+        pl.semaphore_wait(free_sem, 1)
+        gm.sent(FAR)
+        um.send_across(FAR)
+        gm.sent(NEAR)
+        um.send_across(NEAR)
         residual_loads(0, "start")
         residual_loads(1, "start")
         down_again.wait()
@@ -1315,10 +1332,14 @@
             out_partial(m)
         dm.sent_on(2)
         gm.mate_rows()
+        gm.sent(MATE)
+        um.send_across(MATE)
         final(2)
         final(3)
         row_sums()
         gm.send_relay(0)
+        gm.sent(OWN)
+        um.send_across(OWN)
         residual_grad()
         dm.finish()
         down_store = pltpu.make_async_copy(weight_grad, down_grad_all, weights_sem.at[1])
@@ -1337,9 +1358,15 @@
             spreads[t].finish()
         gather_done = pltpu.make_async_copy(early, branch_all, early_sem.at[0, 0])
         gather_done.start()
+        for k in ORDER:
+            total_rows = um.summed(k)
+            rx[0, k] = total_rows.astype(BF)
+            up_store(k).start()
         for j in range(3):
             gm.sent_on(j)
-        gm.sent(*ORDER)
+        um.sent(*ORDER)
+        for k in ORDER:
+            up_store(k).wait()
         for t in range(4):
             side_copy(t).wait_send()
         for t in range(2):
@@ -1363,10 +1390,10 @@
             array(pair, owners, tokens, local, dtype=BF),
             array(rows, 2 * half),
             array(rows, 2 * half),
-            array(total, half, dtype=BF),
+            array(4, rows, half, dtype=BF),
         ],
         in_specs=[ANY, ANY, VMEM, ANY, ANY, ANY, ANY, ANY, ANY, ANY, VMEM, VMEM],
-        out_specs=[VMEM, ANY, VMEM, ANY, ANY, ANY, VMEM],
+        out_specs=[VMEM, ANY, VMEM, ANY, ANY, ANY, ANY],
         scratch_shapes=[
             pltpu.VMEM((total, half), BF),
             pltpu.VMEM((owners * local, half), BF),
@@ -1390,6 +1417,10 @@
             pltpu.SemaphoreType.DMA((4, 3)),
             pltpu.SemaphoreType.DMA((4, 3)),
             pltpu.SemaphoreType.DMA((3, 2)),
+            pltpu.VMEM((total, half), BF),
+            pltpu.SemaphoreType.DMA((8,)),
+            pltpu.SemaphoreType.DMA((4,)),
+            pltpu.SemaphoreType.REGULAR,
         ]
         + pair_scatter_scratch(2, rows, half),
         compiler_params=pltpu.CompilerParams(
@@ -1487,28 +1518,32 @@
 
 
 def mixer_backward(
-    normed_mid, up_rows, branch, whole_out, in_matrix, projected, convolved, mixed, gated, normed_in,
-    masks, conv_weight, stream, middle_grad, gain, inverse, gain_mid_grad, collective,
+    up_blocks, branch, whole_out, in_matrix, projected, convolved, mixed, gated, normed_in,
+    masks, conv_weight, stream, middle_grad, gain, inverse, gain_mid_grad, partials, middle, collective,
 ):
-    pair, owners, tokens, local = normed_mid.shape
-    total, half = up_rows.shape
-    rows = owners * local // 8
+    owners, tokens, local = branch.shape
+    rows, half = up_blocks.shape[1:]
     three = in_matrix.shape[1]
     tile = tokens // 4
     groups = three // local
 
     def kernel(*refs):
-        normed_mid_ref, up_rows_ref, branch_ref, out_ref, in_ref, projected_ref, convolved_ref = refs[:7]
+        refs = (None,) + refs
+        up_ref, branch_ref, out_ref, in_ref, projected_ref, convolved_ref = refs[1:7]
         mixed_ref, gated_ref, normed_in_ref, masks_ref, conv_ref, stream_ref = refs[7:13]
         middle_ref, gain_ref, inverse_ref, gain_mid_ref = refs[13:17]
+        partials_ref, residual_ref = refs[17:19]
+        refs = refs[:17] + refs[19:]
         stream_grad, small_sums, up_grad, out_grad, in_grad = refs[17:22]
+        result_all = refs[22]
+        refs = refs[:22] + refs[23:]
         conv_grad, rows_grad, stage, stage_mixed, weights, to_core, sums, from_y, lanes, near_lanes = refs[22:32]
         smalls, cols, stage_sem, in_sem, move_ss, move_rs, lanes_ss, lanes_rs = refs[32:40]
         small_ss, small_rs, halo_sem, cols_sem = refs[40:44]
         branch_sem = refs[59]
-        sx, rx, sz, rz, rm, held, ss, rs = refs[44:52]
+        res_sums, res_y, res_mate, res_own, res_ss, res_rs, res_sem = refs[60:]
+        own_block, up_sem, sz, rz, rm, held, ss, rs = refs[44:52]
         lx, lrx, lz, lrz, lrm, lss, lrs = refs[52:59]
-        lheld = held.at[:, pl.ds(0, local)]
 
         p = Place()
         p.core = (p.zh, p.zl, p.x, p.y, 1 - p.c)
@@ -1575,6 +1610,10 @@
                 )
                 getattr(copy, act)()
 
+        for k in ORDER:
+            pltpu.make_async_copy(
+                up_ref.at[k], own_block if k == OWN else sz.at[(None, 2, 1, 0)[k]], up_sem.at[k]
+            ).start()
         out_loads("start")
         stage_copies(0, "start")
         stage_copies(1, "start")
@@ -1582,14 +1621,8 @@
         branch_loads(1, "start")
         mixed_load(0).start()
         mixed_load(1).start()
-        feed_jobs = [(normed_mid_ref, k, True) for k in ORDER]
-        feed_jobs += [(normed_mid_ref, FAR, False)]
-        feed_jobs += [(branch_ref, k, True) for k in ORDER]
-        feed_jobs += [(normed_mid_ref, NEAR, False)]
-        feed_jobs += [(normed_in_ref, FAR, True), (normed_in_ref, NEAR, True)]
-        feed_jobs += [(normed_mid_ref, MATE, False)]
-        feed_jobs += [(normed_in_ref, MATE, True), (normed_in_ref, OWN, True)]
-        feed_jobs += [(normed_mid_ref, OWN, False)]
+        feed_jobs = [(branch_ref, k, True) for k in ORDER]
+        feed_jobs += [(normed_in_ref, k, True) for k in ORDER]
         feed_jobs += [(branch_ref, k, False) for k in ORDER]
         feed_jobs += [(normed_in_ref, k, False) for k in ORDER]
         feed = Columns(p, feed_jobs, cols, cols_sem)
@@ -1598,20 +1631,41 @@
         ]
         p.enter_all([device_at(s) for s in others] + [p.core, p.side, diagonal])
 
-        um = PairScatter(
-            p, lambda k, x: feed.times(up_rows_ref[...]), sx, rx.at[0], sz, rz.at[0], rm.at[0], held,
-            up_grad, ss.at[0], rs.at[0],
-        )
+        um = PairScatter(p, None, None, None, sz, rz, rm, None, up_grad, ss, rs)
+
+        def up_load(k):
+            target = own_block if k == OWN else sz.at[(None, 2, 1, 0)[k]]
+            return pltpu.make_async_copy(up_ref.at[k], target, up_sem.at[k])
+
+        def up_send(k, j):
+            up_load(k).wait()
+
+            @pl.when(p.outer)
+            def _():
+                um.outward(j).start()
+
+            if j < 2:
+
+                @pl.when(p.inner)
+                def _():
+                    um.middle(j).start()
+
+        def up_back():
+            @pl.when(p.inner)
+            def _():
+                um.relay(0).wait_recv()
+                sz[2] = (sz[2].astype(F32) + rm[2].astype(F32)).astype(BF)
+                um.back().start()
 
         om = LineScatter(
-            p, lambda k, x: feed.times(gated_ref[...]), lx.at[0], lrx.at[0], lz.at[0], lrz.at[0], lrm.at[0], lheld,
+            p, lambda k, x: feed.times(gated_ref[...]), lx.at[0], lrx.at[0], lz.at[0], lrz.at[0], lrm.at[0], held,
             out_grad, lss.at[0], lrs.at[0],
         )
         ims = [
             LineScatter(
                 p, lambda k, x, g=g: feed.times_next(rows_grad[g], g == 0, g == groups - 1),
                 lx.at[1 + g], lrx.at[1 + g], lz.at[1 + g], lrz.at[1 + g], lrm.at[1 + g],
-                lheld, in_grad.at[:, pl.ds(g * local, local)], lss.at[1 + g], lrs.at[1 + g],
+                held, in_grad.at[:, pl.ds(g * local, local)], lss.at[1 + g], lrs.at[1 + g],
             )
             for g in range(groups)
         ]
@@ -1720,6 +1774,69 @@
             if n + 1 < 4:
                 in_loads(n + 1, "start")
 
+        piece = tokens // 2
+
+        def res_source(j, t):
+            place = p.zl if t >= 2 else 1 - p.zl
+            return partials_ref.at[place, j, pl.ds(t % 2 * piece, piece), :]
+
+        def res_core(b, t):
+            return remote(
+                res_source(owner[2 * b], t), res_sums.at[b, t], res_ss.at[b, t], res_rs.at[b, t], p.core
+            )
+
+        def res_side(t):
+            return remote(res_sums.at[0, t], res_y.at[t], res_ss.at[2, t], res_rs.at[2, t], p.side)
+
+        def res_send(t):
+            return remote(res_sums.at[1, t], res_mate.at[t], res_ss.at[3, t], res_rs.at[3, t], p.mate)
+
+        def res_load(n):
+            source = res_source(owner[2 * (n // 4) + 1], n % 4)
+            return pltpu.make_async_copy(source, res_own.at[n % 2], res_sem.at[n % 2])
+
+        def res_residual(i):
+            here = pl.ds(i * tile, tile)
+            return pltpu.make_async_copy(residual_ref.at[here, :], stage.at[i % 2, i // 2], res_sem.at[2 + i])
+
+        def res_store(i):
+            here = pl.ds(i * tile, tile)
+            return pltpu.make_async_copy(stage.at[i % 2, i // 2], result_all.at[here, :], res_sem.at[6 + i])
+
+        def res_add(n, *others):
+            res_load(n).wait()
+            b, t = n // 4, n % 4
+            res_core(b, t).wait_recv()
+            for part in range(2):
+                here = pl.ds(part * tile, tile)
+                value = res_own[n % 2, here, :].astype(F32) + res_sums[b, t, here, :].astype(F32)
+                for other in others:
+                    value = value + other[here, :].astype(F32)
+                if n < 6:
+                    res_sums[b, t, here, :] = value.astype(BF)
+                else:
+                    i = (n - 6) * 2 + part
+                    res_residual(i).wait()
+                    slot = stage.at[part, n - 6]
+                    slot[...] = slot[...] + value
+                    res_store(i).start()
+            if n + 2 < 8:
+                res_load(n + 2).start()
+
+        def res_to_side(t):
+            res_add(t)
+            res_side(t).start()
+
+        def res_to_mate(t):
+            res_side(t).wait_recv()
+            res_add(4 + t, res_y.at[t])
+            res_send(t).start()
+
+        def res_final(t):
+            res_side(t).wait_recv()
+            res_send(t - 2).wait_recv()
+            res_add(4 + t, res_y.at[t], res_mate.at[t - 2])
+
         def lane_copies():
             return [
                 remote(lanes, near_lanes.at[i], lanes_ss.at[i], lanes_rs.at[i], device)
@@ -1779,37 +1896,46 @@
                 value = value + smalls[s]
             small_sums[...] = value
 
-        for k in ORDER:
-            um.send_across(k)
+        for b in range(2):
+            for t in range(4):
+                res_core(b, t).start()
+        res_load(0).start()
+        res_load(1).start()
+        up_send(FAR, 0)
+        up_send(NEAR, 1)
+        up_send(MATE, 2)
         out_loads("wait")
         for t in range(4):
             gated_backward(t)
             if t == 0:
                 send_halo()
+            else:
+                res_to_side(t - 1)
         in_loads(0, "start")
-        um.send_on(FAR, 0)
+        res_to_side(3)
+        um.send_relay(0)
         take_halo()
         for t in range(4):
             conv_backward(t)
         for k in ORDER:
             om.send_across(k)
-        um.send_on(NEAR, 1)
-        um.send_relay(0)
-        partial_block(0)
-        partial_block(1)
         for k in (FAR, NEAR):
             for m in ims:
                 m.send_across(k)
-        um.mate_rows()
         um.send_relay(1)
         um.send_forward()
-        partial_block(2)
-        partial_block(3)
+        res_to_mate(0)
+        res_to_mate(1)
+        partial_block(0)
+        partial_block(1)
         for k in (MATE, OWN):
             for m in ims:
                 m.send_across(k)
-        um.own_rows()
-        um.send_back()
+        up_load(OWN).wait()
+        up_grad[:, um.cols_of(p.zl)] = own_block[...].astype(F32)
+        up_back()
+        partial_block(2)
+        partial_block(3)
         om.send_on(FAR, 0)
         om.send_on(NEAR, 1)
         om.mate_rows()
@@ -1822,18 +1948,29 @@
         for m in ims:
             m.send_on(NEAR, 1)
         input_grad()
+        for i in range(4):
+            res_residual(i).start()
         om.finish()
         for m in ims:
             m.mate_rows()
             m.send_back()
+        res_final(2)
+        res_final(3)
         sum_smalls()
         for m in ims:
             m.own_rows()
         for m in ims:
             m.finish()
+        for i in range(4):
+            res_store(i).wait()
+        for t in range(4):
+            res_core(0, t).wait_send()
+            res_core(1, t).wait_send()
+            res_side(t).wait_send()
+        for t in range(2):
+            res_send(t).wait_send()
         for j in range(3):
             um.sent_on(j)
-        um.sent(*ORDER)
         for t in range(4):
             core_copy(1, t).wait_send()
             side_copy(t).wait_send()
@@ -1856,10 +1993,12 @@
             array(rows, 2 * half),
             array(rows, local),
             array(rows, three),
+            array(tokens, local),
         ],
-        in_specs=[ANY, VMEM, ANY, ANY, ANY, ANY, ANY, ANY, VMEM, ANY, VMEM, VMEM, ANY, ANY]
-        + [VMEM] * 3,
-        out_specs=[VMEM] * 5,
+        in_specs=[ANY, ANY, ANY, ANY, ANY, ANY, ANY, VMEM, ANY, VMEM, VMEM, ANY, ANY]
+        + [VMEM] * 3
+        + [ANY, ANY],
+        out_specs=[VMEM] * 5 + [ANY],
         scratch_shapes=[
             pltpu.VMEM((tokens + 8, local), F32),
             pltpu.VMEM((groups, tokens, local), BF),
@@ -1872,7 +2011,7 @@
             pltpu.VMEM((8, tokens), F32),
             pltpu.VMEM((3, 8, tokens), F32),
             pltpu.VMEM((8, 8, local), F32),
-            pltpu.VMEM((2, total, rows), BF),
+            pltpu.VMEM((2, tokens, rows), BF),
             pltpu.SemaphoreType.DMA((2, 3)),
             pltpu.SemaphoreType.DMA((owners,)),
             pltpu.SemaphoreType.DMA((3, 4)),
@@ -1882,10 +2021,15 @@
             pltpu.SemaphoreType.DMA((7,)),
             pltpu.SemaphoreType.DMA((8,)),
             pltpu.SemaphoreType.DMA((2,)),
-            pltpu.SemaphoreType.DMA((2, pair)),
-        ]
-        + pair_scatter_scratch(1, rows, half)
-        + [
+            pltpu.SemaphoreType.DMA((2, 1)),
+            pltpu.VMEM((rows, half), BF),
+            pltpu.SemaphoreType.DMA((4,)),
+            pltpu.VMEM((3, rows, half), BF),
+            pltpu.VMEM((3, rows, half), BF),
+            pltpu.VMEM((4, rows, half), BF),
+            pltpu.VMEM((rows, local), F32),
+            pltpu.SemaphoreType.DMA((11,)),
+            pltpu.SemaphoreType.DMA((11,)),
             pltpu.VMEM((n, 4, rows, local), BF),
             pltpu.VMEM((n, 4, rows, local), BF),
             pltpu.VMEM((n, 3, rows, local), BF),
@@ -1894,6 +2038,13 @@
             pltpu.SemaphoreType.DMA((n, 9)),
             pltpu.SemaphoreType.DMA((n, 9)),
             pltpu.SemaphoreType.DMA((2, owners)),
+            pltpu.VMEM((2, 4, tokens // 2, local), BF),
+            pltpu.VMEM((4, tokens // 2, local), BF),
+            pltpu.VMEM((2, tokens // 2, local), BF),
+            pltpu.VMEM((2, tokens // 2, local), BF),
+            pltpu.SemaphoreType.DMA((4, 4)),
+            pltpu.SemaphoreType.DMA((4, 4)),
+            pltpu.SemaphoreType.DMA((10,)),
         ],
         compiler_params=pltpu.CompilerParams(
             collective_id=collective, has_side_effects=True, vmem_limit_bytes=62 << 20
@@ -1901,8 +2052,9 @@
         cost_estimate=pl.CostEstimate(flops=0, bytes_accessed=300 << 20, transcendentals=0),
         name="mixer_backward",
     )(
-        normed_mid, up_rows, branch[None], whole_out, in_matrix, projected, convolved, mixed, gated,
-        normed_in[None], masks, conv_weight, stream, middle_grad, gain, inverse, gain_mid_grad,
+        up_blocks, branch[None], whole_out, in_matrix, projected, convolved, mixed, gated,
+        normed_in[None], masks, conv_weight, stream, middle_grad, gain, inverse, gain_mid_grad, partials,
+        middle,
     )
 
 
@@ -1958,15 +2110,12 @@
     rms_mid = jnp.sqrt(mean_square)
     first_mean = first_squares / (local * lax.axis_size(TP)) + epsilon
     rms_in, inverse_in = jnp.sqrt(first_mean[0]), lax.rsqrt(first_mean)
-    middle_grad, branch_blocks, gain_mid_grad, ffn_partial, down_weight_grad, gate_weight_grad, up_rows = (
+    middle_grad, branch_blocks, gain_mid_grad, ffn_partial, down_weight_grad, gate_weight_grad, up_blocks = (
         feed_forward_backward(
             out_full, normed_mid, hidden, silu, slope, whole_gate, whole_up, whole_down, middle, out_grad,
             squares, norm2_gain[None], 4,
         )
     )
-    result = middle + lax.psum_scatter(
-        ffn_partial.reshape(-1, local), PAIR, scatter_dimension=0, tiled=True
-    ).astype(F32)
     next_one, next_two = lag_masks(doc_starts, positions + 1)[0], lag_masks(doc_starts, positions + 2)[1]
     count = tokens * lax.axis_size(SEQ)
     masks = jnp.concatenate(
@@ -1978,10 +2127,10 @@
         ],
         axis=1,
     )
-    stream_grad, small_sums, up_weight_grad, out_weight_grad, in_weight_grad = mixer_backward(
-        normed_mid, up_rows, branch_blocks, whole_out, in_matrix, projected, convolved, mixed, gated,
+    stream_grad, small_sums, up_weight_grad, out_weight_grad, in_weight_grad, result = mixer_backward(
+        up_blocks, branch_blocks, whole_out, in_matrix, projected, convolved, mixed, gated,
         normed_in, masks, conv_weight, stream, middle_grad, norm1_gain[None],
-        inverse_in, gain_mid_grad, 5,
+        inverse_in, gain_mid_grad, ffn_partial, middle, 5,
     )
     conv_total, gain_in_total, gain_mid_total = small_sums[:3], small_sums[3], small_sums[4]
     return (

time: 626 us -> 620 us (level)
  the two profiles are of different devices: /device:TPU:0 before, /device:TPU:26 now
where the time goes in v7:
time: 620 us; the launch traced here: 614 us
  Pallas kernels  571 us (92%)
  local copies, waits for them, and re-layouts  20.6 us (3%)
  between operations  14.4 us (2%)
  other arithmetic  7.16 us (1%)
    pallas_call x1, Pallas kernels, block_forward(): pl.pallas_call(kernel, out_shape=[o[0] for o in outs], in_specs=[VMEM] *...  271 us
    pallas_call x1, Pallas kernels, mixer_backward(): pl.pallas_call(kernel, out_shape=[array(tokens, local), array(8, local),...  153 us
    pallas_call x1, Pallas kernels, feed_forward_backward(): pl.pallas_call(kernel, out_shape=[array(tokens, local), array(owners, tok...  147 us
    unnamed x22, local copies, waits for them, and re-layouts  13.8 us
  transfers between devices with their start and end apart: 1, of which 0 were waited for; matrix products, arithmetic and copies ran while one was open for 1% of the time, Pallas kernels for 44%

profile of v7, /device:TPU:26, one launch (start us, length us, event | category | flops | bytes accessed | tf_op | source)
XLA Modules:
  0.0 613.6 jit_solution(8976000552744081153)
XLA Ops:
  7.2 0.0 copy-start.4
  7.2 0.0 all-gather.3.cloned.1.call-start
  7.2 2.8 convert_element_type.74
  10.0 0.0 copy-start.6
  10.0 0.0 all-gather.3.cloned.1.call-update
  10.0 0.0 copy-done.4
  10.0 0.3 copy.52
  10.3 1.2 copy.53.refs_5_
  11.5 0.0 copy-done.6
  11.5 0.1 convert_reduce_fusion.1
  11.7 1.0 copy.54.refs_9_
  12.8 0.3 fusion.2
  13.1 1.1 add_convert_fusion.refs_1_
  14.2 271.2 %block_forward.1 = (bf16[2048,1536]{1,0:T(8,128)(2,1)}, bf16[2048,512]{1,0:T(8,128)(2,1)}, bf16[2048,1024]{1,0:T(8,128)(2,1)}, bf16[2048,1024]{1,0:T(8,128)(2,1)...) custom-call(f32[1024,512]{1,0:T(8,128)} %refs_11_.1, ...), custom_call_target="tpu_custom_call" | custom-call | bytes 629145600 | tf_op jit(solution)/shard_map/block_forward/pallas_call | solution.py:989
  285.4 0.8 add_sqrt_fusion
  286.2 1.4 multiply_add_fusion
  287.6 0.6 pad_maximum_fusion.1
  288.2 0.0 all-gather.3.cloned.1.call-done
  288.2 147.3 %feed_forward_backward.1 = (f32[1024,512]{1,0:T(8,128)}, bf16[4,1024,512]{2,1,0:T(8,128)(2,1)}, f32[1,512]{1,0:T(1,128)}, bf16[2,4,1024,512]{3,2,1,0:T(8,128)(2,...) custom-call(bf16[2,4,1024,512]{3,2,1,0:T(8,128)(2,1)} %bitcast.9, ...), custom_call_target="tpu_custom_call" | custom-call | bytes 314572800 | tf_op jit(solution)/shard_map/feed_forward_backward/pallas_call | solution.py:1384
  435.5 152.8 %mixer_backward.1 = (f32[1024,512]{1,0:T(8,128)}, f32[8,512]{1,0:T(8,128)}, f32[256,2048]{1,0:T(8,128)}, f32[256,512]{1,0:T(8,128)}, f32[256,1536]{1,0:T(8,128)}, /*index=5*/f32[1024,512]{1,0:T(8,128)}) custom-call(bf16[4,256,1024]{2,1,0:T(8,128)(2,1)} %get-tuple-element.50.refs_0_, bf16[1,4,1024,512]{3,2,1,0:T(8,128)(2,1)} %bitcast.12, ...), custom_call_target="tpu_custom_call" | custom-call | bytes 314572800 | tf_op jit(solution)/shard_map/mixer_backward/pallas_call | solution.py:1988
  588.4 1.4 fusion.9
  589.8 1.3 slice.16
  591.1 1.9 copy.55
  593.0 1.6 copy.56
  594.6 0.0 copy-start.3
  594.6 3.2 copy.63
  597.8 0.0 copy-done.3
  597.8 0.0 copy-start.5
  597.8 0.0 copy-start.1
  597.8 1.3 copy.64
  599.1 0.1 copy-done.5
  599.2 0.8 copy.65
  600.0 0.5 copy-done.1
  600.5 0.0 copy-start.2
  600.5 1.3 copy.66
  601.8 1.0 copy-done.2
  602.9 0.0 copy-start
  602.9 1.3 copy.67
  604.2 1.0 copy-done
  605.2 1.3 copy.68
  (10 shorter events, 0.1 us)
Async XLA Ops:
  7.2 2.9 copy-start.4
  7.2 281.0 %all-gather.3.cloned.1.call-start = ((), (), s32[]{:S(2)}) async-start(), calls=%async_computation | async-start | bytes 9437184 | tf_op jit(solution)/shard_map/all_gather | solution.py:2071
  10.0 1.5 copy-start.6
  594.6 3.2 copy-start.3
  597.8 1.4 copy-start.5
  597.8 2.7 copy-start.1
  600.5 2.3 copy-start.2
  602.9 2.3 copy-start
Sparse Core Ops, SparseCore 0:
  10.2 80.4 all-gather.2
